TPU v7x, 256 devices: a whole 4x4x8 slice. The times are simulated.
256 devices in a mesh: leaf: 16 (over z, x_lo), chan: 16 (over y, x_hi, core).
Axes of the slice: x: 4 (x_hi: 2, x_lo: 2; x = x_hi * 2 + x_lo), y: 4, z: 8, core: 2. Of those that a mesh axis runs over, the one named last changes fastest.
Arguments:
- features: float32 [512, 32, 512], P('chan', 'leaf'), may hold values from -6 to 6
- leaf_counts: int32 [16], P('leaf'), may hold values from 1 to 2, as said below
- occupancy: int32 [32, 512], P('leaf'), may hold values 0 or 1
- neighbours: int32 [32, 26], P('leaf'), may hold values from -1 to 31, as said below
- weight_in: float32 [27, 512, 512], P(None, 'chan'), may hold values from -0.0625 to 0.0625
- bias_in: float32 [512], P('chan'), may hold values from -3 to 3
- weight_out: float32 [27, 512, 512], P(None, 'chan'), may hold values from -0.125 to 0.125
- bias_out: float32 [512], P('chan'), may hold values from -3 to 3
Outputs:
- result: float32 [512, 32, 512], P('chan', 'leaf')
Inputs may be any that keep to these rules, and one draw needn't show every extreme that they name: `leaf_counts`: each index of leaf has 1 to 2 live slots, and some index has all 2. `neighbours`: entries name live slots only, and dead slots have -1 in every column; the leaves sit on a grid, so a leaf's neighbour in a direction has that leaf as its neighbour in the opposite one.
All inputs are finite; a program needn't handle non-finite values. No bound on the sum of `occupancy` on one device may be relied on, other than what follows from the above.
Results may differ from a plain program's by a relative error of at most 0.0003.
Values sent between devices are 32-bit elements; how exact they have to be, the bound alone decides.
No kernel may reach another device: no remote copies, remote signals or barrier semaphores. Data moves between devices by JAX's collectives and lax.ppermute only.
A program may use at most 64 MiB of HBM per device.

v0:
```python
import functools

import jax
import jax.numpy as jnp
from jax import lax
from jax.experimental import pallas as pl
from jax.experimental.pallas import tpu as pltpu
from jax.sharding import PartitionSpec as P

DIRECTIONS = [
    (first, second, third)
    for first in (-1, 0, 1)
    for second in (-1, 0, 1)
    for third in (-1, 0, 1)
    if (first, second, third) != (0, 0, 0)
]
VMEM = pl.BlockSpec(memory_space=pltpu.VMEM)
SMEM = pl.BlockSpec(memory_space=pltpu.SMEM)
F32 = jnp.float32
BF16 = jnp.bfloat16
ROWS = 24


def call(kernel, outs, scratch=(), flops=1000000, touched=1000000, room=16):
    return functools.partial(
        pl.pallas_call,
        kernel,
        out_shape=outs,
        scratch_shapes=list(scratch),
        compiler_params=pltpu.CompilerParams(vmem_limit_bytes=room * 1024 * 1024),
        cost_estimate=pl.CostEstimate(flops=flops, bytes_accessed=touched, transcendentals=0),
    )


def arr(shape, dtype=F32):
    return jax.ShapeDtypeStruct(shape, dtype)


def close(shape, dtype=F32):
    return pltpu.VMEM(shape, dtype)


def near(values):
    return [pltpu.with_memory_space_constraint(value, pltpu.VMEM) for value in values]


def weights_kernel(place, own, other, high, low):
    core = place[0]

    def step(tap, carry):
        mine, theirs = own[tap], other[tap]
        first = jnp.where(core == 0, mine, theirs)
        second = jnp.where(core == 0, theirs, mine)
        both = jnp.concatenate([first, second], axis=0)
        top = both.astype(BF16)
        high[tap] = top
        low[tap] = (both - top.astype(F32)).astype(BF16)
        return carry

    lax.fori_loop(0, 27, step, 0)


def split_weights(place, own, other):
    outs = (close((27, 64, 512), BF16), close((27, 64, 512), BF16))
    return call(weights_kernel, outs, flops=8000000, touched=9000000)(
        in_specs=[SMEM, VMEM, VMEM], out_specs=(VMEM, VMEM)
    )(place, own, other)


def cut_faces(rows, faces):
    faces[0:64, :] = jnp.concatenate([rows[0:64, :], rows[448:512, :]], axis=1)
    for x in range(8):
        faces[64 + 8 * x : 72 + 8 * x, :] = jnp.concatenate(
            [rows[64 * x : 64 * x + 8, :], rows[64 * x + 56 : 64 * x + 64, :]], axis=1
        )
    faces[128:192, :] = jnp.concatenate(
        [rows[pl.ds(0, 64, stride=8), :], rows[pl.ds(7, 64, stride=8), :]], axis=1
    )


def in_order(core, own, other):
    first = jnp.where(core == 0, own, other)
    second = jnp.where(core == 0, other, own)
    return jnp.concatenate([first, second], axis=0)


def active_voxels(core, counts, occupancy):
    chosen = jnp.where(core == 0, occupancy[0:1, :], occupancy[1:2, :]).astype(F32)
    return chosen * jnp.where(core < counts[0], 1.0, 0.0)


def features_kernel(place, counts, occupancy, own, other, rows, faces):
    core = place[0]
    mine = jnp.where(core == 0, own[:, 0, :], own[:, 1, :])
    theirs = jnp.where(core == 0, other[:, 0, :], other[:, 1, :])
    both = in_order(core, mine, theirs)
    rows[...] = (both * active_voxels(core, counts, occupancy)).T
    cut_faces(rows, faces)


def added(parts):
    value = parts[0][...]
    for part in parts[1:]:
        value = value + part[...]
    return value


def bias_row(core, number, own_bias, other_bias):
    own, other = own_bias[number : number + 1, :], other_bias[number : number + 1, :]
    first = jnp.where(core == 0, own, other)
    second = jnp.where(core == 0, other, own)
    return jnp.concatenate([first, second], axis=1)


def bias_column(row):
    wide = jnp.concatenate([row, row], axis=1)
    return jnp.broadcast_to(wide, (128, 128)).T[0:64, 0:1]


def hidden_kernel(place, counts, occupancy, own_bias, other_bias, *rest):
    core = place[0]
    rows, faces = rest[8:]
    bias = bias_column(bias_row(core, 0, own_bias, other_bias))
    value = jnp.maximum(added(rest[:8]) + bias, 0.0)
    rows[...] = (value * active_voxels(core, counts, occupancy)).T
    cut_faces(rows, faces)


def result_kernel(place, counts, occupancy, own_bias, other_bias, *rest):
    core = place[0]
    keep, give = rest[8:]
    bias = bias_column(bias_row(core, 1, own_bias, other_bias))
    value = (added(rest[:8]) + bias) * active_voxels(core, counts, occupancy)
    keep[...] = jnp.where(core == 0, value[0:32], value[32:64])
    give[...] = jnp.where(core == 0, value[32:64], value[0:32])


def merge_kernel(place, keep, got, out):
    core = place[0]
    out[:, 0, :] = jnp.where(core == 0, keep[...], got[...])
    out[:, 1, :] = jnp.where(core == 0, got[...], keep[...])


def rim_list():
    listed, begin = [], 192
    corner = 240
    for a, b, c in DIRECTIONS:
        steps = [step for step in (a, b, c) if step]
        if steps[0] < 0:
            continue
        if len(steps) == 1:
            listed.append(((a, b, c), 64 * (0 if a else (1 if b else 2)), 64))
        elif len(steps) == 2:
            listed.append(((a, b, c), begin, 8))
            begin += 8
        else:
            listed.append(((a, b, c), corner, 1))
            corner += 1
    return listed


RIM_ROWS = 248


def face_rows(offsets):
    a, b, c = offsets
    y_at, z_at = (7 if b < 0 else 0), (7 if c < 0 else 0)
    if a:
        if b == 0:
            return pl.ds(0, 64) if c == 0 else pl.ds(z_at, 8, stride=8)
        return pl.ds(8 * y_at, 8) if c == 0 else pl.ds(8 * y_at + z_at, 1)
    if b:
        return pl.ds(64, 64) if c == 0 else pl.ds(64 + z_at, 8, stride=8)
    return pl.ds(128, 64)


def rims_kernel(place, own_table, other_table, *rest):
    blocks, outs, gathered = rest[:8], rest[8:12], rest[12]
    core, low_x, depth = place[0], place[1], place[2]
    for number in range(8):
        gathered[number] = blocks[number][...]
    for peer in range(4):
        table = other_table if peer & 1 else own_table
        slot = core ^ (peer >> 1)
        out = outs[peer]
        out[240:248, :] = jnp.zeros((8, 128), F32)

        def load(offsets):
            entry = table[slot, DIRECTIONS.index(offsets)]
            found = jnp.clip(entry, 0, 31)
            here = (entry >= 0) & ((found & 1) == core) & (((found >> 1) & 1) == low_x)
            value = gathered[(depth - (found >> 2)) & 7, face_rows(offsets), :]
            return jnp.where(here, value, 0.0)

        for offsets, begin, count in rim_list():
            up, down = load(offsets), load(tuple(-step for step in offsets))
            lane = lax.broadcasted_iota(jnp.int32, (count, 128), 1)
            out[begin : begin + count, :] = jnp.where(lane < 64, up, down)


def cut_rims(place, own_table, other_table, blocks):
    outs = tuple(close((RIM_ROWS, 128)) for _ in range(4))
    return call(rims_kernel, outs, [pltpu.VMEM((8, 192, 128), F32)], touched=1000000)(
        in_specs=[SMEM, SMEM, SMEM] + [VMEM] * 8, out_specs=tuple([VMEM] * 4)
    )(place, own_table, other_table, *near(blocks))


def fill_rims(rims, padded):
    def at(x, y):
        return (x * 10 + y) * ROWS

    for upward, begin, count in rim_list():
        for sign in (1, -1):
            a, b, c = (sign * step for step in upward)
            side = 0 if sign > 0 else 64
            value = rims[begin : begin + count, side : side + 64]
            px, py = {-1: 0, 1: 9}.get(a), {-1: 0, 1: 9}.get(b)
            row = {-1: 7, 0: 8, 1: 16}[c]
            if count == 64:
                for n in range(8):
                    piece = value[8 * n : 8 * n + 8]
                    if a:
                        padded[pl.ds(at(px, 1 + n) + 8, 8), :] = piece
                    elif b:
                        padded[pl.ds(at(1 + n, py) + 8, 8), :] = piece
                    else:
                        padded[pl.ds(at(1 + n, 1) + row, 8, stride=ROWS), :] = piece
            elif count == 1:
                padded[pl.ds(at(px, py) + row, 1), :] = value
            elif c == 0:
                padded[pl.ds(at(px, py) + 8, 8), :] = value
            elif a:
                padded[pl.ds(at(px, 1) + row, 8, stride=ROWS), :] = value
            else:
                padded[pl.ds(at(1, py) + row, 8, stride=10 * ROWS), :] = value


def conv_kernel(place, rows, *rest):
    pieces = rest[:4]
    high, low = rest[4:6]
    outs = rest[6:14]
    rims, padded, columns, total, turned = rest[14:]
    rims[...] = (pieces[0][...] + pieces[1][...]) + (pieces[2][...] + pieces[3][...])
    for x in range(8):
        for y in range(8):
            padded[pl.ds(((1 + x) * 10 + 1 + y) * ROWS + 8, 8), :] = rows[pl.ds(x * 64 + y * 8, 8), :]
    fill_rims(rims, padded)
    for spot in range(100):
        before = padded[pl.ds(spot * ROWS + 7, 8), :]
        same = padded[pl.ds(spot * ROWS + 8, 8), :]
        after = padded[pl.ds(spot * ROWS + 9, 8), :]
        columns[spot // 10, spot % 10, :, 0:128] = jnp.concatenate([before, same], axis=1)
        columns[spot // 10, spot % 10, :, 128:192] = after

    dot = functools.partial(jnp.dot, preferred_element_type=F32)
    for p in range(3):
        sums = None
        for q in range(3):
            values = columns[p : p + 8, q : q + 8, :, 0:192].reshape(512, 192)
            top = values.astype(BF16)
            rest_of = (values - top.astype(F32)).astype(BF16)
            tap = 9 * p + 3 * q
            heavy = high[tap : tap + 3].reshape(192, 512)
            light = low[tap : tap + 3].reshape(192, 512)
            part = dot(top, heavy) + (dot(rest_of, heavy) + dot(top, light))
            sums = part if sums is None else sums + part
        if p == 0:
            total[...] = sums
        else:
            total[...] += sums
    turned[...] = total[...].T
    chip = place[3]
    for step, (along, across) in enumerate(ROUTES + ((0, 0),)):
        target = (((chip >> 1) + along) & 3) * 2 + ((chip & 1) ^ across)
        outs[step][...] = turned[pl.ds(pl.multiple_of(target * 64, 64), 64), :]


def conv(place, rows, rims, high, low):
    outs = tuple(close((64, 512)) for _ in range(8))
    scratch = [
        pltpu.VMEM((RIM_ROWS, 128), F32),
        pltpu.VMEM((100 * ROWS, 64), F32),
        pltpu.VMEM((10, 10, 8, 256), F32),
        pltpu.VMEM((512, 512), F32),
        pltpu.VMEM((512, 512), F32),
    ]
    return call(
        conv_kernel, outs, scratch, flops=2 * 3 * 1024 * 1728 * 256, touched=8000000, room=24
    )(
        in_specs=[SMEM] + [VMEM] * 7, out_specs=tuple([VMEM] * 8)
    )(place, *near([rows, *rims, high, low]))


def to_other_core(value):
    return lax.ppermute(value, "chan", [(i, i ^ 1) for i in range(16)])


def to_other_x(value):
    return lax.ppermute(value, "leaf", [(i, i ^ 1) for i in range(16)])


def to_other_both(value):
    pairs = [(16 * i + j, 16 * (i ^ 1) + (j ^ 1)) for i in range(16) for j in range(16)]
    return lax.ppermute(value, ("leaf", "chan"), pairs)


def gather_rims(place, tables, faces, early=(), late=()):
    found = [faces] + [None] * 7
    for step in (4, 3, -3, 2, -2, 1, -1):
        if step == 1 and early:
            faces, early, found[4] = lax.optimization_barrier((faces, early, found[4]))
        found[step % 8] = lax.ppermute(faces, "leaf", [(i, (i + 2 * step) % 16) for i in range(16)])
    found, late = lax.optimization_barrier((found, late))
    tables = early[0] if early else tables
    own, beside, across, both = cut_rims(place, *tables, found)
    return [own, to_other_both(both), to_other_x(beside), to_other_core(across)], early, late


ROUTES = ((2, 1), (1, 1), (3, 1), (2, 0), (0, 1), (1, 0), (3, 0))


def route_target(device, route):
    return (device // 4 + route[0]) % 4 * 4 + ((device % 4) ^ (2 * route[1]))


def add_over_chips(parts):
    landed = [parts[7]]
    for part, route in zip(parts, ROUTES):
        landed.append(lax.ppermute(part, "chan", [(i, route_target(i, route)) for i in range(16)]))
    return landed


def body(features, leaf_counts, occupancy, neighbours, weight_in, bias_in, weight_out, bias_out):
    leaf, chan = lax.axis_index("leaf"), lax.axis_index("chan")
    core = chan % 2
    place = jnp.stack([core, leaf % 2, leaf // 2, chan // 2]).astype(jnp.int32)
    others = to_other_core(features)
    _, weight_in, weight_out = lax.optimization_barrier((others, weight_in, weight_out))
    rows, faces = call(features_kernel, (close((512, 64)), close((192, 128))))(
        in_specs=[SMEM, SMEM, VMEM, VMEM, VMEM], out_specs=(VMEM, VMEM)
    )(place, leaf_counts, occupancy, features, *near([others]))
    tables = neighbours, to_other_x(neighbours)
    biases = jnp.stack([bias_in, bias_out])
    biases = biases, to_other_core(biases)
    weights = split_weights(place, weight_in, to_other_core(weight_in))
    weights_out = split_weights(place, weight_out, to_other_core(weight_out))

    rims, (tables, biases), (weights, weights_out) = gather_rims(
        place, tables, faces, (tables, biases), (weights, weights_out)
    )
    parts = add_over_chips(conv(place, rows, rims, *weights))
    rows, faces = call(hidden_kernel, (close((512, 64)), close((192, 128))))(
        in_specs=[SMEM, SMEM] + [VMEM] * 11, out_specs=(VMEM, VMEM)
    )(place, leaf_counts, occupancy, *biases, *near(parts))

    rims, _, _ = gather_rims(place, tables, faces)
    parts = add_over_chips(conv(place, rows, rims, *weights_out))
    keep, give = call(result_kernel, (close((32, 512)), close((32, 512))))(
        in_specs=[SMEM, SMEM] + [VMEM] * 11, out_specs=(VMEM, VMEM)
    )(place, leaf_counts, occupancy, *biases, *near(parts))
    return call(merge_kernel, arr((32, 2, 512)))(in_specs=[SMEM, VMEM, VMEM], out_specs=VMEM)(
        place, *near([keep, to_other_core(give)])
    )


def solution(mesh):
    placed = (
        P("chan", "leaf", None),
        P("leaf"),
        P("leaf", None),
        P("leaf", None),
        P(None, "chan", None),
        P("chan"),
        P(None, "chan", None),
        P("chan"),
    )
    return jax.shard_map(
        body, mesh=mesh, in_specs=placed, out_specs=P("chan", "leaf", None), check_vma=False
    )
```

profile of v0, /device:TPU:1, one launch (start us, length us, event | category | flops | bytes accessed | tf_op | source)
XLA Modules:
  0.0 136.7 jit_solution(13361972804275557422)
XLA Ops:
  0.0 3.2 %collective-permute-start = (f32[32,2,512]{2,1,0:T(2,128)}, f32[32,2,512]{2,1,0:T(2,128)S(1)}, u32[]{:S(2)}, u32[]{:S(2)}) collective-permute-start(f32[32,2,512]{2,1,0:T(2,128)} %own.1), channel_id=1, source_target_pairs={{0,1},{1,0},{2,3},{3,2},{4,5},{5,4},{6,7},{7,6},{8,9},{9,8},{10,11... | collective-permute-start | bytes 393224 | tf_op jit(solution)/shard_map/ppermute | solution.py:295
  9.7 6.5 %collective-permute-start.3 = (f32[192,128]{1,0:T(8,128)S(1)}, f32[192,128]{1,0:T(8,128)S(1)}, u32[]{:S(2)}, u32[]{:S(2)}) collective-permute-start(f32[192,128]{1,0:T(8,128)S(1)} %get-tuple-element.81.rest_0_), channel_id=1, source_target_pairs={{0,128},{16,144},{32,160},{48,176},{64,192},{80,208},{96,224},{112... | collective-permute-start | bytes 294920 | tf_op jit(solution)/shard_map/ppermute | solution.py:312
  20.3 4.3 %collective-permute-start.7 = (f32[192,128]{1,0:T(8,128)S(1)}, f32[192,128]{1,0:T(8,128)S(1)}, u32[]{:S(2)}, u32[]{:S(2)}) collective-permute-start(f32[192,128]{1,0:T(8,128)S(1)} %get-tuple-element.81.rest_0_), channel_id=1, source_target_pairs={{0,160},{16,176},{32,192},{48,208},{64,224},{80,240},{96,0},{112,1... | collective-permute-start | bytes 294920 | tf_op jit(solution)/shard_map/ppermute | solution.py:312
  24.6 2.4 %collective-permute-start.8 = (f32[192,128]{1,0:T(8,128)S(1)}, f32[192,128]{1,0:T(8,128)S(1)}, u32[]{:S(2)}, u32[]{:S(2)}) collective-permute-start(f32[192,128]{1,0:T(8,128)S(1)} %get-tuple-element.81.rest_0_), channel_id=1, source_target_pairs={{0,192},{16,208},{32,224},{48,240},{64,0},{80,16},{96,32},{112,48}... | collective-permute-start | bytes 294920 | tf_op jit(solution)/shard_map/ppermute | solution.py:312
  27.0 2.7 %collective-permute-start.9 = (f32[192,128]{1,0:T(8,128)S(1)}, f32[192,128]{1,0:T(8,128)S(1)}, u32[]{:S(2)}, u32[]{:S(2)}) collective-permute-start(f32[192,128]{1,0:T(8,128)S(1)} %get-tuple-element.81.rest_0_), channel_id=1, source_target_pairs={{0,224},{16,240},{32,0},{48,16},{64,32},{80,48},{96,64},{112,80},{... | collective-permute-start | bytes 294920 | tf_op jit(solution)/shard_map/ppermute | solution.py:312
  35.0 2.1 %collective-permute-done.9.rest_7_ = f32[192,128]{1,0:T(8,128)S(1)} collective-permute-done((f32[192,128]{1,0:T(8,128)S(1)}, f32[192,128]{1,0:T(8,128)S(1)}, u32[]{:S(2)}, u32[]{:S(2)}) %collective-permute-start.9) | collective-permute-done | bytes 98336 | tf_op jit(solution)/shard_map/ppermute | solution.py:312
  38.3 2.4 %collective-permute-start.12 = (f32[248,128]{1,0:T(8,128)S(1)}, f32[248,128]{1,0:T(8,128)S(1)}, u32[]{:S(2)}, u32[]{:S(2)}) collective-permute-start(f32[248,128]{1,0:T(8,128)S(1)} %get-tuple-element.90), channel_id=1, source_target_pairs={{0,17},{1,16},{2,19},{3,18},{4,21},{5,20},{6,23},{7,22},{8,25},{9,... | collective-permute-start | bytes 380936 | tf_op jit(solution)/shard_map/ppermute | solution.py:304
  41.9 2.1 %collective-permute-done.12.rest_1_ = f32[248,128]{1,0:T(8,128)S(1)} collective-permute-done((f32[248,128]{1,0:T(8,128)S(1)}, f32[248,128]{1,0:T(8,128)S(1)}, u32[]{:S(2)}, u32[]{:S(2)}) %collective-permute-start.12) | collective-permute-done | bytes 127008 | tf_op jit(solution)/shard_map/ppermute | solution.py:304
  44.0 3.4 %collective-permute-done.13.rest_2_ = f32[248,128]{1,0:T(8,128)S(1)} collective-permute-done((f32[248,128]{1,0:T(8,128)S(1)}, f32[248,128]{1,0:T(8,128)S(1)}, u32[]{:S(2)}, u32[]{:S(2)}) %collective-permute-start.13) | collective-permute-done | bytes 127008 | tf_op jit(solution)/shard_map/ppermute | solution.py:299
  47.4 5.0 %shard_map.86 = (f32[64,512]{1,0:T(8,128)S(1)}, f32[64,512]{1,0:T(8,128)S(1)}, f32[64,512]{1,0:T(8,128)S(1)}, f32[64,512]{1,0:T(8,128)S(1)}, f32[64,512]{1,0:T(8...) custom-call(s32[4]{0:T(128)S(1)} %pad_add_fusion.place, ...), custom_call_target="tpu_custom_call" | custom-call | flops 2717908992 | bytes 8000000 | tf_op jit(solution)/shard_map/pallas_call | solution.py:287
  52.4 5.5 %collective-permute-start.15 = (f32[64,512]{1,0:T(8,128)S(1)}, f32[64,512]{1,0:T(8,128)S(1)}, u32[]{:S(2)}, u32[]{:S(2)}) collective-permute-start(f32[64,512]{1,0:T(8,128)S(1)} %get-tuple-element.96), channel_id=1, source_target_pairs={{0,10},{1,11},{2,8},{3,9},{4,14},{5,15},{6,12},{7,13},{8,2},{9,3},... | collective-permute-start | bytes 393224 | tf_op jit(solution)/shard_map/ppermute | solution.py:329
  58.2 4.7 %collective-permute-start.17 = (f32[64,512]{1,0:T(8,128)S(1)}, f32[64,512]{1,0:T(8,128)S(1)}, u32[]{:S(2)}, u32[]{:S(2)}) collective-permute-start(f32[64,512]{1,0:T(8,128)S(1)} %get-tuple-element.98), channel_id=1, source_target_pairs={{0,14},{1,15},{2,12},{3,13},{4,2},{5,3},{6,0},{7,1},{8,6},{9,7},{1... | collective-permute-start | bytes 393224 | tf_op jit(solution)/shard_map/ppermute | solution.py:329
  63.9 2.3 %collective-permute-done.16.rest_2_ = f32[64,512]{1,0:T(8,128)S(1)} collective-permute-done((f32[64,512]{1,0:T(8,128)S(1)}, f32[64,512]{1,0:T(8,128)S(1)}, u32[]{:S(2)}, u32[]{:S(2)}) %collective-permute-start.16) | collective-permute-done | bytes 131104 | tf_op jit(solution)/shard_map/ppermute | solution.py:329
  69.8 3.2 %collective-permute-done.20.rest_6_ = f32[64,512]{1,0:T(8,128)S(1)} collective-permute-done((f32[64,512]{1,0:T(8,128)S(1)}, f32[64,512]{1,0:T(8,128)S(1)}, u32[]{:S(2)}, u32[]{:S(2)}) %collective-permute-start.20) | collective-permute-done | bytes 131104 | tf_op jit(solution)/shard_map/ppermute | solution.py:329
  76.1 2.8 %collective-permute-start.24 = (f32[192,128]{1,0:T(8,128)S(1)}, f32[192,128]{1,0:T(8,128)S(1)}, u32[]{:S(2)}, u32[]{:S(2)}) collective-permute-start(f32[192,128]{1,0:T(8,128)S(1)} %get-tuple-element.105.rest_0_), channel_id=1, source_target_pairs={{0,96},{16,112},{32,128},{48,144},{64,160},{80,176},{96,192},{112,... | collective-permute-start | bytes 294920 | tf_op jit(solution)/shard_map/ppermute | solution.py:312
  80.3 3.9 %collective-permute-start.26 = (f32[192,128]{1,0:T(8,128)S(1)}, f32[192,128]{1,0:T(8,128)S(1)}, u32[]{:S(2)}, u32[]{:S(2)}) collective-permute-start(f32[192,128]{1,0:T(8,128)S(1)} %get-tuple-element.105.rest_0_), channel_id=1, source_target_pairs={{0,160},{16,176},{32,192},{48,208},{64,224},{80,240},{96,0},{112,1... | collective-permute-start | bytes 294920 | tf_op jit(solution)/shard_map/ppermute | solution.py:312
  86.6 3.0 %collective-permute-done.24.rest_3_ = f32[192,128]{1,0:T(8,128)S(1)} collective-permute-done((f32[192,128]{1,0:T(8,128)S(1)}, f32[192,128]{1,0:T(8,128)S(1)}, u32[]{:S(2)}, u32[]{:S(2)}) %collective-permute-start.24) | collective-permute-done | bytes 98336 | tf_op jit(solution)/shard_map/ppermute | solution.py:312
  89.6 2.4 %collective-permute-done.25.rest_4_ = f32[192,128]{1,0:T(8,128)S(1)} collective-permute-done((f32[192,128]{1,0:T(8,128)S(1)}, f32[192,128]{1,0:T(8,128)S(1)}, u32[]{:S(2)}, u32[]{:S(2)}) %collective-permute-start.25) | collective-permute-done | bytes 98336 | tf_op jit(solution)/shard_map/ppermute | solution.py:312
  92.0 7.0 %collective-permute-done.27.rest_6_ = f32[192,128]{1,0:T(8,128)S(1)} collective-permute-done((f32[192,128]{1,0:T(8,128)S(1)}, f32[192,128]{1,0:T(8,128)S(1)}, u32[]{:S(2)}, u32[]{:S(2)}) %collective-permute-start.27) | collective-permute-done | bytes 98336 | tf_op jit(solution)/shard_map/ppermute | solution.py:312
  103.9 2.6 %collective-permute-done.29.rest_1_ = f32[248,128]{1,0:T(8,128)S(1)} collective-permute-done((f32[248,128]{1,0:T(8,128)S(1)}, f32[248,128]{1,0:T(8,128)S(1)}, u32[]{:S(2)}, u32[]{:S(2)}) %collective-permute-start.29) | collective-permute-done | bytes 127008 | tf_op jit(solution)/shard_map/ppermute | solution.py:304
  106.5 3.1 %collective-permute-done.30.rest_2_ = f32[248,128]{1,0:T(8,128)S(1)} collective-permute-done((f32[248,128]{1,0:T(8,128)S(1)}, f32[248,128]{1,0:T(8,128)S(1)}, u32[]{:S(2)}, u32[]{:S(2)}) %collective-permute-start.30) | collective-permute-done | bytes 127008 | tf_op jit(solution)/shard_map/ppermute | solution.py:299
  109.6 5.0 %shard_map.89 = (f32[64,512]{1,0:T(8,128)S(1)}, f32[64,512]{1,0:T(8,128)S(1)}, f32[64,512]{1,0:T(8,128)S(1)}, f32[64,512]{1,0:T(8,128)S(1)}, f32[64,512]{1,0:T(8...) custom-call(s32[4]{0:T(128)S(1)} %pad_add_fusion.place, ...), custom_call_target="tpu_custom_call" | custom-call | flops 2717908992 | bytes 8000000 | tf_op jit(solution)/shard_map/pallas_call | solution.py:287
  114.6 3.0 %collective-permute-start.32 = (f32[64,512]{1,0:T(8,128)S(1)}, f32[64,512]{1,0:T(8,128)S(1)}, u32[]{:S(2)}, u32[]{:S(2)}) collective-permute-start(f32[64,512]{1,0:T(8,128)S(1)} %get-tuple-element.120), channel_id=1, source_target_pairs={{0,10},{1,11},{2,8},{3,9},{4,14},{5,15},{6,12},{7,13},{8,2},{9,3},... | collective-permute-start | bytes 393224 | tf_op jit(solution)/shard_map/ppermute | solution.py:329
  118.9 3.8 %collective-permute-start.34 = (f32[64,512]{1,0:T(8,128)S(1)}, f32[64,512]{1,0:T(8,128)S(1)}, u32[]{:S(2)}, u32[]{:S(2)}) collective-permute-start(f32[64,512]{1,0:T(8,128)S(1)} %get-tuple-element.122), channel_id=1, source_target_pairs={{0,14},{1,15},{2,12},{3,13},{4,2},{5,3},{6,0},{7,1},{8,6},{9,7},{1... | collective-permute-start | bytes 393224 | tf_op jit(solution)/shard_map/ppermute | solution.py:329
  (84 shorter events, 49.4 us)
Async XLA Ops:
  5.1 21.9 %collective-permute-start.10 = (f32[27,32,512]{2,1,0:T(8,128)}, f32[27,32,512]{2,1,0:T(8,128)S(1)}, u32[]{:S(2)}, u32[]{:S(2)}) collective-permute-start(f32[27,32,512]{2,1,0:T(8,128)} %own.2), channel_id=1, source_target_pairs={{0,1},{1,0},{2,3},{3,2},{4,5},{5,4},{6,7},{7,6},{8,9},{9,8},{10,11... | collective-permute-start | bytes 5308424 | tf_op jit(solution)/shard_map/ppermute | solution.py:295
  5.5 21.5 %collective-permute-start.11 = (f32[27,32,512]{2,1,0:T(8,128)}, f32[27,32,512]{2,1,0:T(8,128)S(1)}, u32[]{:S(2)}, u32[]{:S(2)}) collective-permute-start(f32[27,32,512]{2,1,0:T(8,128)} %own.3), channel_id=1, source_target_pairs={{0,1},{1,0},{2,3},{3,2},{4,5},{5,4},{6,7},{7,6},{8,9},{9,8},{10,11... | collective-permute-start | bytes 5308424 | tf_op jit(solution)/shard_map/ppermute | solution.py:295
  5.6 12.4 %collective-permute-start.1 = (s32[2,26]{1,0:T(2,128)}, s32[2,26]{1,0:T(2,128)S(1)}, u32[]{:S(2)}, u32[]{:S(2)}) collective-permute-start(s32[2,26]{1,0:T(2,128)} %own_table.1), channel_id=1, source_target_pairs={{0,16},{16,0},{32,48},{48,32},{64,80},{80,64},{96,112},{112,96},{1... | collective-permute-start | bytes 632 | tf_op jit(solution)/shard_map/ppermute | solution.py:299
  9.7 10.6 %collective-permute-start.3 = (f32[192,128]{1,0:T(8,128)S(1)}, f32[192,128]{1,0:T(8,128)S(1)}, u32[]{:S(2)}, u32[]{:S(2)}) collective-permute-start(f32[192,128]{1,0:T(8,128)S(1)} %get-tuple-element.81.rest_0_), channel_id=1, source_target_pairs={{0,128},{16,144},{32,160},{48,176},{64,192},{80,208},{96,224},{112... | collective-permute-start | bytes 294920 | tf_op jit(solution)/shard_map/ppermute | solution.py:312
  16.1 8.5 %collective-permute-start.5 = (f32[192,128]{1,0:T(8,128)S(1)}, f32[192,128]{1,0:T(8,128)S(1)}, u32[]{:S(2)}, u32[]{:S(2)}) collective-permute-start(f32[192,128]{1,0:T(8,128)S(1)} %get-tuple-element.81.rest_0_), channel_id=1, source_target_pairs={{0,64},{16,80},{32,96},{48,112},{64,128},{80,144},{96,160},{112,17... | collective-permute-start | bytes 294920 | tf_op jit(solution)/shard_map/ppermute | solution.py:312
  20.1 13.8 %collective-permute-start.6 = (f32[192,128]{1,0:T(8,128)S(1)}, f32[192,128]{1,0:T(8,128)S(1)}, u32[]{:S(2)}, u32[]{:S(2)}) collective-permute-start(f32[192,128]{1,0:T(8,128)S(1)} %get-tuple-element.81.rest_0_), channel_id=1, source_target_pairs={{0,96},{16,112},{32,128},{48,144},{64,160},{80,176},{96,192},{112,... | collective-permute-start | bytes 294920 | tf_op jit(solution)/shard_map/ppermute | solution.py:312
  20.3 13.6 %collective-permute-start.7 = (f32[192,128]{1,0:T(8,128)S(1)}, f32[192,128]{1,0:T(8,128)S(1)}, u32[]{:S(2)}, u32[]{:S(2)}) collective-permute-start(f32[192,128]{1,0:T(8,128)S(1)} %get-tuple-element.81.rest_0_), channel_id=1, source_target_pairs={{0,160},{16,176},{32,192},{48,208},{64,224},{80,240},{96,0},{112,1... | collective-permute-start | bytes 294920 | tf_op jit(solution)/shard_map/ppermute | solution.py:312
  24.6 10.4 %collective-permute-start.8 = (f32[192,128]{1,0:T(8,128)S(1)}, f32[192,128]{1,0:T(8,128)S(1)}, u32[]{:S(2)}, u32[]{:S(2)}) collective-permute-start(f32[192,128]{1,0:T(8,128)S(1)} %get-tuple-element.81.rest_0_), channel_id=1, source_target_pairs={{0,192},{16,208},{32,224},{48,240},{64,0},{80,16},{96,32},{112,48}... | collective-permute-start | bytes 294920 | tf_op jit(solution)/shard_map/ppermute | solution.py:312
  27.0 8.0 %collective-permute-start.4 = (f32[192,128]{1,0:T(8,128)S(1)}, f32[192,128]{1,0:T(8,128)S(1)}, u32[]{:S(2)}, u32[]{:S(2)}) collective-permute-start(f32[192,128]{1,0:T(8,128)S(1)} %get-tuple-element.81.rest_0_), channel_id=1, source_target_pairs={{0,32},{16,48},{32,64},{48,80},{64,96},{80,112},{96,128},{112,144}... | collective-permute-start | bytes 294920 | tf_op jit(solution)/shard_map/ppermute | solution.py:312
  27.0 10.1 %collective-permute-start.9 = (f32[192,128]{1,0:T(8,128)S(1)}, f32[192,128]{1,0:T(8,128)S(1)}, u32[]{:S(2)}, u32[]{:S(2)}) collective-permute-start(f32[192,128]{1,0:T(8,128)S(1)} %get-tuple-element.81.rest_0_), channel_id=1, source_target_pairs={{0,224},{16,240},{32,0},{48,16},{64,32},{80,48},{96,64},{112,80},{... | collective-permute-start | bytes 294920 | tf_op jit(solution)/shard_map/ppermute | solution.py:312
  52.4 10.8 %collective-permute-start.15 = (f32[64,512]{1,0:T(8,128)S(1)}, f32[64,512]{1,0:T(8,128)S(1)}, u32[]{:S(2)}, u32[]{:S(2)}) collective-permute-start(f32[64,512]{1,0:T(8,128)S(1)} %get-tuple-element.96), channel_id=1, source_target_pairs={{0,10},{1,11},{2,8},{3,9},{4,14},{5,15},{6,12},{7,13},{8,2},{9,3},... | collective-permute-start | bytes 393224 | tf_op jit(solution)/shard_map/ppermute | solution.py:329
  57.9 8.3 %collective-permute-start.16 = (f32[64,512]{1,0:T(8,128)S(1)}, f32[64,512]{1,0:T(8,128)S(1)}, u32[]{:S(2)}, u32[]{:S(2)}) collective-permute-start(f32[64,512]{1,0:T(8,128)S(1)} %get-tuple-element.97), channel_id=1, source_target_pairs={{0,6},{1,7},{2,4},{3,5},{4,10},{5,11},{6,8},{7,9},{8,14},{9,15},{1... | collective-permute-start | bytes 393224 | tf_op jit(solution)/shard_map/ppermute | solution.py:329
  58.2 9.7 %collective-permute-start.17 = (f32[64,512]{1,0:T(8,128)S(1)}, f32[64,512]{1,0:T(8,128)S(1)}, u32[]{:S(2)}, u32[]{:S(2)}) collective-permute-start(f32[64,512]{1,0:T(8,128)S(1)} %get-tuple-element.98), channel_id=1, source_target_pairs={{0,14},{1,15},{2,12},{3,13},{4,2},{5,3},{6,0},{7,1},{8,6},{9,7},{1... | collective-permute-start | bytes 393224 | tf_op jit(solution)/shard_map/ppermute | solution.py:329
  63.2 9.8 %collective-permute-start.20 = (f32[64,512]{1,0:T(8,128)S(1)}, f32[64,512]{1,0:T(8,128)S(1)}, u32[]{:S(2)}, u32[]{:S(2)}) collective-permute-start(f32[64,512]{1,0:T(8,128)S(1)} %get-tuple-element.101), channel_id=1, source_target_pairs={{0,4},{1,5},{2,6},{3,7},{4,8},{5,9},{6,10},{7,11},{8,12},{9,13},{1... | collective-permute-start | bytes 393224 | tf_op jit(solution)/shard_map/ppermute | solution.py:329
  74.1 10.2 %collective-permute-start.22 = (f32[192,128]{1,0:T(8,128)S(1)}, f32[192,128]{1,0:T(8,128)S(1)}, u32[]{:S(2)}, u32[]{:S(2)}) collective-permute-start(f32[192,128]{1,0:T(8,128)S(1)} %get-tuple-element.105.rest_0_), channel_id=1, source_target_pairs={{0,32},{16,48},{32,64},{48,80},{64,96},{80,112},{96,128},{112,144}... | collective-permute-start | bytes 294920 | tf_op jit(solution)/shard_map/ppermute | solution.py:312
  74.2 11.9 %collective-permute-start.23 = (f32[192,128]{1,0:T(8,128)S(1)}, f32[192,128]{1,0:T(8,128)S(1)}, u32[]{:S(2)}, u32[]{:S(2)}) collective-permute-start(f32[192,128]{1,0:T(8,128)S(1)} %get-tuple-element.105.rest_0_), channel_id=1, source_target_pairs={{0,64},{16,80},{32,96},{48,112},{64,128},{80,144},{96,160},{112,17... | collective-permute-start | bytes 294920 | tf_op jit(solution)/shard_map/ppermute | solution.py:312
  76.1 13.5 %collective-permute-start.24 = (f32[192,128]{1,0:T(8,128)S(1)}, f32[192,128]{1,0:T(8,128)S(1)}, u32[]{:S(2)}, u32[]{:S(2)}) collective-permute-start(f32[192,128]{1,0:T(8,128)S(1)} %get-tuple-element.105.rest_0_), channel_id=1, source_target_pairs={{0,96},{16,112},{32,128},{48,144},{64,160},{80,176},{96,192},{112,... | collective-permute-start | bytes 294920 | tf_op jit(solution)/shard_map/ppermute | solution.py:312
  79.0 13.0 %collective-permute-start.25 = (f32[192,128]{1,0:T(8,128)S(1)}, f32[192,128]{1,0:T(8,128)S(1)}, u32[]{:S(2)}, u32[]{:S(2)}) collective-permute-start(f32[192,128]{1,0:T(8,128)S(1)} %get-tuple-element.105.rest_0_), channel_id=1, source_target_pairs={{0,128},{16,144},{32,160},{48,176},{64,192},{80,208},{96,224},{112... | collective-permute-start | bytes 294920 | tf_op jit(solution)/shard_map/ppermute | solution.py:312
  80.3 11.7 %collective-permute-start.26 = (f32[192,128]{1,0:T(8,128)S(1)}, f32[192,128]{1,0:T(8,128)S(1)}, u32[]{:S(2)}, u32[]{:S(2)}) collective-permute-start(f32[192,128]{1,0:T(8,128)S(1)} %get-tuple-element.105.rest_0_), channel_id=1, source_target_pairs={{0,160},{16,176},{32,192},{48,208},{64,224},{80,240},{96,0},{112,1... | collective-permute-start | bytes 294920 | tf_op jit(solution)/shard_map/ppermute | solution.py:312
  84.3 14.7 %collective-permute-start.27 = (f32[192,128]{1,0:T(8,128)S(1)}, f32[192,128]{1,0:T(8,128)S(1)}, u32[]{:S(2)}, u32[]{:S(2)}) collective-permute-start(f32[192,128]{1,0:T(8,128)S(1)} %get-tuple-element.105.rest_0_), channel_id=1, source_target_pairs={{0,192},{16,208},{32,224},{48,240},{64,0},{80,16},{96,32},{112,48}... | collective-permute-start | bytes 294920 | tf_op jit(solution)/shard_map/ppermute | solution.py:312
  86.1 13.7 %collective-permute-start.28 = (f32[192,128]{1,0:T(8,128)S(1)}, f32[192,128]{1,0:T(8,128)S(1)}, u32[]{:S(2)}, u32[]{:S(2)}) collective-permute-start(f32[192,128]{1,0:T(8,128)S(1)} %get-tuple-element.105.rest_0_), channel_id=1, source_target_pairs={{0,224},{16,240},{32,0},{48,16},{64,32},{80,48},{96,64},{112,80},{... | collective-permute-start | bytes 294920 | tf_op jit(solution)/shard_map/ppermute | solution.py:312
  114.6 9.6 %collective-permute-start.32 = (f32[64,512]{1,0:T(8,128)S(1)}, f32[64,512]{1,0:T(8,128)S(1)}, u32[]{:S(2)}, u32[]{:S(2)}) collective-permute-start(f32[64,512]{1,0:T(8,128)S(1)} %get-tuple-element.120), channel_id=1, source_target_pairs={{0,10},{1,11},{2,8},{3,9},{4,14},{5,15},{6,12},{7,13},{8,2},{9,3},... | collective-permute-start | bytes 393224 | tf_op jit(solution)/shard_map/ppermute | solution.py:329
  118.9 9.4 %collective-permute-start.34 = (f32[64,512]{1,0:T(8,128)S(1)}, f32[64,512]{1,0:T(8,128)S(1)}, u32[]{:S(2)}, u32[]{:S(2)}) collective-permute-start(f32[64,512]{1,0:T(8,128)S(1)} %get-tuple-element.122), channel_id=1, source_target_pairs={{0,14},{1,15},{2,12},{3,13},{4,2},{5,3},{6,0},{7,1},{8,6},{9,7},{1... | collective-permute-start | bytes 393224 | tf_op jit(solution)/shard_map/ppermute | solution.py:329
  124.2 8.2 %collective-permute-start.37 = (f32[64,512]{1,0:T(8,128)S(1)}, f32[64,512]{1,0:T(8,128)S(1)}, u32[]{:S(2)}, u32[]{:S(2)}) collective-permute-start(f32[64,512]{1,0:T(8,128)S(1)} %get-tuple-element.125), channel_id=1, source_target_pairs={{0,4},{1,5},{2,6},{3,7},{4,8},{5,9},{6,10},{7,11},{8,12},{9,13},{1... | collective-permute-start | bytes 393224 | tf_op jit(solution)/shard_map/ppermute | solution.py:329
  (24 other events, 129.3 us)
where the time goes:
time: 137 us
  starting transfers between devices  64.8 us (47%)
  waiting for transfers between devices  46.4 us (34%)
  Pallas kernels  19.1 us (14%)
  local copies, waits for them, and re-layouts  4.82 us (4%)
    ppermute x14, starting transfers between devices, gather_rims(): lax.ppermute(faces, 'leaf', [(i, (i + 2 * step) % 16) for i in range(16)])  29.7 us
    ppermute x14, starting transfers between devices, add_over_chips(): lax.ppermute(part, 'chan', [(i, route_target(i, route)) for i in range(16)])  22.4 us
    ppermute x14, waiting for transfers between devices, gather_rims(): lax.ppermute(faces, 'leaf', [(i, (i + 2 * step) % 16) for i in range(16)])  16.3 us
    ppermute x14, waiting for transfers between devices, add_over_chips(): lax.ppermute(part, 'chan', [(i, route_target(i, route)) for i in range(16)])  16 us
    pallas_call x2, Pallas kernels, conv(): call(conv_kernel, outs, scratch, flops=2 * 3 * 1024 * 1728 * 256, touched...  10.1 us
    ppermute x3, waiting for transfers between devices, to_other_x(): return lax.ppermute(value, 'leaf', [(i, i ^ 1) for i in range(16)])  6.42 us
    ppermute x7, starting transfers between devices, to_other_core(): return lax.ppermute(value, 'chan', [(i, i ^ 1) for i in range(16)])  6.26 us
    unnamed x16, local copies, waits for them, and re-layouts  4.82 us
  transfers between devices with their start and end apart: 40, of which 23 were waited for; matrix products, arithmetic and copies ran while one was open for 1% of the time, Pallas kernels for 2%

commit v1 on v0

--- a/solution.py
+++ b/solution.py
@@ -160,6 +160,7 @@
 
 
 RIM_ROWS = 248
+SENT = (4, 3, -3, 2, -2, 1, -1)
 
 
 def face_rows(offsets):
@@ -177,8 +178,8 @@
 def rims_kernel(place, own_table, other_table, *rest):
     blocks, outs, gathered = rest[:8], rest[8:12], rest[12]
     core, low_x, depth = place[0], place[1], place[2]
-    for number in range(8):
-        gathered[number] = blocks[number][...]
+    for number, step in enumerate(SENT + (0,)):
+        gathered[step % 8] = blocks[number][...]
     for peer in range(4):
         table = other_table if peer & 1 else own_table
         slot = core ^ (peer >> 1)
@@ -304,16 +305,19 @@
     return lax.ppermute(value, ("leaf", "chan"), pairs)
 
 
-def gather_rims(place, tables, faces, early=(), late=()):
-    found = [faces] + [None] * 7
-    for step in (4, 3, -3, 2, -2, 1, -1):
+def gather_rims(place, tables, faces, early=(), weight=None):
+    found = []
+    for step in SENT:
         if step == 1 and early:
-            faces, early, found[4] = lax.optimization_barrier((faces, early, found[4]))
-        found[step % 8] = lax.ppermute(faces, "leaf", [(i, (i + 2 * step) % 16) for i in range(16)])
-    found, late = lax.optimization_barrier((found, late))
+            faces, early, found[0] = lax.optimization_barrier((faces, early, found[0]))
+        found.append(lax.ppermute(faces, "leaf", [(i, (i + 2 * step) % 16) for i in range(16)]))
+    if weight is not None:
+        found[1], weight = lax.optimization_barrier((found[1], weight))
+        weight = split_weights(place, weight, to_other_core(weight))
+        found, weight = lax.optimization_barrier((found, weight))
     tables = early[0] if early else tables
-    own, beside, across, both = cut_rims(place, *tables, found)
-    return [own, to_other_both(both), to_other_x(beside), to_other_core(across)], early, late
+    own, beside, across, both = cut_rims(place, *tables, found + [faces])
+    return [own, to_other_both(both), to_other_x(beside), to_other_core(across)], early, weight
 
 
 ROUTES = ((2, 1), (1, 1), (3, 1), (2, 0), (0, 1), (1, 0), (3, 0))
@@ -335,20 +339,18 @@
     core = chan % 2
     place = jnp.stack([core, leaf % 2, leaf // 2, chan // 2]).astype(jnp.int32)
     others = to_other_core(features)
-    _, weight_in, weight_out = lax.optimization_barrier((others, weight_in, weight_out))
     rows, faces = call(features_kernel, (close((512, 64)), close((192, 128))))(
         in_specs=[SMEM, SMEM, VMEM, VMEM, VMEM], out_specs=(VMEM, VMEM)
     )(place, leaf_counts, occupancy, features, *near([others]))
     tables = neighbours, to_other_x(neighbours)
     biases = jnp.stack([bias_in, bias_out])
     biases = biases, to_other_core(biases)
-    weights = split_weights(place, weight_in, to_other_core(weight_in))
-    weights_out = split_weights(place, weight_out, to_other_core(weight_out))
-
-    rims, (tables, biases), (weights, weights_out) = gather_rims(
-        place, tables, faces, (tables, biases), (weights, weights_out)
-    )
-    parts = add_over_chips(conv(place, rows, rims, *weights))
+    rims, (tables, biases), weights = gather_rims(place, tables, faces, (tables, biases), weight_in)
+    rims, weight_out = lax.optimization_barrier((rims, weight_out))
+    swapped = to_other_core(weight_out)
+    parts, swapped = lax.optimization_barrier((conv(place, rows, rims, *weights), swapped))
+    weights_out = split_weights(place, weight_out, swapped)
+    parts = add_over_chips(parts)
     rows, faces = call(hidden_kernel, (close((512, 64)), close((192, 128))))(
         in_specs=[SMEM, SMEM] + [VMEM] * 11, out_specs=(VMEM, VMEM)
     )(place, leaf_counts, occupancy, *biases, *near(parts))

time: 137 us -> 139 us (1.015)
  starting transfers between devices: 64.8 us -> 67 us
  local copies, waits for them, and re-layouts: 4.82 us -> 3.08 us
    ppermute x14, waiting for transfers between devices: 16.3 us -> 19.3 us  [gather_rims(): lax.ppermute(faces, 'leaf', [(i, (i + 2 * step) % 16) for i in range(16)])]
    ppermute x7, starting transfers between devices: 6.26 us -> 8.59 us  [to_other_core(): return lax.ppermute(value, 'chan', [(i, i ^ 1) for i in range(16)])]
    unnamed x16 -> x12, local copies, waits for them, and re-layouts: 4.82 us -> 3.08 us
    ppermute x7, waiting for transfers between devices: 2.93 us -> 1.37 us  [to_other_core(): return lax.ppermute(value, 'chan', [(i, i ^ 1) for i in range(16)])]
    ppermute x14, starting transfers between devices: 29.7 us -> 28.2 us  [gather_rims(): lax.ppermute(faces, 'leaf', [(i, (i + 2 * step) % 16) for i in range(16)])]
  transfers between devices with their start and end apart: 40 -> 40, of which waited for: 23 -> 20; matrix products, arithmetic and copies ran while one was open for 1% -> 1% of each run, Pallas kernels for 2% -> 5%
where the time goes in v1:
time: 139 us; the launch traced here: 138 us
  starting transfers between devices  67 us (48%)
  waiting for transfers between devices  47.3 us (34%)
  Pallas kernels  19 us (14%)
  local copies, waits for them, and re-layouts  3.08 us (2%)
    ppermute x14, starting transfers between devices, gather_rims(): lax.ppermute(faces, 'leaf', [(i, (i + 2 * step) % 16) for i in range(16)])  28.2 us
    ppermute x14, starting transfers between devices, add_over_chips(): lax.ppermute(part, 'chan', [(i, route_target(i, route)) for i in range(16)])  22.2 us
    ppermute x14, waiting for transfers between devices, gather_rims(): lax.ppermute(faces, 'leaf', [(i, (i + 2 * step) % 16) for i in range(16)])  19.3 us
    ppermute x14, waiting for transfers between devices, add_over_chips(): lax.ppermute(part, 'chan', [(i, route_target(i, route)) for i in range(16)])  16.7 us
    pallas_call x2, Pallas kernels, conv(): call(conv_kernel, outs, scratch, flops=2 * 3 * 1024 * 1728 * 256, touched...  9.98 us
    ppermute x7, starting transfers between devices, to_other_core(): return lax.ppermute(value, 'chan', [(i, i ^ 1) for i in range(16)])  8.59 us
    ppermute x3, waiting for transfers between devices, to_other_x(): return lax.ppermute(value, 'leaf', [(i, i ^ 1) for i in range(16)])  6.5 us
    ppermute x2, starting transfers between devices, to_other_both(): return lax.ppermute(value, ('leaf', 'chan'), pairs)  4.07 us
  transfers between devices with their start and end apart: 40, of which 20 were waited for; matrix products, arithmetic and copies ran while one was open for 1% of the time, Pallas kernels for 5%

profile of v1, /device:TPU:1, one launch (start us, length us, event | category | flops | bytes accessed | tf_op | source)
XLA Modules:
  0.0 138.0 jit_solution(14305009856520833667)
XLA Ops:
  0.0 3.2 %collective-permute-start = (f32[32,2,512]{2,1,0:T(2,128)}, f32[32,2,512]{2,1,0:T(2,128)S(1)}, u32[]{:S(2)}, u32[]{:S(2)}) collective-permute-start(f32[32,2,512]{2,1,0:T(2,128)} %own.1), channel_id=1, source_target_pairs={{0,1},{1,0},{2,3},{3,2},{4,5},{5,4},{6,7},{7,6},{8,9},{9,8},{10,11... | collective-permute-start | bytes 393224 | tf_op jit(solution)/shard_map/ppermute | solution.py:296
  6.8 2.7 %collective-permute-start.4 = (f32[192,128]{1,0:T(8,128)S(1)}, f32[192,128]{1,0:T(8,128)S(1)}, u32[]{:S(2)}, u32[]{:S(2)}) collective-permute-start(f32[192,128]{1,0:T(8,128)S(1)} %get-tuple-element.78.rest_7_), channel_id=1, source_target_pairs={{0,96},{16,112},{32,128},{48,144},{64,160},{80,176},{96,192},{112,... | collective-permute-start | bytes 294920 | tf_op jit(solution)/shard_map/ppermute | solution.py:313
  9.5 5.1 %collective-permute-done.4.rest_1_ = f32[192,128]{1,0:T(8,128)S(1)} collective-permute-done((f32[192,128]{1,0:T(8,128)S(1)}, f32[192,128]{1,0:T(8,128)S(1)}, u32[]{:S(2)}, u32[]{:S(2)}) %collective-permute-start.4) | collective-permute-done | bytes 98336 | tf_op jit(solution)/shard_map/ppermute | solution.py:313
  14.6 3.1 %collective-permute-start.10 = (f32[27,32,512]{2,1,0:T(8,128)}, f32[27,32,512]{2,1,0:T(8,128)S(1)}, u32[]{:S(2)}, u32[]{:S(2)}) collective-permute-start(f32[27,32,512]{2,1,0:T(8,128)} %own.2), channel_id=1, source_target_pairs={{0,1},{1,0},{2,3},{3,2},{4,5},{5,4},{6,7},{7,6},{8,9},{9,8},{10,11... | collective-permute-start | bytes 5308424 | tf_op jit(solution)/shard_map/ppermute | solution.py:296
  19.0 5.3 %collective-permute-start.3 = (f32[192,128]{1,0:T(8,128)S(1)}, f32[192,128]{1,0:T(8,128)S(1)}, u32[]{:S(2)}, u32[]{:S(2)}) collective-permute-start(f32[192,128]{1,0:T(8,128)S(1)} %get-tuple-element.78.rest_7_), channel_id=1, source_target_pairs={{0,128},{16,144},{32,160},{48,176},{64,192},{80,208},{96,224},{112... | collective-permute-start | bytes 294920 | tf_op jit(solution)/shard_map/ppermute | solution.py:313
  25.8 2.4 %collective-permute-start.6 = (f32[192,128]{1,0:T(8,128)S(1)}, f32[192,128]{1,0:T(8,128)S(1)}, u32[]{:S(2)}, u32[]{:S(2)}) collective-permute-start(f32[192,128]{1,0:T(8,128)S(1)} %get-tuple-element.78.rest_7_), channel_id=1, source_target_pairs={{0,64},{16,80},{32,96},{48,112},{64,128},{80,144},{96,160},{112,17... | collective-permute-start | bytes 294920 | tf_op jit(solution)/shard_map/ppermute | solution.py:313
  29.5 2.4 %collective-permute-start.9 = (f32[192,128]{1,0:T(8,128)S(1)}, f32[192,128]{1,0:T(8,128)S(1)}, u32[]{:S(2)}, u32[]{:S(2)}) collective-permute-start(f32[192,128]{1,0:T(8,128)S(1)} %get-tuple-element.78.rest_7_), channel_id=1, source_target_pairs={{0,224},{16,240},{32,0},{48,16},{64,32},{80,48},{96,64},{112,80},{... | collective-permute-start | bytes 294920 | tf_op jit(solution)/shard_map/ppermute | solution.py:313
  37.6 4.3 %collective-permute-done.9.rest_6_ = f32[192,128]{1,0:T(8,128)S(1)} collective-permute-done((f32[192,128]{1,0:T(8,128)S(1)}, f32[192,128]{1,0:T(8,128)S(1)}, u32[]{:S(2)}, u32[]{:S(2)}) %collective-permute-start.9) | collective-permute-done | bytes 98336 | tf_op jit(solution)/shard_map/ppermute | solution.py:313
  45.6 3.3 %collective-permute-done.11.rest_1_ = f32[248,128]{1,0:T(8,128)S(1)} collective-permute-done((f32[248,128]{1,0:T(8,128)S(1)}, f32[248,128]{1,0:T(8,128)S(1)}, u32[]{:S(2)}, u32[]{:S(2)}) %collective-permute-start.11) | collective-permute-done | bytes 127008 | tf_op jit(solution)/shard_map/ppermute | solution.py:305
  49.0 2.7 %collective-permute-done.12.rest_2_ = f32[248,128]{1,0:T(8,128)S(1)} collective-permute-done((f32[248,128]{1,0:T(8,128)S(1)}, f32[248,128]{1,0:T(8,128)S(1)}, u32[]{:S(2)}, u32[]{:S(2)}) %collective-permute-start.12) | collective-permute-done | bytes 127008 | tf_op jit(solution)/shard_map/ppermute | solution.py:300
  52.1 5.0 %shard_map.85 = (f32[64,512]{1,0:T(8,128)S(1)}, f32[64,512]{1,0:T(8,128)S(1)}, f32[64,512]{1,0:T(8,128)S(1)}, f32[64,512]{1,0:T(8,128)S(1)}, f32[64,512]{1,0:T(8...) custom-call(s32[4]{0:T(128)S(1)} %pad_add_fusion.place, ...), custom_call_target="tpu_custom_call" | custom-call | flops 2717908992 | bytes 8000000 | tf_op jit(solution)/shard_map/pallas_call | solution.py:288
  57.1 5.2 %collective-permute-start.15 = (f32[64,512]{1,0:T(8,128)S(1)}, f32[64,512]{1,0:T(8,128)S(1)}, u32[]{:S(2)}, u32[]{:S(2)}) collective-permute-start(f32[64,512]{1,0:T(8,128)S(1)} %get-tuple-element.109), channel_id=1, source_target_pairs={{0,10},{1,11},{2,8},{3,9},{4,14},{5,15},{6,12},{7,13},{8,2},{9,3},... | collective-permute-start | bytes 393224 | tf_op jit(solution)/shard_map/ppermute | solution.py:333
  62.9 4.5 %collective-permute-start.17 = (f32[64,512]{1,0:T(8,128)S(1)}, f32[64,512]{1,0:T(8,128)S(1)}, u32[]{:S(2)}, u32[]{:S(2)}) collective-permute-start(f32[64,512]{1,0:T(8,128)S(1)} %get-tuple-element.111), channel_id=1, source_target_pairs={{0,14},{1,15},{2,12},{3,13},{4,2},{5,3},{6,0},{7,1},{8,6},{9,7},{1... | collective-permute-start | bytes 393224 | tf_op jit(solution)/shard_map/ppermute | solution.py:333
  68.2 2.3 %collective-permute-done.16.rest_2_ = f32[64,512]{1,0:T(8,128)S(1)} collective-permute-done((f32[64,512]{1,0:T(8,128)S(1)}, f32[64,512]{1,0:T(8,128)S(1)}, u32[]{:S(2)}, u32[]{:S(2)}) %collective-permute-start.16) | collective-permute-done | bytes 131104 | tf_op jit(solution)/shard_map/ppermute | solution.py:333
  74.6 2.8 %collective-permute-done.20.rest_6_ = f32[64,512]{1,0:T(8,128)S(1)} collective-permute-done((f32[64,512]{1,0:T(8,128)S(1)}, f32[64,512]{1,0:T(8,128)S(1)}, u32[]{:S(2)}, u32[]{:S(2)}) %collective-permute-start.20) | collective-permute-done | bytes 131104 | tf_op jit(solution)/shard_map/ppermute | solution.py:333
  83.3 4.7 %collective-permute-start.24 = (f32[192,128]{1,0:T(8,128)S(1)}, f32[192,128]{1,0:T(8,128)S(1)}, u32[]{:S(2)}, u32[]{:S(2)}) collective-permute-start(f32[192,128]{1,0:T(8,128)S(1)} %get-tuple-element.117.rest_7_), channel_id=1, source_target_pairs={{0,160},{16,176},{32,192},{48,208},{64,224},{80,240},{96,0},{112,1... | collective-permute-start | bytes 294920 | tf_op jit(solution)/shard_map/ppermute | solution.py:313
  90.9 3.6 %collective-permute-done.24.rest_2_ = f32[192,128]{1,0:T(8,128)S(1)} collective-permute-done((f32[192,128]{1,0:T(8,128)S(1)}, f32[192,128]{1,0:T(8,128)S(1)}, u32[]{:S(2)}, u32[]{:S(2)}) %collective-permute-start.24) | collective-permute-done | bytes 98336 | tf_op jit(solution)/shard_map/ppermute | solution.py:313
  94.5 3.5 %collective-permute-done.23.rest_1_ = f32[192,128]{1,0:T(8,128)S(1)} collective-permute-done((f32[192,128]{1,0:T(8,128)S(1)}, f32[192,128]{1,0:T(8,128)S(1)}, u32[]{:S(2)}, u32[]{:S(2)}) %collective-permute-start.23) | collective-permute-done | bytes 98336 | tf_op jit(solution)/shard_map/ppermute | solution.py:313
  100.6 2.8 %collective-permute-start.29 = (f32[248,128]{1,0:T(8,128)S(1)}, f32[248,128]{1,0:T(8,128)S(1)}, u32[]{:S(2)}, u32[]{:S(2)}) collective-permute-start(f32[248,128]{1,0:T(8,128)S(1)} %get-tuple-element.119), channel_id=1, source_target_pairs={{0,17},{1,16},{2,19},{3,18},{4,21},{5,20},{6,23},{7,22},{8,25},{9,... | collective-permute-start | bytes 380936 | tf_op jit(solution)/shard_map/ppermute | solution.py:305
  106.4 3.8 %collective-permute-done.30.rest_2_ = f32[248,128]{1,0:T(8,128)S(1)} collective-permute-done((f32[248,128]{1,0:T(8,128)S(1)}, f32[248,128]{1,0:T(8,128)S(1)}, u32[]{:S(2)}, u32[]{:S(2)}) %collective-permute-start.30) | collective-permute-done | bytes 127008 | tf_op jit(solution)/shard_map/ppermute | solution.py:300
  110.2 5.0 %shard_map.89 = (f32[64,512]{1,0:T(8,128)S(1)}, f32[64,512]{1,0:T(8,128)S(1)}, f32[64,512]{1,0:T(8,128)S(1)}, f32[64,512]{1,0:T(8,128)S(1)}, f32[64,512]{1,0:T(8...) custom-call(s32[4]{0:T(128)S(1)} %pad_add_fusion.place, ...), custom_call_target="tpu_custom_call" | custom-call | flops 2717908992 | bytes 8000000 | tf_op jit(solution)/shard_map/pallas_call | solution.py:288
  115.1 3.4 %collective-permute-start.32 = (f32[64,512]{1,0:T(8,128)S(1)}, f32[64,512]{1,0:T(8,128)S(1)}, u32[]{:S(2)}, u32[]{:S(2)}) collective-permute-start(f32[64,512]{1,0:T(8,128)S(1)} %get-tuple-element.126), channel_id=1, source_target_pairs={{0,10},{1,11},{2,8},{3,9},{4,14},{5,15},{6,12},{7,13},{8,2},{9,3},... | collective-permute-start | bytes 393224 | tf_op jit(solution)/shard_map/ppermute | solution.py:333
  120.2 3.4 %collective-permute-start.34 = (f32[64,512]{1,0:T(8,128)S(1)}, f32[64,512]{1,0:T(8,128)S(1)}, u32[]{:S(2)}, u32[]{:S(2)}) collective-permute-start(f32[64,512]{1,0:T(8,128)S(1)} %get-tuple-element.128), channel_id=1, source_target_pairs={{0,14},{1,15},{2,12},{3,13},{4,2},{5,3},{6,0},{7,1},{8,6},{9,7},{1... | collective-permute-start | bytes 393224 | tf_op jit(solution)/shard_map/ppermute | solution.py:333
  131.3 2.4 %collective-permute-done.37.rest_6_ = f32[64,512]{1,0:T(8,128)S(1)} collective-permute-done((f32[64,512]{1,0:T(8,128)S(1)}, f32[64,512]{1,0:T(8,128)S(1)}, u32[]{:S(2)}, u32[]{:S(2)}) %collective-permute-start.37) | collective-permute-done | bytes 131104 | tf_op jit(solution)/shard_map/ppermute | solution.py:333
  (80 shorter events, 50.1 us)
Async XLA Ops:
  6.8 7.8 %collective-permute-start.4 = (f32[192,128]{1,0:T(8,128)S(1)}, f32[192,128]{1,0:T(8,128)S(1)}, u32[]{:S(2)}, u32[]{:S(2)}) collective-permute-start(f32[192,128]{1,0:T(8,128)S(1)} %get-tuple-element.78.rest_7_), channel_id=1, source_target_pairs={{0,96},{16,112},{32,128},{48,144},{64,160},{80,176},{96,192},{112,... | collective-permute-start | bytes 294920 | tf_op jit(solution)/shard_map/ppermute | solution.py:313
  14.6 17.3 %collective-permute-start.10 = (f32[27,32,512]{2,1,0:T(8,128)}, f32[27,32,512]{2,1,0:T(8,128)S(1)}, u32[]{:S(2)}, u32[]{:S(2)}) collective-permute-start(f32[27,32,512]{2,1,0:T(8,128)} %own.2), channel_id=1, source_target_pairs={{0,1},{1,0},{2,3},{3,2},{4,5},{5,4},{6,7},{7,6},{8,9},{9,8},{10,11... | collective-permute-start | bytes 5308424 | tf_op jit(solution)/shard_map/ppermute | solution.py:296
  17.8 8.1 %collective-permute-start.1 = (s32[2,26]{1,0:T(2,128)}, s32[2,26]{1,0:T(2,128)S(1)}, u32[]{:S(2)}, u32[]{:S(2)}) collective-permute-start(s32[2,26]{1,0:T(2,128)} %own_table.1), channel_id=1, source_target_pairs={{0,16},{16,0},{32,48},{48,32},{64,80},{80,64},{96,112},{112,96},{1... | collective-permute-start | bytes 632 | tf_op jit(solution)/shard_map/ppermute | solution.py:300
  19.0 10.5 %collective-permute-start.3 = (f32[192,128]{1,0:T(8,128)S(1)}, f32[192,128]{1,0:T(8,128)S(1)}, u32[]{:S(2)}, u32[]{:S(2)}) collective-permute-start(f32[192,128]{1,0:T(8,128)S(1)} %get-tuple-element.78.rest_7_), channel_id=1, source_target_pairs={{0,128},{16,144},{32,160},{48,176},{64,192},{80,208},{96,224},{112... | collective-permute-start | bytes 294920 | tf_op jit(solution)/shard_map/ppermute | solution.py:313
  25.6 12.0 %collective-permute-start.7 = (f32[192,128]{1,0:T(8,128)S(1)}, f32[192,128]{1,0:T(8,128)S(1)}, u32[]{:S(2)}, u32[]{:S(2)}) collective-permute-start(f32[192,128]{1,0:T(8,128)S(1)} %get-tuple-element.78.rest_7_), channel_id=1, source_target_pairs={{0,192},{16,208},{32,224},{48,240},{64,0},{80,16},{96,32},{112,48}... | collective-permute-start | bytes 294920 | tf_op jit(solution)/shard_map/ppermute | solution.py:313
  25.8 11.7 %collective-permute-start.6 = (f32[192,128]{1,0:T(8,128)S(1)}, f32[192,128]{1,0:T(8,128)S(1)}, u32[]{:S(2)}, u32[]{:S(2)}) collective-permute-start(f32[192,128]{1,0:T(8,128)S(1)} %get-tuple-element.78.rest_7_), channel_id=1, source_target_pairs={{0,64},{16,80},{32,96},{48,112},{64,128},{80,144},{96,160},{112,17... | collective-permute-start | bytes 294920 | tf_op jit(solution)/shard_map/ppermute | solution.py:313
  28.2 9.4 %collective-permute-start.5 = (f32[192,128]{1,0:T(8,128)S(1)}, f32[192,128]{1,0:T(8,128)S(1)}, u32[]{:S(2)}, u32[]{:S(2)}) collective-permute-start(f32[192,128]{1,0:T(8,128)S(1)} %get-tuple-element.78.rest_7_), channel_id=1, source_target_pairs={{0,160},{16,176},{32,192},{48,208},{64,224},{80,240},{96,0},{112,1... | collective-permute-start | bytes 294920 | tf_op jit(solution)/shard_map/ppermute | solution.py:313
  29.5 12.5 %collective-permute-start.9 = (f32[192,128]{1,0:T(8,128)S(1)}, f32[192,128]{1,0:T(8,128)S(1)}, u32[]{:S(2)}, u32[]{:S(2)}) collective-permute-start(f32[192,128]{1,0:T(8,128)S(1)} %get-tuple-element.78.rest_7_), channel_id=1, source_target_pairs={{0,224},{16,240},{32,0},{48,16},{64,32},{80,48},{96,64},{112,80},{... | collective-permute-start | bytes 294920 | tf_op jit(solution)/shard_map/ppermute | solution.py:313
  31.9 10.0 %collective-permute-start.8 = (f32[192,128]{1,0:T(8,128)S(1)}, f32[192,128]{1,0:T(8,128)S(1)}, u32[]{:S(2)}, u32[]{:S(2)}) collective-permute-start(f32[192,128]{1,0:T(8,128)S(1)} %get-tuple-element.78.rest_7_), channel_id=1, source_target_pairs={{0,32},{16,48},{32,64},{48,80},{64,96},{80,112},{96,128},{112,144}... | collective-permute-start | bytes 294920 | tf_op jit(solution)/shard_map/ppermute | solution.py:313
  57.1 10.8 %collective-permute-start.15 = (f32[64,512]{1,0:T(8,128)S(1)}, f32[64,512]{1,0:T(8,128)S(1)}, u32[]{:S(2)}, u32[]{:S(2)}) collective-permute-start(f32[64,512]{1,0:T(8,128)S(1)} %get-tuple-element.109), channel_id=1, source_target_pairs={{0,10},{1,11},{2,8},{3,9},{4,14},{5,15},{6,12},{7,13},{8,2},{9,3},... | collective-permute-start | bytes 393224 | tf_op jit(solution)/shard_map/ppermute | solution.py:333
  62.3 8.3 %collective-permute-start.16 = (f32[64,512]{1,0:T(8,128)S(1)}, f32[64,512]{1,0:T(8,128)S(1)}, u32[]{:S(2)}, u32[]{:S(2)}) collective-permute-start(f32[64,512]{1,0:T(8,128)S(1)} %get-tuple-element.110), channel_id=1, source_target_pairs={{0,6},{1,7},{2,4},{3,5},{4,10},{5,11},{6,8},{7,9},{8,14},{9,15},{1... | collective-permute-start | bytes 393224 | tf_op jit(solution)/shard_map/ppermute | solution.py:333
  62.9 9.1 %collective-permute-start.17 = (f32[64,512]{1,0:T(8,128)S(1)}, f32[64,512]{1,0:T(8,128)S(1)}, u32[]{:S(2)}, u32[]{:S(2)}) collective-permute-start(f32[64,512]{1,0:T(8,128)S(1)} %get-tuple-element.111), channel_id=1, source_target_pairs={{0,14},{1,15},{2,12},{3,13},{4,2},{5,3},{6,0},{7,1},{8,6},{9,7},{1... | collective-permute-start | bytes 393224 | tf_op jit(solution)/shard_map/ppermute | solution.py:333
  67.9 9.6 %collective-permute-start.20 = (f32[64,512]{1,0:T(8,128)S(1)}, f32[64,512]{1,0:T(8,128)S(1)}, u32[]{:S(2)}, u32[]{:S(2)}) collective-permute-start(f32[64,512]{1,0:T(8,128)S(1)} %get-tuple-element.114), channel_id=1, source_target_pairs={{0,4},{1,5},{2,6},{3,7},{4,8},{5,9},{6,10},{7,11},{8,12},{9,13},{1... | collective-permute-start | bytes 393224 | tf_op jit(solution)/shard_map/ppermute | solution.py:333
  78.5 9.4 %collective-permute-start.28 = (f32[192,128]{1,0:T(8,128)S(1)}, f32[192,128]{1,0:T(8,128)S(1)}, u32[]{:S(2)}, u32[]{:S(2)}) collective-permute-start(f32[192,128]{1,0:T(8,128)S(1)} %get-tuple-element.117.rest_7_), channel_id=1, source_target_pairs={{0,224},{16,240},{32,0},{48,16},{64,32},{80,48},{96,64},{112,80},{... | collective-permute-start | bytes 294920 | tf_op jit(solution)/shard_map/ppermute | solution.py:313
  80.4 8.8 %collective-permute-start.27 = (f32[192,128]{1,0:T(8,128)S(1)}, f32[192,128]{1,0:T(8,128)S(1)}, u32[]{:S(2)}, u32[]{:S(2)}) collective-permute-start(f32[192,128]{1,0:T(8,128)S(1)} %get-tuple-element.117.rest_7_), channel_id=1, source_target_pairs={{0,32},{16,48},{32,64},{48,80},{64,96},{80,112},{96,128},{112,144}... | collective-permute-start | bytes 294920 | tf_op jit(solution)/shard_map/ppermute | solution.py:313
  80.9 10.0 %collective-permute-start.26 = (f32[192,128]{1,0:T(8,128)S(1)}, f32[192,128]{1,0:T(8,128)S(1)}, u32[]{:S(2)}, u32[]{:S(2)}) collective-permute-start(f32[192,128]{1,0:T(8,128)S(1)} %get-tuple-element.117.rest_7_), channel_id=1, source_target_pairs={{0,192},{16,208},{32,224},{48,240},{64,0},{80,16},{96,32},{112,48}... | collective-permute-start | bytes 294920 | tf_op jit(solution)/shard_map/ppermute | solution.py:313
  82.8 8.1 %collective-permute-start.25 = (f32[192,128]{1,0:T(8,128)S(1)}, f32[192,128]{1,0:T(8,128)S(1)}, u32[]{:S(2)}, u32[]{:S(2)}) collective-permute-start(f32[192,128]{1,0:T(8,128)S(1)} %get-tuple-element.117.rest_7_), channel_id=1, source_target_pairs={{0,64},{16,80},{32,96},{48,112},{64,128},{80,144},{96,160},{112,17... | collective-permute-start | bytes 294920 | tf_op jit(solution)/shard_map/ppermute | solution.py:313
  83.3 11.2 %collective-permute-start.24 = (f32[192,128]{1,0:T(8,128)S(1)}, f32[192,128]{1,0:T(8,128)S(1)}, u32[]{:S(2)}, u32[]{:S(2)}) collective-permute-start(f32[192,128]{1,0:T(8,128)S(1)} %get-tuple-element.117.rest_7_), channel_id=1, source_target_pairs={{0,160},{16,176},{32,192},{48,208},{64,224},{80,240},{96,0},{112,1... | collective-permute-start | bytes 294920 | tf_op jit(solution)/shard_map/ppermute | solution.py:313
  88.0 10.0 %collective-permute-start.23 = (f32[192,128]{1,0:T(8,128)S(1)}, f32[192,128]{1,0:T(8,128)S(1)}, u32[]{:S(2)}, u32[]{:S(2)}) collective-permute-start(f32[192,128]{1,0:T(8,128)S(1)} %get-tuple-element.117.rest_7_), channel_id=1, source_target_pairs={{0,96},{16,112},{32,128},{48,144},{64,160},{80,176},{96,192},{112,... | collective-permute-start | bytes 294920 | tf_op jit(solution)/shard_map/ppermute | solution.py:313
  89.1 10.2 %collective-permute-start.22 = (f32[192,128]{1,0:T(8,128)S(1)}, f32[192,128]{1,0:T(8,128)S(1)}, u32[]{:S(2)}, u32[]{:S(2)}) collective-permute-start(f32[192,128]{1,0:T(8,128)S(1)} %get-tuple-element.117.rest_7_), channel_id=1, source_target_pairs={{0,128},{16,144},{32,160},{48,176},{64,192},{80,208},{96,224},{112... | collective-permute-start | bytes 294920 | tf_op jit(solution)/shard_map/ppermute | solution.py:313
  115.1 9.6 %collective-permute-start.32 = (f32[64,512]{1,0:T(8,128)S(1)}, f32[64,512]{1,0:T(8,128)S(1)}, u32[]{:S(2)}, u32[]{:S(2)}) collective-permute-start(f32[64,512]{1,0:T(8,128)S(1)} %get-tuple-element.126), channel_id=1, source_target_pairs={{0,10},{1,11},{2,8},{3,9},{4,14},{5,15},{6,12},{7,13},{8,2},{9,3},... | collective-permute-start | bytes 393224 | tf_op jit(solution)/shard_map/ppermute | solution.py:333
  118.5 9.2 %collective-permute-start.33 = (f32[64,512]{1,0:T(8,128)S(1)}, f32[64,512]{1,0:T(8,128)S(1)}, u32[]{:S(2)}, u32[]{:S(2)}) collective-permute-start(f32[64,512]{1,0:T(8,128)S(1)} %get-tuple-element.127), channel_id=1, source_target_pairs={{0,6},{1,7},{2,4},{3,5},{4,10},{5,11},{6,8},{7,9},{8,14},{9,15},{1... | collective-permute-start | bytes 393224 | tf_op jit(solution)/shard_map/ppermute | solution.py:333
  120.2 9.4 %collective-permute-start.34 = (f32[64,512]{1,0:T(8,128)S(1)}, f32[64,512]{1,0:T(8,128)S(1)}, u32[]{:S(2)}, u32[]{:S(2)}) collective-permute-start(f32[64,512]{1,0:T(8,128)S(1)} %get-tuple-element.128), channel_id=1, source_target_pairs={{0,14},{1,15},{2,12},{3,13},{4,2},{5,3},{6,0},{7,1},{8,6},{9,7},{1... | collective-permute-start | bytes 393224 | tf_op jit(solution)/shard_map/ppermute | solution.py:333
  124.8 9.0 %collective-permute-start.37 = (f32[64,512]{1,0:T(8,128)S(1)}, f32[64,512]{1,0:T(8,128)S(1)}, u32[]{:S(2)}, u32[]{:S(2)}) collective-permute-start(f32[64,512]{1,0:T(8,128)S(1)} %get-tuple-element.131), channel_id=1, source_target_pairs={{0,4},{1,5},{2,6},{3,7},{4,8},{5,9},{6,10},{7,11},{8,12},{9,13},{1... | collective-permute-start | bytes 393224 | tf_op jit(solution)/shard_map/ppermute | solution.py:333
  (22 other events, 154.6 us)

commit v2 on v1

--- a/solution.py
+++ b/solution.py
@@ -105,8 +105,8 @@
     return value
 
 
-def bias_row(core, number, own_bias, other_bias):
-    own, other = own_bias[number : number + 1, :], other_bias[number : number + 1, :]
+def bias_row(core, own_bias, other_bias):
+    own, other = own_bias[...], other_bias[...]
     first = jnp.where(core == 0, own, other)
     second = jnp.where(core == 0, other, own)
     return jnp.concatenate([first, second], axis=1)
@@ -120,7 +120,7 @@
 def hidden_kernel(place, counts, occupancy, own_bias, other_bias, *rest):
     core = place[0]
     rows, faces = rest[8:]
-    bias = bias_column(bias_row(core, 0, own_bias, other_bias))
+    bias = bias_column(bias_row(core, own_bias, other_bias))
     value = jnp.maximum(added(rest[:8]) + bias, 0.0)
     rows[...] = (value * active_voxels(core, counts, occupancy)).T
     cut_faces(rows, faces)
@@ -129,7 +129,7 @@
 def result_kernel(place, counts, occupancy, own_bias, other_bias, *rest):
     core = place[0]
     keep, give = rest[8:]
-    bias = bias_column(bias_row(core, 1, own_bias, other_bias))
+    bias = bias_column(bias_row(core, own_bias, other_bias))
     value = (added(rest[:8]) + bias) * active_voxels(core, counts, occupancy)
     keep[...] = jnp.where(core == 0, value[0:32], value[32:64])
     give[...] = jnp.where(core == 0, value[32:64], value[0:32])
@@ -160,7 +160,7 @@
 
 
 RIM_ROWS = 248
-SENT = (4, 3, -3, 2, -2, 1, -1)
+SENT = (-1, 1, -2, 2, -3, 3, 4)
 
 
 def face_rows(offsets):
@@ -305,19 +305,20 @@
     return lax.ppermute(value, ("leaf", "chan"), pairs)
 
 
-def gather_rims(place, tables, faces, early=(), weight=None):
+def gather_rims(place, tables, faces, weights=()):
     found = []
     for step in SENT:
-        if step == 1 and early:
-            faces, early, found[0] = lax.optimization_barrier((faces, early, found[0]))
         found.append(lax.ppermute(faces, "leaf", [(i, (i + 2 * step) % 16) for i in range(16)]))
-    if weight is not None:
-        found[1], weight = lax.optimization_barrier((found[1], weight))
-        weight = split_weights(place, weight, to_other_core(weight))
-        found, weight = lax.optimization_barrier((found, weight))
-    tables = early[0] if early else tables
+    if weights:
+        found, weights = lax.optimization_barrier((found, weights))
     own, beside, across, both = cut_rims(place, *tables, found + [faces])
-    return [own, to_other_both(both), to_other_x(beside), to_other_core(across)], early, weight
+    return [own, to_other_both(both), to_other_x(beside), to_other_core(across)], weights
+
+
+def conv_beside(place, rows, rims, weights, moved):
+    rims, moved = lax.optimization_barrier((rims, moved))
+    parts = conv(place, rows, rims, *weights)
+    return lax.optimization_barrier((parts, [to_other_core(value) for value in moved]))
 
 
 ROUTES = ((2, 1), (1, 1), (3, 1), (2, 0), (0, 1), (1, 0), (3, 0))
@@ -343,23 +344,23 @@
         in_specs=[SMEM, SMEM, VMEM, VMEM, VMEM], out_specs=(VMEM, VMEM)
     )(place, leaf_counts, occupancy, features, *near([others]))
     tables = neighbours, to_other_x(neighbours)
-    biases = jnp.stack([bias_in, bias_out])
-    biases = biases, to_other_core(biases)
-    rims, (tables, biases), weights = gather_rims(place, tables, faces, (tables, biases), weight_in)
-    rims, weight_out = lax.optimization_barrier((rims, weight_out))
-    swapped = to_other_core(weight_out)
-    parts, swapped = lax.optimization_barrier((conv(place, rows, rims, *weights), swapped))
-    weights_out = split_weights(place, weight_out, swapped)
+    bias_in, bias_out = bias_in.reshape(1, 32), bias_out.reshape(1, 32)
+    weights = split_weights(place, weight_in, to_other_core(weight_in))
+
+    rims, weights = gather_rims(place, tables, faces, weights)
+    parts, (swapped, other_bias) = conv_beside(place, rows, rims, weights, [weight_out, bias_in])
+    weights = split_weights(place, weight_out, swapped)
     parts = add_over_chips(parts)
     rows, faces = call(hidden_kernel, (close((512, 64)), close((192, 128))))(
         in_specs=[SMEM, SMEM] + [VMEM] * 11, out_specs=(VMEM, VMEM)
-    )(place, leaf_counts, occupancy, *biases, *near(parts))
-
-    rims, _, _ = gather_rims(place, tables, faces)
-    parts = add_over_chips(conv(place, rows, rims, *weights_out))
+    )(place, leaf_counts, occupancy, bias_in, other_bias, *near(parts))
+
+    rims, _ = gather_rims(place, tables, faces)
+    parts, (other_bias,) = conv_beside(place, rows, rims, weights, [bias_out])
+    parts = add_over_chips(parts)
     keep, give = call(result_kernel, (close((32, 512)), close((32, 512))))(
         in_specs=[SMEM, SMEM] + [VMEM] * 11, out_specs=(VMEM, VMEM)
-    )(place, leaf_counts, occupancy, *biases, *near(parts))
+    )(place, leaf_counts, occupancy, bias_out, other_bias, *near(parts))
     return call(merge_kernel, arr((32, 2, 512)))(in_specs=[SMEM, VMEM, VMEM], out_specs=VMEM)(
         place, *near([keep, to_other_core(give)])
     )

time: 139 us -> 135 us (0.971)
  starting transfers between devices: 67 us -> 63.4 us
    ppermute x14, waiting for transfers between devices: 19.3 us -> 15.5 us  [gather_rims(): lax.ppermute(faces, 'leaf', [(i, (i + 2 * step) % 16) for i in range(16)])]
    ppermute x7 -> x8, starting transfers between devices: 8.59 us -> 5.61 us  [to_other_core(): return lax.ppermute(value, 'chan', [(i, i ^ 1) for i in range(16)])]
    ppermute x2, waiting for transfers between devices: 3.35 us -> 6.14 us  [to_other_both(): return lax.ppermute(value, ('leaf', 'chan'), pairs)]
    ppermute x7 -> x8, waiting for transfers between devices: 1.37 us -> 3.89 us  [to_other_core(): return lax.ppermute(value, 'chan', [(i, i ^ 1) for i in range(16)])]
    unnamed x12 -> x16, local copies, waits for them, and re-layouts: 3.08 us -> 3.09 us
  transfers between devices with their start and end apart: 40 -> 41, of which waited for: 20 -> 22; matrix products, arithmetic and copies ran while one was open for 1% -> 0% of each run, Pallas kernels for 5% -> 10%
where the time goes in v2:
time: 135 us; the launch traced here: 134 us
  starting transfers between devices  63.4 us (47%)
  waiting for transfers between devices  48 us (36%)
  Pallas kernels  19 us (14%)
  local copies, waits for them, and re-layouts  3.09 us (2%)
    ppermute x14, starting transfers between devices, gather_rims(): lax.ppermute(faces, 'leaf', [(i, (i + 2 * step) % 16) for i in range(16)])  28.9 us
    ppermute x14, starting transfers between devices, add_over_chips(): lax.ppermute(part, 'chan', [(i, route_target(i, route)) for i in range(16)])  21.8 us
    ppermute x14, waiting for transfers between devices, add_over_chips(): lax.ppermute(part, 'chan', [(i, route_target(i, route)) for i in range(16)])  15.7 us
    ppermute x14, waiting for transfers between devices, gather_rims(): lax.ppermute(faces, 'leaf', [(i, (i + 2 * step) % 16) for i in range(16)])  15.5 us
    pallas_call x2, Pallas kernels, conv(): call(conv_kernel, outs, scratch, flops=2 * 3 * 1024 * 1728 * 256, touched...  9.96 us
    ppermute x3, waiting for transfers between devices, to_other_x(): return lax.ppermute(value, 'leaf', [(i, i ^ 1) for i in range(16)])  6.77 us
    ppermute x2, waiting for transfers between devices, to_other_both(): return lax.ppermute(value, ('leaf', 'chan'), pairs)  6.14 us
    ppermute x8, starting transfers between devices, to_other_core(): return lax.ppermute(value, 'chan', [(i, i ^ 1) for i in range(16)])  5.61 us
  transfers between devices with their start and end apart: 41, of which 22 were waited for; matrix products, arithmetic and copies ran while one was open for 0% of the time, Pallas kernels for 10%

profile of v2, /device:TPU:1, one launch (start us, length us, event | category | flops | bytes accessed | tf_op | source)
XLA Modules:
  0.0 134.4 jit_solution(2347144457441500806)
XLA Ops:
  0.0 3.2 %collective-permute-start.9 = (f32[27,32,512]{2,1,0:T(8,128)}, f32[27,32,512]{2,1,0:T(8,128)S(1)}, u32[]{:S(2)}, u32[]{:S(2)}) collective-permute-start(f32[27,32,512]{2,1,0:T(8,128)} %own.4), channel_id=1, source_target_pairs={{0,1},{1,0},{2,3},{3,2},{4,5},{5,4},{6,7},{7,6},{8,9},{9,8},{10,11... | collective-permute-start | bytes 5308424 | tf_op jit(solution)/shard_map/ppermute | solution.py:296
  4.0 3.0 %collective-permute-done.other = f32[32,2,512]{2,1,0:T(2,128)S(1)} collective-permute-done((f32[32,2,512]{2,1,0:T(2,128)}, f32[32,2,512]{2,1,0:T(2,128)S(1)}, u32[]{:S(2)}, u32[]{:S(2)}) %collective-permute-start) | collective-permute-done | bytes 131104 | tf_op jit(solution)/shard_map/ppermute | solution.py:296
  9.4 5.3 %collective-permute-start.8 = (f32[192,128]{1,0:T(8,128)S(1)}, f32[192,128]{1,0:T(8,128)S(1)}, u32[]{:S(2)}, u32[]{:S(2)}) collective-permute-start(f32[192,128]{1,0:T(8,128)S(1)} %get-tuple-element.79.rest_7_), channel_id=1, source_target_pairs={{0,128},{16,144},{32,160},{48,176},{64,192},{80,208},{96,224},{112... | collective-permute-start | bytes 294920 | tf_op jit(solution)/shard_map/ppermute | solution.py:311
  16.3 2.8 %collective-permute-start.6 = (f32[192,128]{1,0:T(8,128)S(1)}, f32[192,128]{1,0:T(8,128)S(1)}, u32[]{:S(2)}, u32[]{:S(2)}) collective-permute-start(f32[192,128]{1,0:T(8,128)S(1)} %get-tuple-element.79.rest_7_), channel_id=1, source_target_pairs={{0,160},{16,176},{32,192},{48,208},{64,224},{80,240},{96,0},{112,1... | collective-permute-start | bytes 294920 | tf_op jit(solution)/shard_map/ppermute | solution.py:311
  20.3 3.6 %collective-permute-start.4 = (f32[192,128]{1,0:T(8,128)S(1)}, f32[192,128]{1,0:T(8,128)S(1)}, u32[]{:S(2)}, u32[]{:S(2)}) collective-permute-start(f32[192,128]{1,0:T(8,128)S(1)} %get-tuple-element.79.rest_7_), channel_id=1, source_target_pairs={{0,192},{16,208},{32,224},{48,240},{64,0},{80,16},{96,32},{112,48}... | collective-permute-start | bytes 294920 | tf_op jit(solution)/shard_map/ppermute | solution.py:311
  23.9 4.3 %collective-permute-done.7.rest_5_ = f32[192,128]{1,0:T(8,128)S(1)} collective-permute-done((f32[192,128]{1,0:T(8,128)S(1)}, f32[192,128]{1,0:T(8,128)S(1)}, u32[]{:S(2)}, u32[]{:S(2)}) %collective-permute-start.7) | collective-permute-done | bytes 98336 | tf_op jit(solution)/shard_map/ppermute | solution.py:311
  28.3 2.7 %collective-permute-start.2 = (f32[192,128]{1,0:T(8,128)S(1)}, f32[192,128]{1,0:T(8,128)S(1)}, u32[]{:S(2)}, u32[]{:S(2)}) collective-permute-start(f32[192,128]{1,0:T(8,128)S(1)} %get-tuple-element.79.rest_7_), channel_id=1, source_target_pairs={{0,224},{16,240},{32,0},{48,16},{64,32},{80,48},{96,64},{112,80},{... | collective-permute-start | bytes 294920 | tf_op jit(solution)/shard_map/ppermute | solution.py:311
  37.5 3.3 %collective-permute-start.10 = (f32[248,128]{1,0:T(8,128)S(1)}, f32[248,128]{1,0:T(8,128)S(1)}, u32[]{:S(2)}, u32[]{:S(2)}) collective-permute-start(f32[248,128]{1,0:T(8,128)S(1)} %get-tuple-element.90), channel_id=1, source_target_pairs={{0,17},{1,16},{2,19},{3,18},{4,21},{5,20},{6,23},{7,22},{8,25},{9,... | collective-permute-start | bytes 380936 | tf_op jit(solution)/shard_map/ppermute | solution.py:305
  41.3 3.7 %collective-permute-done.10.rest_1_ = f32[248,128]{1,0:T(8,128)S(1)} collective-permute-done((f32[248,128]{1,0:T(8,128)S(1)}, f32[248,128]{1,0:T(8,128)S(1)}, u32[]{:S(2)}, u32[]{:S(2)}) %collective-permute-start.10) | collective-permute-done | bytes 127008 | tf_op jit(solution)/shard_map/ppermute | solution.py:305
  45.0 2.7 %collective-permute-done.11.rest_2_ = f32[248,128]{1,0:T(8,128)S(1)} collective-permute-done((f32[248,128]{1,0:T(8,128)S(1)}, f32[248,128]{1,0:T(8,128)S(1)}, u32[]{:S(2)}, u32[]{:S(2)}) %collective-permute-start.11) | collective-permute-done | bytes 127008 | tf_op jit(solution)/shard_map/ppermute | solution.py:300
  48.4 5.0 %shard_map.85 = (f32[64,512]{1,0:T(8,128)S(1)}, f32[64,512]{1,0:T(8,128)S(1)}, f32[64,512]{1,0:T(8,128)S(1)}, f32[64,512]{1,0:T(8,128)S(1)}, f32[64,512]{1,0:T(8...) custom-call(s32[4]{0:T(128)S(1)} %pad_add_fusion.place, ...), custom_call_target="tpu_custom_call" | custom-call | flops 2717908992 | bytes 8000000 | tf_op jit(solution)/shard_map/pallas_call | solution.py:288
  53.4 5.0 %collective-permute-start.15 = (f32[64,512]{1,0:T(8,128)S(1)}, f32[64,512]{1,0:T(8,128)S(1)}, u32[]{:S(2)}, u32[]{:S(2)}) collective-permute-start(f32[64,512]{1,0:T(8,128)S(1)} %get-tuple-element.111), channel_id=1, source_target_pairs={{0,10},{1,11},{2,8},{3,9},{4,14},{5,15},{6,12},{7,13},{8,2},{9,3},... | collective-permute-start | bytes 393224 | tf_op jit(solution)/shard_map/ppermute | solution.py:334
  59.3 4.3 %collective-permute-start.17 = (f32[64,512]{1,0:T(8,128)S(1)}, f32[64,512]{1,0:T(8,128)S(1)}, u32[]{:S(2)}, u32[]{:S(2)}) collective-permute-start(f32[64,512]{1,0:T(8,128)S(1)} %get-tuple-element.113), channel_id=1, source_target_pairs={{0,14},{1,15},{2,12},{3,13},{4,2},{5,3},{6,0},{7,1},{8,6},{9,7},{1... | collective-permute-start | bytes 393224 | tf_op jit(solution)/shard_map/ppermute | solution.py:334
  64.4 2.2 %collective-permute-done.16.rest_2_ = f32[64,512]{1,0:T(8,128)S(1)} collective-permute-done((f32[64,512]{1,0:T(8,128)S(1)}, f32[64,512]{1,0:T(8,128)S(1)}, u32[]{:S(2)}, u32[]{:S(2)}) %collective-permute-start.16) | collective-permute-done | bytes 131104 | tf_op jit(solution)/shard_map/ppermute | solution.py:334
  70.9 2.8 %collective-permute-done.20.rest_6_ = f32[64,512]{1,0:T(8,128)S(1)} collective-permute-done((f32[64,512]{1,0:T(8,128)S(1)}, f32[64,512]{1,0:T(8,128)S(1)}, u32[]{:S(2)}, u32[]{:S(2)}) %collective-permute-start.20) | collective-permute-done | bytes 131104 | tf_op jit(solution)/shard_map/ppermute | solution.py:334
  77.8 3.3 %collective-permute-start.26 = (f32[192,128]{1,0:T(8,128)S(1)}, f32[192,128]{1,0:T(8,128)S(1)}, u32[]{:S(2)}, u32[]{:S(2)}) collective-permute-start(f32[192,128]{1,0:T(8,128)S(1)} %get-tuple-element.119.rest_7_), channel_id=1, source_target_pairs={{0,160},{16,176},{32,192},{48,208},{64,224},{80,240},{96,0},{112,1... | collective-permute-start | bytes 294920 | tf_op jit(solution)/shard_map/ppermute | solution.py:311
  86.4 5.3 %collective-permute-done.27.rest_5_ = f32[192,128]{1,0:T(8,128)S(1)} collective-permute-done((f32[192,128]{1,0:T(8,128)S(1)}, f32[192,128]{1,0:T(8,128)S(1)}, u32[]{:S(2)}, u32[]{:S(2)}) %collective-permute-start.27) | collective-permute-done | bytes 98336 | tf_op jit(solution)/shard_map/ppermute | solution.py:311
  94.4 3.2 %collective-permute-done.23.rest_1_ = f32[192,128]{1,0:T(8,128)S(1)} collective-permute-done((f32[192,128]{1,0:T(8,128)S(1)}, f32[192,128]{1,0:T(8,128)S(1)}, u32[]{:S(2)}, u32[]{:S(2)}) %collective-permute-start.23) | collective-permute-done | bytes 98336 | tf_op jit(solution)/shard_map/ppermute | solution.py:311
  102.4 2.5 %collective-permute-done.29.rest_1_ = f32[248,128]{1,0:T(8,128)S(1)} collective-permute-done((f32[248,128]{1,0:T(8,128)S(1)}, f32[248,128]{1,0:T(8,128)S(1)}, u32[]{:S(2)}, u32[]{:S(2)}) %collective-permute-start.29) | collective-permute-done | bytes 127008 | tf_op jit(solution)/shard_map/ppermute | solution.py:305
  104.9 2.7 %collective-permute-done.30.rest_2_ = f32[248,128]{1,0:T(8,128)S(1)} collective-permute-done((f32[248,128]{1,0:T(8,128)S(1)}, f32[248,128]{1,0:T(8,128)S(1)}, u32[]{:S(2)}, u32[]{:S(2)}) %collective-permute-start.30) | collective-permute-done | bytes 127008 | tf_op jit(solution)/shard_map/ppermute | solution.py:300
  108.0 5.0 %shard_map.89 = (f32[64,512]{1,0:T(8,128)S(1)}, f32[64,512]{1,0:T(8,128)S(1)}, f32[64,512]{1,0:T(8,128)S(1)}, f32[64,512]{1,0:T(8,128)S(1)}, f32[64,512]{1,0:T(8...) custom-call(s32[4]{0:T(128)S(1)} %pad_add_fusion.place, ...), custom_call_target="tpu_custom_call" | custom-call | flops 2717908992 | bytes 8000000 | tf_op jit(solution)/shard_map/pallas_call | solution.py:288
  114.6 2.3 %collective-permute-start.34 = (f32[64,512]{1,0:T(8,128)S(1)}, f32[64,512]{1,0:T(8,128)S(1)}, u32[]{:S(2)}, u32[]{:S(2)}) collective-permute-start(f32[64,512]{1,0:T(8,128)S(1)} %get-tuple-element.143), channel_id=1, source_target_pairs={{0,6},{1,7},{2,4},{3,5},{4,10},{5,11},{6,8},{7,9},{8,14},{9,15},{1... | collective-permute-start | bytes 393224 | tf_op jit(solution)/shard_map/ppermute | solution.py:334
  116.9 2.8 %collective-permute-start.35 = (f32[64,512]{1,0:T(8,128)S(1)}, f32[64,512]{1,0:T(8,128)S(1)}, u32[]{:S(2)}, u32[]{:S(2)}) collective-permute-start(f32[64,512]{1,0:T(8,128)S(1)} %get-tuple-element.144), channel_id=1, source_target_pairs={{0,14},{1,15},{2,12},{3,13},{4,2},{5,3},{6,0},{7,1},{8,6},{9,7},{1... | collective-permute-start | bytes 393224 | tf_op jit(solution)/shard_map/ppermute | solution.py:334
  119.7 2.9 %collective-permute-start.37 = (f32[64,512]{1,0:T(8,128)S(1)}, f32[64,512]{1,0:T(8,128)S(1)}, u32[]{:S(2)}, u32[]{:S(2)}) collective-permute-start(f32[64,512]{1,0:T(8,128)S(1)} %get-tuple-element.146), channel_id=1, source_target_pairs={{0,2},{1,3},{2,0},{3,1},{4,6},{5,7},{6,4},{7,5},{8,10},{9,11},{10,... | collective-permute-start | bytes 393224 | tf_op jit(solution)/shard_map/ppermute | solution.py:334
  (85 shorter events, 49.6 us)
Async XLA Ops:
  0.0 28.3 %collective-permute-start.9 = (f32[27,32,512]{2,1,0:T(8,128)}, f32[27,32,512]{2,1,0:T(8,128)S(1)}, u32[]{:S(2)}, u32[]{:S(2)}) collective-permute-start(f32[27,32,512]{2,1,0:T(8,128)} %own.4), channel_id=1, source_target_pairs={{0,1},{1,0},{2,3},{3,2},{4,5},{5,4},{6,7},{7,6},{8,9},{9,8},{10,11... | collective-permute-start | bytes 5308424 | tf_op jit(solution)/shard_map/ppermute | solution.py:296
  9.4 10.9 %collective-permute-start.8 = (f32[192,128]{1,0:T(8,128)S(1)}, f32[192,128]{1,0:T(8,128)S(1)}, u32[]{:S(2)}, u32[]{:S(2)}) collective-permute-start(f32[192,128]{1,0:T(8,128)S(1)} %get-tuple-element.79.rest_7_), channel_id=1, source_target_pairs={{0,128},{16,144},{32,160},{48,176},{64,192},{80,208},{96,224},{112... | collective-permute-start | bytes 294920 | tf_op jit(solution)/shard_map/ppermute | solution.py:311
  14.7 13.6 %collective-permute-start.7 = (f32[192,128]{1,0:T(8,128)S(1)}, f32[192,128]{1,0:T(8,128)S(1)}, u32[]{:S(2)}, u32[]{:S(2)}) collective-permute-start(f32[192,128]{1,0:T(8,128)S(1)} %get-tuple-element.79.rest_7_), channel_id=1, source_target_pairs={{0,96},{16,112},{32,128},{48,144},{64,160},{80,176},{96,192},{112,... | collective-permute-start | bytes 294920 | tf_op jit(solution)/shard_map/ppermute | solution.py:311
  16.3 17.4 %collective-permute-start.6 = (f32[192,128]{1,0:T(8,128)S(1)}, f32[192,128]{1,0:T(8,128)S(1)}, u32[]{:S(2)}, u32[]{:S(2)}) collective-permute-start(f32[192,128]{1,0:T(8,128)S(1)} %get-tuple-element.79.rest_7_), channel_id=1, source_target_pairs={{0,160},{16,176},{32,192},{48,208},{64,224},{80,240},{96,0},{112,1... | collective-permute-start | bytes 294920 | tf_op jit(solution)/shard_map/ppermute | solution.py:311
  19.1 15.8 %collective-permute-start.5 = (f32[192,128]{1,0:T(8,128)S(1)}, f32[192,128]{1,0:T(8,128)S(1)}, u32[]{:S(2)}, u32[]{:S(2)}) collective-permute-start(f32[192,128]{1,0:T(8,128)S(1)} %get-tuple-element.79.rest_7_), channel_id=1, source_target_pairs={{0,64},{16,80},{32,96},{48,112},{64,128},{80,144},{96,160},{112,17... | collective-permute-start | bytes 294920 | tf_op jit(solution)/shard_map/ppermute | solution.py:311
  20.3 14.6 %collective-permute-start.4 = (f32[192,128]{1,0:T(8,128)S(1)}, f32[192,128]{1,0:T(8,128)S(1)}, u32[]{:S(2)}, u32[]{:S(2)}) collective-permute-start(f32[192,128]{1,0:T(8,128)S(1)} %get-tuple-element.79.rest_7_), channel_id=1, source_target_pairs={{0,192},{16,208},{32,224},{48,240},{64,0},{80,16},{96,32},{112,48}... | collective-permute-start | bytes 294920 | tf_op jit(solution)/shard_map/ppermute | solution.py:311
  37.5 7.5 %collective-permute-start.10 = (f32[248,128]{1,0:T(8,128)S(1)}, f32[248,128]{1,0:T(8,128)S(1)}, u32[]{:S(2)}, u32[]{:S(2)}) collective-permute-start(f32[248,128]{1,0:T(8,128)S(1)} %get-tuple-element.90), channel_id=1, source_target_pairs={{0,17},{1,16},{2,19},{3,18},{4,21},{5,20},{6,23},{7,22},{8,25},{9,... | collective-permute-start | bytes 380936 | tf_op jit(solution)/shard_map/ppermute | solution.py:305
  53.4 10.8 %collective-permute-start.15 = (f32[64,512]{1,0:T(8,128)S(1)}, f32[64,512]{1,0:T(8,128)S(1)}, u32[]{:S(2)}, u32[]{:S(2)}) collective-permute-start(f32[64,512]{1,0:T(8,128)S(1)} %get-tuple-element.111), channel_id=1, source_target_pairs={{0,10},{1,11},{2,8},{3,9},{4,14},{5,15},{6,12},{7,13},{8,2},{9,3},... | collective-permute-start | bytes 393224 | tf_op jit(solution)/shard_map/ppermute | solution.py:334
  58.4 8.2 %collective-permute-start.16 = (f32[64,512]{1,0:T(8,128)S(1)}, f32[64,512]{1,0:T(8,128)S(1)}, u32[]{:S(2)}, u32[]{:S(2)}) collective-permute-start(f32[64,512]{1,0:T(8,128)S(1)} %get-tuple-element.112), channel_id=1, source_target_pairs={{0,6},{1,7},{2,4},{3,5},{4,10},{5,11},{6,8},{7,9},{8,14},{9,15},{1... | collective-permute-start | bytes 393224 | tf_op jit(solution)/shard_map/ppermute | solution.py:334
  59.3 9.0 %collective-permute-start.17 = (f32[64,512]{1,0:T(8,128)S(1)}, f32[64,512]{1,0:T(8,128)S(1)}, u32[]{:S(2)}, u32[]{:S(2)}) collective-permute-start(f32[64,512]{1,0:T(8,128)S(1)} %get-tuple-element.113), channel_id=1, source_target_pairs={{0,14},{1,15},{2,12},{3,13},{4,2},{5,3},{6,0},{7,1},{8,6},{9,7},{1... | collective-permute-start | bytes 393224 | tf_op jit(solution)/shard_map/ppermute | solution.py:334
  64.2 9.4 %collective-permute-start.20 = (f32[64,512]{1,0:T(8,128)S(1)}, f32[64,512]{1,0:T(8,128)S(1)}, u32[]{:S(2)}, u32[]{:S(2)}) collective-permute-start(f32[64,512]{1,0:T(8,128)S(1)} %get-tuple-element.116), channel_id=1, source_target_pairs={{0,4},{1,5},{2,6},{3,7},{4,8},{5,9},{6,10},{7,11},{8,12},{9,13},{1... | collective-permute-start | bytes 393224 | tf_op jit(solution)/shard_map/ppermute | solution.py:334
  74.7 10.0 %collective-permute-start.28 = (f32[192,128]{1,0:T(8,128)S(1)}, f32[192,128]{1,0:T(8,128)S(1)}, u32[]{:S(2)}, u32[]{:S(2)}) collective-permute-start(f32[192,128]{1,0:T(8,128)S(1)} %get-tuple-element.119.rest_7_), channel_id=1, source_target_pairs={{0,128},{16,144},{32,160},{48,176},{64,192},{80,208},{96,224},{112... | collective-permute-start | bytes 294920 | tf_op jit(solution)/shard_map/ppermute | solution.py:311
  76.6 15.1 %collective-permute-start.27 = (f32[192,128]{1,0:T(8,128)S(1)}, f32[192,128]{1,0:T(8,128)S(1)}, u32[]{:S(2)}, u32[]{:S(2)}) collective-permute-start(f32[192,128]{1,0:T(8,128)S(1)} %get-tuple-element.119.rest_7_), channel_id=1, source_target_pairs={{0,96},{16,112},{32,128},{48,144},{64,160},{80,176},{96,192},{112,... | collective-permute-start | bytes 294920 | tf_op jit(solution)/shard_map/ppermute | solution.py:311
  77.8 13.9 %collective-permute-start.26 = (f32[192,128]{1,0:T(8,128)S(1)}, f32[192,128]{1,0:T(8,128)S(1)}, u32[]{:S(2)}, u32[]{:S(2)}) collective-permute-start(f32[192,128]{1,0:T(8,128)S(1)} %get-tuple-element.119.rest_7_), channel_id=1, source_target_pairs={{0,160},{16,176},{32,192},{48,208},{64,224},{80,240},{96,0},{112,1... | collective-permute-start | bytes 294920 | tf_op jit(solution)/shard_map/ppermute | solution.py:311
  81.1 12.0 %collective-permute-start.25 = (f32[192,128]{1,0:T(8,128)S(1)}, f32[192,128]{1,0:T(8,128)S(1)}, u32[]{:S(2)}, u32[]{:S(2)}) collective-permute-start(f32[192,128]{1,0:T(8,128)S(1)} %get-tuple-element.119.rest_7_), channel_id=1, source_target_pairs={{0,64},{16,80},{32,96},{48,112},{64,128},{80,144},{96,160},{112,17... | collective-permute-start | bytes 294920 | tf_op jit(solution)/shard_map/ppermute | solution.py:311
  82.8 11.6 %collective-permute-start.24 = (f32[192,128]{1,0:T(8,128)S(1)}, f32[192,128]{1,0:T(8,128)S(1)}, u32[]{:S(2)}, u32[]{:S(2)}) collective-permute-start(f32[192,128]{1,0:T(8,128)S(1)} %get-tuple-element.119.rest_7_), channel_id=1, source_target_pairs={{0,192},{16,208},{32,224},{48,240},{64,0},{80,16},{96,32},{112,48}... | collective-permute-start | bytes 294920 | tf_op jit(solution)/shard_map/ppermute | solution.py:311
  84.7 12.9 %collective-permute-start.23 = (f32[192,128]{1,0:T(8,128)S(1)}, f32[192,128]{1,0:T(8,128)S(1)}, u32[]{:S(2)}, u32[]{:S(2)}) collective-permute-start(f32[192,128]{1,0:T(8,128)S(1)} %get-tuple-element.119.rest_7_), channel_id=1, source_target_pairs={{0,32},{16,48},{32,64},{48,80},{64,96},{80,112},{96,128},{112,144}... | collective-permute-start | bytes 294920 | tf_op jit(solution)/shard_map/ppermute | solution.py:311
  99.3 8.2 %collective-permute-start.30 = (f32[248,128]{1,0:T(8,128)S(1)}, f32[248,128]{1,0:T(8,128)S(1)}, u32[]{:S(2)}, u32[]{:S(2)}) collective-permute-start(f32[248,128]{1,0:T(8,128)S(1)} %get-tuple-element.122), channel_id=1, source_target_pairs={{0,16},{16,0},{32,48},{48,32},{64,80},{80,64},{96,112},{112,96},{1... | collective-permute-start | bytes 380936 | tf_op jit(solution)/shard_map/ppermute | solution.py:300
  113.0 9.6 %collective-permute-start.33 = (f32[64,512]{1,0:T(8,128)S(1)}, f32[64,512]{1,0:T(8,128)S(1)}, u32[]{:S(2)}, u32[]{:S(2)}) collective-permute-start(f32[64,512]{1,0:T(8,128)S(1)} %get-tuple-element.142), channel_id=1, source_target_pairs={{0,10},{1,11},{2,8},{3,9},{4,14},{5,15},{6,12},{7,13},{8,2},{9,3},... | collective-permute-start | bytes 393224 | tf_op jit(solution)/shard_map/ppermute | solution.py:334
  114.6 9.8 %collective-permute-start.34 = (f32[64,512]{1,0:T(8,128)S(1)}, f32[64,512]{1,0:T(8,128)S(1)}, u32[]{:S(2)}, u32[]{:S(2)}) collective-permute-start(f32[64,512]{1,0:T(8,128)S(1)} %get-tuple-element.143), channel_id=1, source_target_pairs={{0,6},{1,7},{2,4},{3,5},{4,10},{5,11},{6,8},{7,9},{8,14},{9,15},{1... | collective-permute-start | bytes 393224 | tf_op jit(solution)/shard_map/ppermute | solution.py:334
  116.9 9.1 %collective-permute-start.35 = (f32[64,512]{1,0:T(8,128)S(1)}, f32[64,512]{1,0:T(8,128)S(1)}, u32[]{:S(2)}, u32[]{:S(2)}) collective-permute-start(f32[64,512]{1,0:T(8,128)S(1)} %get-tuple-element.144), channel_id=1, source_target_pairs={{0,14},{1,15},{2,12},{3,13},{4,2},{5,3},{6,0},{7,1},{8,6},{9,7},{1... | collective-permute-start | bytes 393224 | tf_op jit(solution)/shard_map/ppermute | solution.py:334
  119.7 8.1 %collective-permute-start.36 = (f32[64,512]{1,0:T(8,128)S(1)}, f32[64,512]{1,0:T(8,128)S(1)}, u32[]{:S(2)}, u32[]{:S(2)}) collective-permute-start(f32[64,512]{1,0:T(8,128)S(1)} %get-tuple-element.145), channel_id=1, source_target_pairs={{0,8},{1,9},{2,10},{3,11},{4,12},{5,13},{6,14},{7,15},{8,0},{9,1},... | collective-permute-start | bytes 393224 | tf_op jit(solution)/shard_map/ppermute | solution.py:334
  119.7 8.8 %collective-permute-start.37 = (f32[64,512]{1,0:T(8,128)S(1)}, f32[64,512]{1,0:T(8,128)S(1)}, u32[]{:S(2)}, u32[]{:S(2)}) collective-permute-start(f32[64,512]{1,0:T(8,128)S(1)} %get-tuple-element.146), channel_id=1, source_target_pairs={{0,2},{1,3},{2,0},{3,1},{4,6},{5,7},{6,4},{7,5},{8,10},{9,11},{10,... | collective-permute-start | bytes 393224 | tf_op jit(solution)/shard_map/ppermute | solution.py:334
  122.6 7.6 %collective-permute-start.38 = (f32[64,512]{1,0:T(8,128)S(1)}, f32[64,512]{1,0:T(8,128)S(1)}, u32[]{:S(2)}, u32[]{:S(2)}) collective-permute-start(f32[64,512]{1,0:T(8,128)S(1)} %get-tuple-element.147), channel_id=1, source_target_pairs={{0,4},{1,5},{2,6},{3,7},{4,8},{5,9},{6,10},{7,11},{8,12},{9,13},{1... | collective-permute-start | bytes 393224 | tf_op jit(solution)/shard_map/ppermute | solution.py:334
  (25 other events, 208.9 us)

commit v3 on v2

--- a/solution.py
+++ b/solution.py
@@ -44,26 +44,28 @@
     return [pltpu.with_memory_space_constraint(value, pltpu.VMEM) for value in values]
 
 
-def weights_kernel(place, own, other, high, low):
-    core = place[0]
-
-    def step(tap, carry):
-        mine, theirs = own[tap], other[tap]
-        first = jnp.where(core == 0, mine, theirs)
-        second = jnp.where(core == 0, theirs, mine)
-        both = jnp.concatenate([first, second], axis=0)
+DEPTH = 3 * 9 * 64
+
+
+def weights_kernel(place, own, other, stacked):
+    core = place[0]
+    for tap in range(27):
+        p, q, r = tap // 9, tap // 3 % 3, tap % 3
+        both = in_order(core, own[tap], other[tap])
         top = both.astype(BF16)
-        high[tap] = top
-        low[tap] = (both - top.astype(F32)).astype(BF16)
-        return carry
-
-    lax.fori_loop(0, 27, step, 0)
+        low = (both - top.astype(F32)).astype(BF16)
+        if r < 2:
+            begin = 384 * q + 64 * r
+            rows = (begin, begin + 128, begin + 256)
+        else:
+            rows = (1152 + 128 * q, 1216 + 128 * q, 1536 + 64 * q)
+        for row, value in zip(rows, (top, top, low)):
+            stacked[p, row : row + 64, :] = value
 
 
 def split_weights(place, own, other):
-    outs = (close((27, 64, 512), BF16), close((27, 64, 512), BF16))
-    return call(weights_kernel, outs, flops=8000000, touched=9000000)(
-        in_specs=[SMEM, VMEM, VMEM], out_specs=(VMEM, VMEM)
+    return call(weights_kernel, close((3, DEPTH, 512), BF16), flops=8000000, touched=9000000)(
+        in_specs=[SMEM, VMEM, VMEM], out_specs=VMEM
     )(place, own, other)
 
 
@@ -238,9 +240,9 @@
 
 def conv_kernel(place, rows, *rest):
     pieces = rest[:4]
-    high, low = rest[4:6]
-    outs = rest[6:14]
-    rims, padded, columns, total, turned = rest[14:]
+    stacked = rest[4]
+    outs = rest[5:13]
+    rims, padded, columns, total, turned = rest[13:]
     rims[...] = (pieces[0][...] + pieces[1][...]) + (pieces[2][...] + pieces[3][...])
     for x in range(8):
         for y in range(8):
@@ -253,18 +255,18 @@
         columns[spot // 10, spot % 10, :, 0:128] = jnp.concatenate([before, same], axis=1)
         columns[spot // 10, spot % 10, :, 128:192] = after
 
-    dot = functools.partial(jnp.dot, preferred_element_type=F32)
     for p in range(3):
-        sums = None
+        firsts, pairs, tails = [], [], []
         for q in range(3):
             values = columns[p : p + 8, q : q + 8, :, 0:192].reshape(512, 192)
-            top = values.astype(BF16)
-            rest_of = (values - top.astype(F32)).astype(BF16)
-            tap = 9 * p + 3 * q
-            heavy = high[tap : tap + 3].reshape(192, 512)
-            light = low[tap : tap + 3].reshape(192, 512)
-            part = dot(top, heavy) + (dot(rest_of, heavy) + dot(top, light))
-            sums = part if sums is None else sums + part
+            top = values.astype(BF16).astype(F32)
+            low = values - top
+            firsts += [top[:, 0:128], low[:, 0:128], top[:, 0:128]]
+            pairs.append(jnp.concatenate([top[:, 128:192], low[:, 128:192]], axis=1))
+            tails.append(top[:, 128:192])
+        ends = [jnp.concatenate(tails[:2], axis=1), tails[2]]
+        left = jnp.concatenate([piece.astype(BF16) for piece in firsts + pairs + ends], axis=1)
+        sums = jnp.dot(left, stacked[p], preferred_element_type=F32)
         if p == 0:
             total[...] = sums
         else:
@@ -276,7 +278,7 @@
         outs[step][...] = turned[pl.ds(pl.multiple_of(target * 64, 64), 64), :]
 
 
-def conv(place, rows, rims, high, low):
+def conv(place, rows, rims, stacked):
     outs = tuple(close((64, 512)) for _ in range(8))
     scratch = [
         pltpu.VMEM((RIM_ROWS, 128), F32),
@@ -288,8 +290,8 @@
     return call(
         conv_kernel, outs, scratch, flops=2 * 3 * 1024 * 1728 * 256, touched=8000000, room=24
     )(
-        in_specs=[SMEM] + [VMEM] * 7, out_specs=tuple([VMEM] * 8)
-    )(place, *near([rows, *rims, high, low]))
+        in_specs=[SMEM] + [VMEM] * 6, out_specs=tuple([VMEM] * 8)
+    )(place, *near([rows, *rims, stacked]))
 
 
 def to_other_core(value):
@@ -305,11 +307,11 @@
     return lax.ppermute(value, ("leaf", "chan"), pairs)
 
 
-def gather_rims(place, tables, faces, weights=()):
+def gather_rims(place, tables, faces, weights=None):
     found = []
     for step in SENT:
         found.append(lax.ppermute(faces, "leaf", [(i, (i + 2 * step) % 16) for i in range(16)]))
-    if weights:
+    if weights is not None:
         found, weights = lax.optimization_barrier((found, weights))
     own, beside, across, both = cut_rims(place, *tables, found + [faces])
     return [own, to_other_both(both), to_other_x(beside), to_other_core(across)], weights
@@ -317,7 +319,7 @@
 
 def conv_beside(place, rows, rims, weights, moved):
     rims, moved = lax.optimization_barrier((rims, moved))
-    parts = conv(place, rows, rims, *weights)
+    parts = conv(place, rows, rims, weights)
     return lax.optimization_barrier((parts, [to_other_core(value) for value in moved]))
 
 
@@ -339,13 +341,15 @@
     leaf, chan = lax.axis_index("leaf"), lax.axis_index("chan")
     core = chan % 2
     place = jnp.stack([core, leaf % 2, leaf // 2, chan // 2]).astype(jnp.int32)
+    place, weight_in = lax.optimization_barrier((place, weight_in))
     others = to_other_core(features)
     rows, faces = call(features_kernel, (close((512, 64)), close((192, 128))))(
         in_specs=[SMEM, SMEM, VMEM, VMEM, VMEM], out_specs=(VMEM, VMEM)
     )(place, leaf_counts, occupancy, features, *near([others]))
     tables = neighbours, to_other_x(neighbours)
     bias_in, bias_out = bias_in.reshape(1, 32), bias_out.reshape(1, 32)
-    weights = split_weights(place, weight_in, to_other_core(weight_in))
+    swapped, tables = lax.optimization_barrier((to_other_core(weight_in), tables))
+    weights = split_weights(place, weight_in, swapped)
 
     rims, weights = gather_rims(place, tables, faces, weights)
     parts, (swapped, other_bias) = conv_beside(place, rows, rims, weights, [weight_out, bias_in])

time: 135 us -> 130 us (0.963)
  starting transfers between devices: 63.4 us -> 61 us
  Pallas kernels: 19 us -> 17 us
    pallas_call x2, Pallas kernels: 9.96 us -> 8.34 us  [conv(): call(conv_kernel, outs, scratch, flops=2 * 3 * 1024 * 1728 * 256, touched...]
  transfers between devices with their start and end apart: 41 -> 41, of which waited for: 22 -> 22; matrix products, arithmetic and copies ran while one was open for 0% -> 0% of each run, Pallas kernels for 10% -> 9%
where the time goes in v3:
time: 130 us; the launch traced here: 129 us
  starting transfers between devices  61 us (47%)
  waiting for transfers between devices  47.3 us (36%)
  Pallas kernels  17 us (13%)
  local copies, waits for them, and re-layouts  3.09 us (2%)
    ppermute x14, starting transfers between devices, gather_rims(): lax.ppermute(faces, 'leaf', [(i, (i + 2 * step) % 16) for i in range(16)])  27.6 us
    ppermute x14, starting transfers between devices, add_over_chips(): lax.ppermute(part, 'chan', [(i, route_target(i, route)) for i in range(16)])  21.9 us
    ppermute x14, waiting for transfers between devices, gather_rims(): lax.ppermute(faces, 'leaf', [(i, (i + 2 * step) % 16) for i in range(16)])  15.9 us
    ppermute x14, waiting for transfers between devices, add_over_chips(): lax.ppermute(part, 'chan', [(i, route_target(i, route)) for i in range(16)])  15.8 us
    pallas_call x2, Pallas kernels, conv(): call(conv_kernel, outs, scratch, flops=2 * 3 * 1024 * 1728 * 256, touched...  8.34 us
    ppermute x2, waiting for transfers between devices, to_other_both(): return lax.ppermute(value, ('leaf', 'chan'), pairs)  6.26 us
    ppermute x8, starting transfers between devices, to_other_core(): return lax.ppermute(value, 'chan', [(i, i ^ 1) for i in range(16)])  5.68 us
    ppermute x3, waiting for transfers between devices, to_other_x(): return lax.ppermute(value, 'leaf', [(i, i ^ 1) for i in range(16)])  5.44 us
  transfers between devices with their start and end apart: 41, of which 22 were waited for; matrix products, arithmetic and copies ran while one was open for 0% of the time, Pallas kernels for 9%

profile of v3, /device:TPU:1, one launch (start us, length us, event | category | flops | bytes accessed | tf_op | source)
XLA Modules:
  0.0 129.4 jit_solution(10229655967369351036)
XLA Ops:
  0.1 3.3 %collective-permute-start.1 = (f32[27,32,512]{2,1,0:T(8,128)}, f32[27,32,512]{2,1,0:T(8,128)S(1)}, u32[]{:S(2)}, u32[]{:S(2)}) collective-permute-start(f32[27,32,512]{2,1,0:T(8,128)} %own.3), channel_id=1, source_target_pairs={{0,1},{1,0},{2,3},{3,2},{4,5},{5,4},{6,7},{7,6},{8,9},{9,8},{10,11... | collective-permute-start | bytes 5308424 | tf_op jit(solution)/shard_map/ppermute | solution.py:298
  4.1 3.0 %collective-permute-done.other = f32[32,2,512]{2,1,0:T(2,128)S(1)} collective-permute-done((f32[32,2,512]{2,1,0:T(2,128)}, f32[32,2,512]{2,1,0:T(2,128)S(1)}, u32[]{:S(2)}, u32[]{:S(2)}) %collective-permute-start) | collective-permute-done | bytes 131104 | tf_op jit(solution)/shard_map/ppermute | solution.py:298
  9.5 5.3 %collective-permute-start.9 = (f32[192,128]{1,0:T(8,128)S(1)}, f32[192,128]{1,0:T(8,128)S(1)}, u32[]{:S(2)}, u32[]{:S(2)}) collective-permute-start(f32[192,128]{1,0:T(8,128)S(1)} %get-tuple-element.83.rest_7_), channel_id=1, source_target_pairs={{0,128},{16,144},{32,160},{48,176},{64,192},{80,208},{96,224},{112... | collective-permute-start | bytes 294920 | tf_op jit(solution)/shard_map/ppermute | solution.py:313
  17.6 2.8 %collective-permute-start.7 = (f32[192,128]{1,0:T(8,128)S(1)}, f32[192,128]{1,0:T(8,128)S(1)}, u32[]{:S(2)}, u32[]{:S(2)}) collective-permute-start(f32[192,128]{1,0:T(8,128)S(1)} %get-tuple-element.83.rest_7_), channel_id=1, source_target_pairs={{0,160},{16,176},{32,192},{48,208},{64,224},{80,240},{96,0},{112,1... | collective-permute-start | bytes 294920 | tf_op jit(solution)/shard_map/ppermute | solution.py:313
  21.6 2.4 %collective-permute-start.5 = (f32[192,128]{1,0:T(8,128)S(1)}, f32[192,128]{1,0:T(8,128)S(1)}, u32[]{:S(2)}, u32[]{:S(2)}) collective-permute-start(f32[192,128]{1,0:T(8,128)S(1)} %get-tuple-element.83.rest_7_), channel_id=1, source_target_pairs={{0,192},{16,208},{32,224},{48,240},{64,0},{80,16},{96,32},{112,48}... | collective-permute-start | bytes 294920 | tf_op jit(solution)/shard_map/ppermute | solution.py:313
  24.0 3.1 %collective-permute-done.8.rest_5_ = f32[192,128]{1,0:T(8,128)S(1)} collective-permute-done((f32[192,128]{1,0:T(8,128)S(1)}, f32[192,128]{1,0:T(8,128)S(1)}, u32[]{:S(2)}, u32[]{:S(2)}) %collective-permute-start.8) | collective-permute-done | bytes 98336 | tf_op jit(solution)/shard_map/ppermute | solution.py:313
  27.1 2.7 %collective-permute-start.3 = (f32[192,128]{1,0:T(8,128)S(1)}, f32[192,128]{1,0:T(8,128)S(1)}, u32[]{:S(2)}, u32[]{:S(2)}) collective-permute-start(f32[192,128]{1,0:T(8,128)S(1)} %get-tuple-element.83.rest_7_), channel_id=1, source_target_pairs={{0,224},{16,240},{32,0},{48,16},{64,32},{80,48},{96,64},{112,80},{... | collective-permute-start | bytes 294920 | tf_op jit(solution)/shard_map/ppermute | solution.py:313
  38.1 3.6 %collective-permute-done.10.rest_1_ = f32[248,128]{1,0:T(8,128)S(1)} collective-permute-done((f32[248,128]{1,0:T(8,128)S(1)}, f32[248,128]{1,0:T(8,128)S(1)}, u32[]{:S(2)}, u32[]{:S(2)}) %collective-permute-start.10) | collective-permute-done | bytes 127008 | tf_op jit(solution)/shard_map/ppermute | solution.py:307
  41.8 2.7 %collective-permute-done.11.rest_2_ = f32[248,128]{1,0:T(8,128)S(1)} collective-permute-done((f32[248,128]{1,0:T(8,128)S(1)}, f32[248,128]{1,0:T(8,128)S(1)}, u32[]{:S(2)}, u32[]{:S(2)}) %collective-permute-start.11) | collective-permute-done | bytes 127008 | tf_op jit(solution)/shard_map/ppermute | solution.py:302
  45.2 4.2 %shard_map.85 = (f32[64,512]{1,0:T(8,128)S(1)}, f32[64,512]{1,0:T(8,128)S(1)}, f32[64,512]{1,0:T(8,128)S(1)}, f32[64,512]{1,0:T(8,128)S(1)}, f32[64,512]{1,0:T(8...) custom-call(s32[4]{0:T(128)S(1)} %pad_add_fusion.place, ...), custom_call_target="tpu_custom_call" | custom-call | flops 2717908992 | bytes 8000000 | tf_op jit(solution)/shard_map/pallas_call | solution.py:290
  49.4 5.1 %collective-permute-start.15 = (f32[64,512]{1,0:T(8,128)S(1)}, f32[64,512]{1,0:T(8,128)S(1)}, u32[]{:S(2)}, u32[]{:S(2)}) collective-permute-start(f32[64,512]{1,0:T(8,128)S(1)} %get-tuple-element.113), channel_id=1, source_target_pairs={{0,10},{1,11},{2,8},{3,9},{4,14},{5,15},{6,12},{7,13},{8,2},{9,3},... | collective-permute-start | bytes 393224 | tf_op jit(solution)/shard_map/ppermute | solution.py:336
  55.2 4.4 %collective-permute-start.17 = (f32[64,512]{1,0:T(8,128)S(1)}, f32[64,512]{1,0:T(8,128)S(1)}, u32[]{:S(2)}, u32[]{:S(2)}) collective-permute-start(f32[64,512]{1,0:T(8,128)S(1)} %get-tuple-element.115), channel_id=1, source_target_pairs={{0,14},{1,15},{2,12},{3,13},{4,2},{5,3},{6,0},{7,1},{8,6},{9,7},{1... | collective-permute-start | bytes 393224 | tf_op jit(solution)/shard_map/ppermute | solution.py:336
  60.4 2.2 %collective-permute-done.16.rest_2_ = f32[64,512]{1,0:T(8,128)S(1)} collective-permute-done((f32[64,512]{1,0:T(8,128)S(1)}, f32[64,512]{1,0:T(8,128)S(1)}, u32[]{:S(2)}, u32[]{:S(2)}) %collective-permute-start.16) | collective-permute-done | bytes 131104 | tf_op jit(solution)/shard_map/ppermute | solution.py:336
  66.8 2.9 %collective-permute-done.20.rest_6_ = f32[64,512]{1,0:T(8,128)S(1)} collective-permute-done((f32[64,512]{1,0:T(8,128)S(1)}, f32[64,512]{1,0:T(8,128)S(1)}, u32[]{:S(2)}, u32[]{:S(2)}) %collective-permute-start.20) | collective-permute-done | bytes 131104 | tf_op jit(solution)/shard_map/ppermute | solution.py:336
  70.7 3.5 %collective-permute-start.28 = (f32[192,128]{1,0:T(8,128)S(1)}, f32[192,128]{1,0:T(8,128)S(1)}, u32[]{:S(2)}, u32[]{:S(2)}) collective-permute-start(f32[192,128]{1,0:T(8,128)S(1)} %get-tuple-element.121.rest_7_), channel_id=1, source_target_pairs={{0,128},{16,144},{32,160},{48,176},{64,192},{80,208},{96,224},{112... | collective-permute-start | bytes 294920 | tf_op jit(solution)/shard_map/ppermute | solution.py:313
  75.3 3.5 %collective-permute-start.26 = (f32[192,128]{1,0:T(8,128)S(1)}, f32[192,128]{1,0:T(8,128)S(1)}, u32[]{:S(2)}, u32[]{:S(2)}) collective-permute-start(f32[192,128]{1,0:T(8,128)S(1)} %get-tuple-element.121.rest_7_), channel_id=1, source_target_pairs={{0,160},{16,176},{32,192},{48,208},{64,224},{80,240},{96,0},{112,1... | collective-permute-start | bytes 294920 | tf_op jit(solution)/shard_map/ppermute | solution.py:313
  79.2 3.1 %collective-permute-start.24 = (f32[192,128]{1,0:T(8,128)S(1)}, f32[192,128]{1,0:T(8,128)S(1)}, u32[]{:S(2)}, u32[]{:S(2)}) collective-permute-start(f32[192,128]{1,0:T(8,128)S(1)} %get-tuple-element.121.rest_7_), channel_id=1, source_target_pairs={{0,192},{16,208},{32,224},{48,240},{64,0},{80,16},{96,32},{112,48}... | collective-permute-start | bytes 294920 | tf_op jit(solution)/shard_map/ppermute | solution.py:313
  82.3 6.0 %collective-permute-done.27.rest_5_ = f32[192,128]{1,0:T(8,128)S(1)} collective-permute-done((f32[192,128]{1,0:T(8,128)S(1)}, f32[192,128]{1,0:T(8,128)S(1)}, u32[]{:S(2)}, u32[]{:S(2)}) %collective-permute-start.27) | collective-permute-done | bytes 98336 | tf_op jit(solution)/shard_map/ppermute | solution.py:313
  98.0 2.6 %collective-permute-done.29.rest_1_ = f32[248,128]{1,0:T(8,128)S(1)} collective-permute-done((f32[248,128]{1,0:T(8,128)S(1)}, f32[248,128]{1,0:T(8,128)S(1)}, u32[]{:S(2)}, u32[]{:S(2)}) %collective-permute-start.29) | collective-permute-done | bytes 127008 | tf_op jit(solution)/shard_map/ppermute | solution.py:307
  100.6 2.7 %collective-permute-done.30.rest_2_ = f32[248,128]{1,0:T(8,128)S(1)} collective-permute-done((f32[248,128]{1,0:T(8,128)S(1)}, f32[248,128]{1,0:T(8,128)S(1)}, u32[]{:S(2)}, u32[]{:S(2)}) %collective-permute-start.30) | collective-permute-done | bytes 127008 | tf_op jit(solution)/shard_map/ppermute | solution.py:302
  103.8 4.2 %shard_map.89 = (f32[64,512]{1,0:T(8,128)S(1)}, f32[64,512]{1,0:T(8,128)S(1)}, f32[64,512]{1,0:T(8,128)S(1)}, f32[64,512]{1,0:T(8,128)S(1)}, f32[64,512]{1,0:T(8...) custom-call(s32[4]{0:T(128)S(1)} %pad_add_fusion.place, ...), custom_call_target="tpu_custom_call" | custom-call | flops 2717908992 | bytes 8000000 | tf_op jit(solution)/shard_map/pallas_call | solution.py:290
  110.1 2.5 %collective-permute-start.34 = (f32[64,512]{1,0:T(8,128)S(1)}, f32[64,512]{1,0:T(8,128)S(1)}, u32[]{:S(2)}, u32[]{:S(2)}) collective-permute-start(f32[64,512]{1,0:T(8,128)S(1)} %get-tuple-element.143), channel_id=1, source_target_pairs={{0,6},{1,7},{2,4},{3,5},{4,10},{5,11},{6,8},{7,9},{8,14},{9,15},{1... | collective-permute-start | bytes 393224 | tf_op jit(solution)/shard_map/ppermute | solution.py:336
  112.6 2.6 %collective-permute-start.35 = (f32[64,512]{1,0:T(8,128)S(1)}, f32[64,512]{1,0:T(8,128)S(1)}, u32[]{:S(2)}, u32[]{:S(2)}) collective-permute-start(f32[64,512]{1,0:T(8,128)S(1)} %get-tuple-element.144), channel_id=1, source_target_pairs={{0,14},{1,15},{2,12},{3,13},{4,2},{5,3},{6,0},{7,1},{8,6},{9,7},{1... | collective-permute-start | bytes 393224 | tf_op jit(solution)/shard_map/ppermute | solution.py:336
  115.2 2.4 %collective-permute-start.37 = (f32[64,512]{1,0:T(8,128)S(1)}, f32[64,512]{1,0:T(8,128)S(1)}, u32[]{:S(2)}, u32[]{:S(2)}) collective-permute-start(f32[64,512]{1,0:T(8,128)S(1)} %get-tuple-element.146), channel_id=1, source_target_pairs={{0,2},{1,3},{2,0},{3,1},{4,6},{5,7},{6,4},{7,5},{8,10},{9,11},{10,... | collective-permute-start | bytes 393224 | tf_op jit(solution)/shard_map/ppermute | solution.py:336
  (85 shorter events, 48.0 us)
Async XLA Ops:
  0.1 27.0 %collective-permute-start.1 = (f32[27,32,512]{2,1,0:T(8,128)}, f32[27,32,512]{2,1,0:T(8,128)S(1)}, u32[]{:S(2)}, u32[]{:S(2)}) collective-permute-start(f32[27,32,512]{2,1,0:T(8,128)} %own.3), channel_id=1, source_target_pairs={{0,1},{1,0},{2,3},{3,2},{4,5},{5,4},{6,7},{7,6},{8,9},{9,8},{10,11... | collective-permute-start | bytes 5308424 | tf_op jit(solution)/shard_map/ppermute | solution.py:298
  9.5 12.1 %collective-permute-start.9 = (f32[192,128]{1,0:T(8,128)S(1)}, f32[192,128]{1,0:T(8,128)S(1)}, u32[]{:S(2)}, u32[]{:S(2)}) collective-permute-start(f32[192,128]{1,0:T(8,128)S(1)} %get-tuple-element.83.rest_7_), channel_id=1, source_target_pairs={{0,128},{16,144},{32,160},{48,176},{64,192},{80,208},{96,224},{112... | collective-permute-start | bytes 294920 | tf_op jit(solution)/shard_map/ppermute | solution.py:313
  14.8 12.4 %collective-permute-start.8 = (f32[192,128]{1,0:T(8,128)S(1)}, f32[192,128]{1,0:T(8,128)S(1)}, u32[]{:S(2)}, u32[]{:S(2)}) collective-permute-start(f32[192,128]{1,0:T(8,128)S(1)} %get-tuple-element.83.rest_7_), channel_id=1, source_target_pairs={{0,96},{16,112},{32,128},{48,144},{64,160},{80,176},{96,192},{112,... | collective-permute-start | bytes 294920 | tf_op jit(solution)/shard_map/ppermute | solution.py:313
  17.6 14.8 %collective-permute-start.7 = (f32[192,128]{1,0:T(8,128)S(1)}, f32[192,128]{1,0:T(8,128)S(1)}, u32[]{:S(2)}, u32[]{:S(2)}) collective-permute-start(f32[192,128]{1,0:T(8,128)S(1)} %get-tuple-element.83.rest_7_), channel_id=1, source_target_pairs={{0,160},{16,176},{32,192},{48,208},{64,224},{80,240},{96,0},{112,1... | collective-permute-start | bytes 294920 | tf_op jit(solution)/shard_map/ppermute | solution.py:313
  20.4 12.0 %collective-permute-start.6 = (f32[192,128]{1,0:T(8,128)S(1)}, f32[192,128]{1,0:T(8,128)S(1)}, u32[]{:S(2)}, u32[]{:S(2)}) collective-permute-start(f32[192,128]{1,0:T(8,128)S(1)} %get-tuple-element.83.rest_7_), channel_id=1, source_target_pairs={{0,64},{16,80},{32,96},{48,112},{64,128},{80,144},{96,160},{112,17... | collective-permute-start | bytes 294920 | tf_op jit(solution)/shard_map/ppermute | solution.py:313
  21.6 10.8 %collective-permute-start.5 = (f32[192,128]{1,0:T(8,128)S(1)}, f32[192,128]{1,0:T(8,128)S(1)}, u32[]{:S(2)}, u32[]{:S(2)}) collective-permute-start(f32[192,128]{1,0:T(8,128)S(1)} %get-tuple-element.83.rest_7_), channel_id=1, source_target_pairs={{0,192},{16,208},{32,224},{48,240},{64,0},{80,16},{96,32},{112,48}... | collective-permute-start | bytes 294920 | tf_op jit(solution)/shard_map/ppermute | solution.py:313
  49.4 10.8 %collective-permute-start.15 = (f32[64,512]{1,0:T(8,128)S(1)}, f32[64,512]{1,0:T(8,128)S(1)}, u32[]{:S(2)}, u32[]{:S(2)}) collective-permute-start(f32[64,512]{1,0:T(8,128)S(1)} %get-tuple-element.113), channel_id=1, source_target_pairs={{0,10},{1,11},{2,8},{3,9},{4,14},{5,15},{6,12},{7,13},{8,2},{9,3},... | collective-permute-start | bytes 393224 | tf_op jit(solution)/shard_map/ppermute | solution.py:336
  54.4 8.2 %collective-permute-start.16 = (f32[64,512]{1,0:T(8,128)S(1)}, f32[64,512]{1,0:T(8,128)S(1)}, u32[]{:S(2)}, u32[]{:S(2)}) collective-permute-start(f32[64,512]{1,0:T(8,128)S(1)} %get-tuple-element.114), channel_id=1, source_target_pairs={{0,6},{1,7},{2,4},{3,5},{4,10},{5,11},{6,8},{7,9},{8,14},{9,15},{1... | collective-permute-start | bytes 393224 | tf_op jit(solution)/shard_map/ppermute | solution.py:336
  55.2 9.0 %collective-permute-start.17 = (f32[64,512]{1,0:T(8,128)S(1)}, f32[64,512]{1,0:T(8,128)S(1)}, u32[]{:S(2)}, u32[]{:S(2)}) collective-permute-start(f32[64,512]{1,0:T(8,128)S(1)} %get-tuple-element.115), channel_id=1, source_target_pairs={{0,14},{1,15},{2,12},{3,13},{4,2},{5,3},{6,0},{7,1},{8,6},{9,7},{1... | collective-permute-start | bytes 393224 | tf_op jit(solution)/shard_map/ppermute | solution.py:336
  59.5 7.3 %collective-permute-start.19 = (f32[64,512]{1,0:T(8,128)S(1)}, f32[64,512]{1,0:T(8,128)S(1)}, u32[]{:S(2)}, u32[]{:S(2)}) collective-permute-start(f32[64,512]{1,0:T(8,128)S(1)} %get-tuple-element.117), channel_id=1, source_target_pairs={{0,2},{1,3},{2,0},{3,1},{4,6},{5,7},{6,4},{7,5},{8,10},{9,11},{10,... | collective-permute-start | bytes 393224 | tf_op jit(solution)/shard_map/ppermute | solution.py:336
  60.1 9.5 %collective-permute-start.20 = (f32[64,512]{1,0:T(8,128)S(1)}, f32[64,512]{1,0:T(8,128)S(1)}, u32[]{:S(2)}, u32[]{:S(2)}) collective-permute-start(f32[64,512]{1,0:T(8,128)S(1)} %get-tuple-element.118), channel_id=1, source_target_pairs={{0,4},{1,5},{2,6},{3,7},{4,8},{5,9},{6,10},{7,11},{8,12},{9,13},{1... | collective-permute-start | bytes 393224 | tf_op jit(solution)/shard_map/ppermute | solution.py:336
  70.7 11.6 %collective-permute-start.28 = (f32[192,128]{1,0:T(8,128)S(1)}, f32[192,128]{1,0:T(8,128)S(1)}, u32[]{:S(2)}, u32[]{:S(2)}) collective-permute-start(f32[192,128]{1,0:T(8,128)S(1)} %get-tuple-element.121.rest_7_), channel_id=1, source_target_pairs={{0,128},{16,144},{32,160},{48,176},{64,192},{80,208},{96,224},{112... | collective-permute-start | bytes 294920 | tf_op jit(solution)/shard_map/ppermute | solution.py:313
  74.3 14.0 %collective-permute-start.27 = (f32[192,128]{1,0:T(8,128)S(1)}, f32[192,128]{1,0:T(8,128)S(1)}, u32[]{:S(2)}, u32[]{:S(2)}) collective-permute-start(f32[192,128]{1,0:T(8,128)S(1)} %get-tuple-element.121.rest_7_), channel_id=1, source_target_pairs={{0,96},{16,112},{32,128},{48,144},{64,160},{80,176},{96,192},{112,... | collective-permute-start | bytes 294920 | tf_op jit(solution)/shard_map/ppermute | solution.py:313
  75.3 13.0 %collective-permute-start.26 = (f32[192,128]{1,0:T(8,128)S(1)}, f32[192,128]{1,0:T(8,128)S(1)}, u32[]{:S(2)}, u32[]{:S(2)}) collective-permute-start(f32[192,128]{1,0:T(8,128)S(1)} %get-tuple-element.121.rest_7_), channel_id=1, source_target_pairs={{0,160},{16,176},{32,192},{48,208},{64,224},{80,240},{96,0},{112,1... | collective-permute-start | bytes 294920 | tf_op jit(solution)/shard_map/ppermute | solution.py:313
  78.7 10.5 %collective-permute-start.25 = (f32[192,128]{1,0:T(8,128)S(1)}, f32[192,128]{1,0:T(8,128)S(1)}, u32[]{:S(2)}, u32[]{:S(2)}) collective-permute-start(f32[192,128]{1,0:T(8,128)S(1)} %get-tuple-element.121.rest_7_), channel_id=1, source_target_pairs={{0,64},{16,80},{32,96},{48,112},{64,128},{80,144},{96,160},{112,17... | collective-permute-start | bytes 294920 | tf_op jit(solution)/shard_map/ppermute | solution.py:313
  79.2 12.2 %collective-permute-start.24 = (f32[192,128]{1,0:T(8,128)S(1)}, f32[192,128]{1,0:T(8,128)S(1)}, u32[]{:S(2)}, u32[]{:S(2)}) collective-permute-start(f32[192,128]{1,0:T(8,128)S(1)} %get-tuple-element.121.rest_7_), channel_id=1, source_target_pairs={{0,192},{16,208},{32,224},{48,240},{64,0},{80,16},{96,32},{112,48}... | collective-permute-start | bytes 294920 | tf_op jit(solution)/shard_map/ppermute | solution.py:313
  82.3 11.0 %collective-permute-start.23 = (f32[192,128]{1,0:T(8,128)S(1)}, f32[192,128]{1,0:T(8,128)S(1)}, u32[]{:S(2)}, u32[]{:S(2)}) collective-permute-start(f32[192,128]{1,0:T(8,128)S(1)} %get-tuple-element.121.rest_7_), channel_id=1, source_target_pairs={{0,32},{16,48},{32,64},{48,80},{64,96},{80,112},{96,128},{112,144}... | collective-permute-start | bytes 294920 | tf_op jit(solution)/shard_map/ppermute | solution.py:313
  95.4 7.9 %collective-permute-start.30 = (f32[248,128]{1,0:T(8,128)S(1)}, f32[248,128]{1,0:T(8,128)S(1)}, u32[]{:S(2)}, u32[]{:S(2)}) collective-permute-start(f32[248,128]{1,0:T(8,128)S(1)} %get-tuple-element.124), channel_id=1, source_target_pairs={{0,16},{16,0},{32,48},{48,32},{64,80},{80,64},{96,112},{112,96},{1... | collective-permute-start | bytes 380936 | tf_op jit(solution)/shard_map/ppermute | solution.py:302
  108.0 9.6 %collective-permute-start.33 = (f32[64,512]{1,0:T(8,128)S(1)}, f32[64,512]{1,0:T(8,128)S(1)}, u32[]{:S(2)}, u32[]{:S(2)}) collective-permute-start(f32[64,512]{1,0:T(8,128)S(1)} %get-tuple-element.142), channel_id=1, source_target_pairs={{0,10},{1,11},{2,8},{3,9},{4,14},{5,15},{6,12},{7,13},{8,2},{9,3},... | collective-permute-start | bytes 393224 | tf_op jit(solution)/shard_map/ppermute | solution.py:336
  110.1 9.4 %collective-permute-start.34 = (f32[64,512]{1,0:T(8,128)S(1)}, f32[64,512]{1,0:T(8,128)S(1)}, u32[]{:S(2)}, u32[]{:S(2)}) collective-permute-start(f32[64,512]{1,0:T(8,128)S(1)} %get-tuple-element.143), channel_id=1, source_target_pairs={{0,6},{1,7},{2,4},{3,5},{4,10},{5,11},{6,8},{7,9},{8,14},{9,15},{1... | collective-permute-start | bytes 393224 | tf_op jit(solution)/shard_map/ppermute | solution.py:336
  112.6 9.2 %collective-permute-start.35 = (f32[64,512]{1,0:T(8,128)S(1)}, f32[64,512]{1,0:T(8,128)S(1)}, u32[]{:S(2)}, u32[]{:S(2)}) collective-permute-start(f32[64,512]{1,0:T(8,128)S(1)} %get-tuple-element.144), channel_id=1, source_target_pairs={{0,14},{1,15},{2,12},{3,13},{4,2},{5,3},{6,0},{7,1},{8,6},{9,7},{1... | collective-permute-start | bytes 393224 | tf_op jit(solution)/shard_map/ppermute | solution.py:336
  115.2 7.4 %collective-permute-start.36 = (f32[64,512]{1,0:T(8,128)S(1)}, f32[64,512]{1,0:T(8,128)S(1)}, u32[]{:S(2)}, u32[]{:S(2)}) collective-permute-start(f32[64,512]{1,0:T(8,128)S(1)} %get-tuple-element.145), channel_id=1, source_target_pairs={{0,8},{1,9},{2,10},{3,11},{4,12},{5,13},{6,14},{7,15},{8,0},{9,1},... | collective-permute-start | bytes 393224 | tf_op jit(solution)/shard_map/ppermute | solution.py:336
  115.2 9.2 %collective-permute-start.37 = (f32[64,512]{1,0:T(8,128)S(1)}, f32[64,512]{1,0:T(8,128)S(1)}, u32[]{:S(2)}, u32[]{:S(2)}) collective-permute-start(f32[64,512]{1,0:T(8,128)S(1)} %get-tuple-element.146), channel_id=1, source_target_pairs={{0,2},{1,3},{2,0},{3,1},{4,6},{5,7},{6,4},{7,5},{8,10},{9,11},{10,... | collective-permute-start | bytes 393224 | tf_op jit(solution)/shard_map/ppermute | solution.py:336
  117.6 7.8 %collective-permute-start.38 = (f32[64,512]{1,0:T(8,128)S(1)}, f32[64,512]{1,0:T(8,128)S(1)}, u32[]{:S(2)}, u32[]{:S(2)}) collective-permute-start(f32[64,512]{1,0:T(8,128)S(1)} %get-tuple-element.147), channel_id=1, source_target_pairs={{0,4},{1,5},{2,6},{3,7},{4,8},{5,9},{6,10},{7,11},{8,12},{9,13},{1... | collective-permute-start | bytes 393224 | tf_op jit(solution)/shard_map/ppermute | solution.py:336
  (25 other events, 199.7 us)

commit v4 on v3

--- a/solution.py
+++ b/solution.py
@@ -91,12 +91,16 @@
     return chosen * jnp.where(core < counts[0], 1.0, 0.0)
 
 
-def features_kernel(place, counts, occupancy, own, other, rows, faces):
-    core = place[0]
-    mine = jnp.where(core == 0, own[:, 0, :], own[:, 1, :])
-    theirs = jnp.where(core == 0, other[:, 0, :], other[:, 1, :])
-    both = in_order(core, mine, theirs)
-    rows[...] = (both * active_voxels(core, counts, occupancy)).T
+def own_kernel(place, counts, occupancy, own, masked, active):
+    core = place[0]
+    active[...] = active_voxels(core, counts, occupancy)
+    masked[...] = jnp.where(core == 0, own[:, 0, :], own[:, 1, :]) * active[...]
+
+
+def features_kernel(place, masked, active, other, rows, faces):
+    core = place[0]
+    theirs = jnp.where(core == 0, other[:, 0, :], other[:, 1, :]) * active[...]
+    rows[...] = in_order(core, masked[...], theirs).T
     cut_faces(rows, faces)
 
 
@@ -343,9 +347,12 @@
     place = jnp.stack([core, leaf % 2, leaf // 2, chan // 2]).astype(jnp.int32)
     place, weight_in = lax.optimization_barrier((place, weight_in))
     others = to_other_core(features)
+    masked, active = call(own_kernel, (close((32, 512)), close((1, 512))))(
+        in_specs=[SMEM, SMEM, VMEM, VMEM], out_specs=(VMEM, VMEM)
+    )(place, leaf_counts, occupancy, features)
     rows, faces = call(features_kernel, (close((512, 64)), close((192, 128))))(
-        in_specs=[SMEM, SMEM, VMEM, VMEM, VMEM], out_specs=(VMEM, VMEM)
-    )(place, leaf_counts, occupancy, features, *near([others]))
+        in_specs=[SMEM, VMEM, VMEM, VMEM], out_specs=(VMEM, VMEM)
+    )(place, *near([masked, active, others]))
     tables = neighbours, to_other_x(neighbours)
     bias_in, bias_out = bias_in.reshape(1, 32), bias_out.reshape(1, 32)
     swapped, tables = lax.optimization_barrier((to_other_core(weight_in), tables))

time: 130 us -> 128 us (0.985)
  waiting for transfers between devices: 47.3 us -> 45.1 us
    ppermute x8, waiting for transfers between devices: 3.88 us -> 1.71 us  [to_other_core(): return lax.ppermute(value, 'chan', [(i, i ^ 1) for i in range(16)])]
where the time goes in v4:
time: 128 us
  starting transfers between devices  61.1 us (48%)
  waiting for transfers between devices  45.1 us (35%)
  Pallas kernels  17.6 us (14%)
  local copies, waits for them, and re-layouts  3.08 us (2%)
    ppermute x14, starting transfers between devices, gather_rims(): lax.ppermute(faces, 'leaf', [(i, (i + 2 * step) % 16) for i in range(16)])  27.6 us
    ppermute x14, starting transfers between devices, add_over_chips(): lax.ppermute(part, 'chan', [(i, route_target(i, route)) for i in range(16)])  22 us
    ppermute x14, waiting for transfers between devices, gather_rims(): lax.ppermute(faces, 'leaf', [(i, (i + 2 * step) % 16) for i in range(16)])  15.9 us
    ppermute x14, waiting for transfers between devices, add_over_chips(): lax.ppermute(part, 'chan', [(i, route_target(i, route)) for i in range(16)])  15.7 us
    pallas_call x2, Pallas kernels, conv(): call(conv_kernel, outs, scratch, flops=2 * 3 * 1024 * 1728 * 256, touched...  8.33 us
    ppermute x2, waiting for transfers between devices, to_other_both(): return lax.ppermute(value, ('leaf', 'chan'), pairs)  6.25 us
    ppermute x8, starting transfers between devices, to_other_core(): return lax.ppermute(value, 'chan', [(i, i ^ 1) for i in range(16)])  5.71 us
    ppermute x3, waiting for transfers between devices, to_other_x(): return lax.ppermute(value, 'leaf', [(i, i ^ 1) for i in range(16)])  5.44 us
  transfers between devices with their start and end apart: 41, of which 22 were waited for; matrix products, arithmetic and copies ran while one was open for 0% of the time, Pallas kernels for 9%

profile of v4, /device:TPU:1, one launch (start us, length us, event | category | flops | bytes accessed | tf_op | source)
XLA Modules:
  0.0 127.8 jit_solution(1341809349039989573)
XLA Ops:
  0.1 3.3 %collective-permute-start.1 = (f32[27,32,512]{2,1,0:T(8,128)}, f32[27,32,512]{2,1,0:T(8,128)S(1)}, u32[]{:S(2)}, u32[]{:S(2)}) collective-permute-start(f32[27,32,512]{2,1,0:T(8,128)} %own.3), channel_id=1, source_target_pairs={{0,1},{1,0},{2,3},{3,2},{4,5},{5,4},{6,7},{7,6},{8,9},{9,8},{10,11... | collective-permute-start | bytes 5308424 | tf_op jit(solution)/shard_map/ppermute | solution.py:302
  7.9 5.3 %collective-permute-start.9 = (f32[192,128]{1,0:T(8,128)S(1)}, f32[192,128]{1,0:T(8,128)S(1)}, u32[]{:S(2)}, u32[]{:S(2)}) collective-permute-start(f32[192,128]{1,0:T(8,128)S(1)} %get-tuple-element.87.rest_7_), channel_id=1, source_target_pairs={{0,128},{16,144},{32,160},{48,176},{64,192},{80,208},{96,224},{112... | collective-permute-start | bytes 294920 | tf_op jit(solution)/shard_map/ppermute | solution.py:317
  16.0 2.8 %collective-permute-start.7 = (f32[192,128]{1,0:T(8,128)S(1)}, f32[192,128]{1,0:T(8,128)S(1)}, u32[]{:S(2)}, u32[]{:S(2)}) collective-permute-start(f32[192,128]{1,0:T(8,128)S(1)} %get-tuple-element.87.rest_7_), channel_id=1, source_target_pairs={{0,160},{16,176},{32,192},{48,208},{64,224},{80,240},{96,0},{112,1... | collective-permute-start | bytes 294920 | tf_op jit(solution)/shard_map/ppermute | solution.py:317
  20.0 2.4 %collective-permute-start.5 = (f32[192,128]{1,0:T(8,128)S(1)}, f32[192,128]{1,0:T(8,128)S(1)}, u32[]{:S(2)}, u32[]{:S(2)}) collective-permute-start(f32[192,128]{1,0:T(8,128)S(1)} %get-tuple-element.87.rest_7_), channel_id=1, source_target_pairs={{0,192},{16,208},{32,224},{48,240},{64,0},{80,16},{96,32},{112,48}... | collective-permute-start | bytes 294920 | tf_op jit(solution)/shard_map/ppermute | solution.py:317
  22.4 3.1 %collective-permute-done.8.rest_5_ = f32[192,128]{1,0:T(8,128)S(1)} collective-permute-done((f32[192,128]{1,0:T(8,128)S(1)}, f32[192,128]{1,0:T(8,128)S(1)}, u32[]{:S(2)}, u32[]{:S(2)}) %collective-permute-start.8) | collective-permute-done | bytes 98336 | tf_op jit(solution)/shard_map/ppermute | solution.py:317
  25.5 2.7 %collective-permute-start.3 = (f32[192,128]{1,0:T(8,128)S(1)}, f32[192,128]{1,0:T(8,128)S(1)}, u32[]{:S(2)}, u32[]{:S(2)}) collective-permute-start(f32[192,128]{1,0:T(8,128)S(1)} %get-tuple-element.87.rest_7_), channel_id=1, source_target_pairs={{0,224},{16,240},{32,0},{48,16},{64,32},{80,48},{96,64},{112,80},{... | collective-permute-start | bytes 294920 | tf_op jit(solution)/shard_map/ppermute | solution.py:317
  33.9 2.2 %collective-permute-start.10 = (f32[248,128]{1,0:T(8,128)S(1)}, f32[248,128]{1,0:T(8,128)S(1)}, u32[]{:S(2)}, u32[]{:S(2)}) collective-permute-start(f32[248,128]{1,0:T(8,128)S(1)} %get-tuple-element.97), channel_id=1, source_target_pairs={{0,17},{1,16},{2,19},{3,18},{4,21},{5,20},{6,23},{7,22},{8,25},{9,... | collective-permute-start | bytes 380936 | tf_op jit(solution)/shard_map/ppermute | solution.py:311
  36.5 3.6 %collective-permute-done.10.rest_1_ = f32[248,128]{1,0:T(8,128)S(1)} collective-permute-done((f32[248,128]{1,0:T(8,128)S(1)}, f32[248,128]{1,0:T(8,128)S(1)}, u32[]{:S(2)}, u32[]{:S(2)}) %collective-permute-start.10) | collective-permute-done | bytes 127008 | tf_op jit(solution)/shard_map/ppermute | solution.py:311
  40.2 2.7 %collective-permute-done.11.rest_2_ = f32[248,128]{1,0:T(8,128)S(1)} collective-permute-done((f32[248,128]{1,0:T(8,128)S(1)}, f32[248,128]{1,0:T(8,128)S(1)}, u32[]{:S(2)}, u32[]{:S(2)}) %collective-permute-start.11) | collective-permute-done | bytes 127008 | tf_op jit(solution)/shard_map/ppermute | solution.py:306
  43.6 4.2 %shard_map.86 = (f32[64,512]{1,0:T(8,128)S(1)}, f32[64,512]{1,0:T(8,128)S(1)}, f32[64,512]{1,0:T(8,128)S(1)}, f32[64,512]{1,0:T(8,128)S(1)}, f32[64,512]{1,0:T(8...) custom-call(s32[4]{0:T(128)S(1)} %pad_add_fusion.place, ...), custom_call_target="tpu_custom_call" | custom-call | flops 2717908992 | bytes 8000000 | tf_op jit(solution)/shard_map/pallas_call | solution.py:294
  47.8 5.1 %collective-permute-start.15 = (f32[64,512]{1,0:T(8,128)S(1)}, f32[64,512]{1,0:T(8,128)S(1)}, u32[]{:S(2)}, u32[]{:S(2)}) collective-permute-start(f32[64,512]{1,0:T(8,128)S(1)} %get-tuple-element.117), channel_id=1, source_target_pairs={{0,10},{1,11},{2,8},{3,9},{4,14},{5,15},{6,12},{7,13},{8,2},{9,3},... | collective-permute-start | bytes 393224 | tf_op jit(solution)/shard_map/ppermute | solution.py:340
  53.6 4.4 %collective-permute-start.17 = (f32[64,512]{1,0:T(8,128)S(1)}, f32[64,512]{1,0:T(8,128)S(1)}, u32[]{:S(2)}, u32[]{:S(2)}) collective-permute-start(f32[64,512]{1,0:T(8,128)S(1)} %get-tuple-element.119), channel_id=1, source_target_pairs={{0,14},{1,15},{2,12},{3,13},{4,2},{5,3},{6,0},{7,1},{8,6},{9,7},{1... | collective-permute-start | bytes 393224 | tf_op jit(solution)/shard_map/ppermute | solution.py:340
  58.8 2.2 %collective-permute-done.16.rest_2_ = f32[64,512]{1,0:T(8,128)S(1)} collective-permute-done((f32[64,512]{1,0:T(8,128)S(1)}, f32[64,512]{1,0:T(8,128)S(1)}, u32[]{:S(2)}, u32[]{:S(2)}) %collective-permute-start.16) | collective-permute-done | bytes 131104 | tf_op jit(solution)/shard_map/ppermute | solution.py:340
  65.2 2.9 %collective-permute-done.20.rest_6_ = f32[64,512]{1,0:T(8,128)S(1)} collective-permute-done((f32[64,512]{1,0:T(8,128)S(1)}, f32[64,512]{1,0:T(8,128)S(1)}, u32[]{:S(2)}, u32[]{:S(2)}) %collective-permute-start.20) | collective-permute-done | bytes 131104 | tf_op jit(solution)/shard_map/ppermute | solution.py:340
  69.1 3.5 %collective-permute-start.28 = (f32[192,128]{1,0:T(8,128)S(1)}, f32[192,128]{1,0:T(8,128)S(1)}, u32[]{:S(2)}, u32[]{:S(2)}) collective-permute-start(f32[192,128]{1,0:T(8,128)S(1)} %get-tuple-element.125.rest_7_), channel_id=1, source_target_pairs={{0,128},{16,144},{32,160},{48,176},{64,192},{80,208},{96,224},{112... | collective-permute-start | bytes 294920 | tf_op jit(solution)/shard_map/ppermute | solution.py:317
  73.6 3.5 %collective-permute-start.26 = (f32[192,128]{1,0:T(8,128)S(1)}, f32[192,128]{1,0:T(8,128)S(1)}, u32[]{:S(2)}, u32[]{:S(2)}) collective-permute-start(f32[192,128]{1,0:T(8,128)S(1)} %get-tuple-element.125.rest_7_), channel_id=1, source_target_pairs={{0,160},{16,176},{32,192},{48,208},{64,224},{80,240},{96,0},{112,1... | collective-permute-start | bytes 294920 | tf_op jit(solution)/shard_map/ppermute | solution.py:317
  77.6 3.1 %collective-permute-start.24 = (f32[192,128]{1,0:T(8,128)S(1)}, f32[192,128]{1,0:T(8,128)S(1)}, u32[]{:S(2)}, u32[]{:S(2)}) collective-permute-start(f32[192,128]{1,0:T(8,128)S(1)} %get-tuple-element.125.rest_7_), channel_id=1, source_target_pairs={{0,192},{16,208},{32,224},{48,240},{64,0},{80,16},{96,32},{112,48}... | collective-permute-start | bytes 294920 | tf_op jit(solution)/shard_map/ppermute | solution.py:317
  80.7 6.0 %collective-permute-done.27.rest_5_ = f32[192,128]{1,0:T(8,128)S(1)} collective-permute-done((f32[192,128]{1,0:T(8,128)S(1)}, f32[192,128]{1,0:T(8,128)S(1)}, u32[]{:S(2)}, u32[]{:S(2)}) %collective-permute-start.27) | collective-permute-done | bytes 98336 | tf_op jit(solution)/shard_map/ppermute | solution.py:317
  96.4 2.6 %collective-permute-done.29.rest_1_ = f32[248,128]{1,0:T(8,128)S(1)} collective-permute-done((f32[248,128]{1,0:T(8,128)S(1)}, f32[248,128]{1,0:T(8,128)S(1)}, u32[]{:S(2)}, u32[]{:S(2)}) %collective-permute-start.29) | collective-permute-done | bytes 127008 | tf_op jit(solution)/shard_map/ppermute | solution.py:311
  99.0 2.7 %collective-permute-done.30.rest_2_ = f32[248,128]{1,0:T(8,128)S(1)} collective-permute-done((f32[248,128]{1,0:T(8,128)S(1)}, f32[248,128]{1,0:T(8,128)S(1)}, u32[]{:S(2)}, u32[]{:S(2)}) %collective-permute-start.30) | collective-permute-done | bytes 127008 | tf_op jit(solution)/shard_map/ppermute | solution.py:306
  102.2 4.2 %shard_map.90 = (f32[64,512]{1,0:T(8,128)S(1)}, f32[64,512]{1,0:T(8,128)S(1)}, f32[64,512]{1,0:T(8,128)S(1)}, f32[64,512]{1,0:T(8,128)S(1)}, f32[64,512]{1,0:T(8...) custom-call(s32[4]{0:T(128)S(1)} %pad_add_fusion.place, ...), custom_call_target="tpu_custom_call" | custom-call | flops 2717908992 | bytes 8000000 | tf_op jit(solution)/shard_map/pallas_call | solution.py:294
  108.4 2.5 %collective-permute-start.34 = (f32[64,512]{1,0:T(8,128)S(1)}, f32[64,512]{1,0:T(8,128)S(1)}, u32[]{:S(2)}, u32[]{:S(2)}) collective-permute-start(f32[64,512]{1,0:T(8,128)S(1)} %get-tuple-element.147), channel_id=1, source_target_pairs={{0,6},{1,7},{2,4},{3,5},{4,10},{5,11},{6,8},{7,9},{8,14},{9,15},{1... | collective-permute-start | bytes 393224 | tf_op jit(solution)/shard_map/ppermute | solution.py:340
  110.9 2.6 %collective-permute-start.35 = (f32[64,512]{1,0:T(8,128)S(1)}, f32[64,512]{1,0:T(8,128)S(1)}, u32[]{:S(2)}, u32[]{:S(2)}) collective-permute-start(f32[64,512]{1,0:T(8,128)S(1)} %get-tuple-element.148), channel_id=1, source_target_pairs={{0,14},{1,15},{2,12},{3,13},{4,2},{5,3},{6,0},{7,1},{8,6},{9,7},{1... | collective-permute-start | bytes 393224 | tf_op jit(solution)/shard_map/ppermute | solution.py:340
  113.5 2.4 %collective-permute-start.37 = (f32[64,512]{1,0:T(8,128)S(1)}, f32[64,512]{1,0:T(8,128)S(1)}, u32[]{:S(2)}, u32[]{:S(2)}) collective-permute-start(f32[64,512]{1,0:T(8,128)S(1)} %get-tuple-element.150), channel_id=1, source_target_pairs={{0,2},{1,3},{2,0},{3,1},{4,6},{5,7},{6,4},{7,5},{8,10},{9,11},{10,... | collective-permute-start | bytes 393224 | tf_op jit(solution)/shard_map/ppermute | solution.py:340
  (86 shorter events, 47.1 us)
Async XLA Ops:
  0.1 25.4 %collective-permute-start.1 = (f32[27,32,512]{2,1,0:T(8,128)}, f32[27,32,512]{2,1,0:T(8,128)S(1)}, u32[]{:S(2)}, u32[]{:S(2)}) collective-permute-start(f32[27,32,512]{2,1,0:T(8,128)} %own.3), channel_id=1, source_target_pairs={{0,1},{1,0},{2,3},{3,2},{4,5},{5,4},{6,7},{7,6},{8,9},{9,8},{10,11... | collective-permute-start | bytes 5308424 | tf_op jit(solution)/shard_map/ppermute | solution.py:302
  7.9 12.1 %collective-permute-start.9 = (f32[192,128]{1,0:T(8,128)S(1)}, f32[192,128]{1,0:T(8,128)S(1)}, u32[]{:S(2)}, u32[]{:S(2)}) collective-permute-start(f32[192,128]{1,0:T(8,128)S(1)} %get-tuple-element.87.rest_7_), channel_id=1, source_target_pairs={{0,128},{16,144},{32,160},{48,176},{64,192},{80,208},{96,224},{112... | collective-permute-start | bytes 294920 | tf_op jit(solution)/shard_map/ppermute | solution.py:317
  13.1 12.4 %collective-permute-start.8 = (f32[192,128]{1,0:T(8,128)S(1)}, f32[192,128]{1,0:T(8,128)S(1)}, u32[]{:S(2)}, u32[]{:S(2)}) collective-permute-start(f32[192,128]{1,0:T(8,128)S(1)} %get-tuple-element.87.rest_7_), channel_id=1, source_target_pairs={{0,96},{16,112},{32,128},{48,144},{64,160},{80,176},{96,192},{112,... | collective-permute-start | bytes 294920 | tf_op jit(solution)/shard_map/ppermute | solution.py:317
  16.0 14.8 %collective-permute-start.7 = (f32[192,128]{1,0:T(8,128)S(1)}, f32[192,128]{1,0:T(8,128)S(1)}, u32[]{:S(2)}, u32[]{:S(2)}) collective-permute-start(f32[192,128]{1,0:T(8,128)S(1)} %get-tuple-element.87.rest_7_), channel_id=1, source_target_pairs={{0,160},{16,176},{32,192},{48,208},{64,224},{80,240},{96,0},{112,1... | collective-permute-start | bytes 294920 | tf_op jit(solution)/shard_map/ppermute | solution.py:317
  18.8 12.0 %collective-permute-start.6 = (f32[192,128]{1,0:T(8,128)S(1)}, f32[192,128]{1,0:T(8,128)S(1)}, u32[]{:S(2)}, u32[]{:S(2)}) collective-permute-start(f32[192,128]{1,0:T(8,128)S(1)} %get-tuple-element.87.rest_7_), channel_id=1, source_target_pairs={{0,64},{16,80},{32,96},{48,112},{64,128},{80,144},{96,160},{112,17... | collective-permute-start | bytes 294920 | tf_op jit(solution)/shard_map/ppermute | solution.py:317
  20.0 10.8 %collective-permute-start.5 = (f32[192,128]{1,0:T(8,128)S(1)}, f32[192,128]{1,0:T(8,128)S(1)}, u32[]{:S(2)}, u32[]{:S(2)}) collective-permute-start(f32[192,128]{1,0:T(8,128)S(1)} %get-tuple-element.87.rest_7_), channel_id=1, source_target_pairs={{0,192},{16,208},{32,224},{48,240},{64,0},{80,16},{96,32},{112,48}... | collective-permute-start | bytes 294920 | tf_op jit(solution)/shard_map/ppermute | solution.py:317
  47.8 10.8 %collective-permute-start.15 = (f32[64,512]{1,0:T(8,128)S(1)}, f32[64,512]{1,0:T(8,128)S(1)}, u32[]{:S(2)}, u32[]{:S(2)}) collective-permute-start(f32[64,512]{1,0:T(8,128)S(1)} %get-tuple-element.117), channel_id=1, source_target_pairs={{0,10},{1,11},{2,8},{3,9},{4,14},{5,15},{6,12},{7,13},{8,2},{9,3},... | collective-permute-start | bytes 393224 | tf_op jit(solution)/shard_map/ppermute | solution.py:340
  52.8 8.2 %collective-permute-start.16 = (f32[64,512]{1,0:T(8,128)S(1)}, f32[64,512]{1,0:T(8,128)S(1)}, u32[]{:S(2)}, u32[]{:S(2)}) collective-permute-start(f32[64,512]{1,0:T(8,128)S(1)} %get-tuple-element.118), channel_id=1, source_target_pairs={{0,6},{1,7},{2,4},{3,5},{4,10},{5,11},{6,8},{7,9},{8,14},{9,15},{1... | collective-permute-start | bytes 393224 | tf_op jit(solution)/shard_map/ppermute | solution.py:340
  53.6 9.0 %collective-permute-start.17 = (f32[64,512]{1,0:T(8,128)S(1)}, f32[64,512]{1,0:T(8,128)S(1)}, u32[]{:S(2)}, u32[]{:S(2)}) collective-permute-start(f32[64,512]{1,0:T(8,128)S(1)} %get-tuple-element.119), channel_id=1, source_target_pairs={{0,14},{1,15},{2,12},{3,13},{4,2},{5,3},{6,0},{7,1},{8,6},{9,7},{1... | collective-permute-start | bytes 393224 | tf_op jit(solution)/shard_map/ppermute | solution.py:340
  57.9 7.3 %collective-permute-start.19 = (f32[64,512]{1,0:T(8,128)S(1)}, f32[64,512]{1,0:T(8,128)S(1)}, u32[]{:S(2)}, u32[]{:S(2)}) collective-permute-start(f32[64,512]{1,0:T(8,128)S(1)} %get-tuple-element.121), channel_id=1, source_target_pairs={{0,2},{1,3},{2,0},{3,1},{4,6},{5,7},{6,4},{7,5},{8,10},{9,11},{10,... | collective-permute-start | bytes 393224 | tf_op jit(solution)/shard_map/ppermute | solution.py:340
  58.5 9.5 %collective-permute-start.20 = (f32[64,512]{1,0:T(8,128)S(1)}, f32[64,512]{1,0:T(8,128)S(1)}, u32[]{:S(2)}, u32[]{:S(2)}) collective-permute-start(f32[64,512]{1,0:T(8,128)S(1)} %get-tuple-element.122), channel_id=1, source_target_pairs={{0,4},{1,5},{2,6},{3,7},{4,8},{5,9},{6,10},{7,11},{8,12},{9,13},{1... | collective-permute-start | bytes 393224 | tf_op jit(solution)/shard_map/ppermute | solution.py:340
  69.1 11.6 %collective-permute-start.28 = (f32[192,128]{1,0:T(8,128)S(1)}, f32[192,128]{1,0:T(8,128)S(1)}, u32[]{:S(2)}, u32[]{:S(2)}) collective-permute-start(f32[192,128]{1,0:T(8,128)S(1)} %get-tuple-element.125.rest_7_), channel_id=1, source_target_pairs={{0,128},{16,144},{32,160},{48,176},{64,192},{80,208},{96,224},{112... | collective-permute-start | bytes 294920 | tf_op jit(solution)/shard_map/ppermute | solution.py:317
  72.6 14.1 %collective-permute-start.27 = (f32[192,128]{1,0:T(8,128)S(1)}, f32[192,128]{1,0:T(8,128)S(1)}, u32[]{:S(2)}, u32[]{:S(2)}) collective-permute-start(f32[192,128]{1,0:T(8,128)S(1)} %get-tuple-element.125.rest_7_), channel_id=1, source_target_pairs={{0,96},{16,112},{32,128},{48,144},{64,160},{80,176},{96,192},{112,... | collective-permute-start | bytes 294920 | tf_op jit(solution)/shard_map/ppermute | solution.py:317
  73.6 13.1 %collective-permute-start.26 = (f32[192,128]{1,0:T(8,128)S(1)}, f32[192,128]{1,0:T(8,128)S(1)}, u32[]{:S(2)}, u32[]{:S(2)}) collective-permute-start(f32[192,128]{1,0:T(8,128)S(1)} %get-tuple-element.125.rest_7_), channel_id=1, source_target_pairs={{0,160},{16,176},{32,192},{48,208},{64,224},{80,240},{96,0},{112,1... | collective-permute-start | bytes 294920 | tf_op jit(solution)/shard_map/ppermute | solution.py:317
  77.1 10.5 %collective-permute-start.25 = (f32[192,128]{1,0:T(8,128)S(1)}, f32[192,128]{1,0:T(8,128)S(1)}, u32[]{:S(2)}, u32[]{:S(2)}) collective-permute-start(f32[192,128]{1,0:T(8,128)S(1)} %get-tuple-element.125.rest_7_), channel_id=1, source_target_pairs={{0,64},{16,80},{32,96},{48,112},{64,128},{80,144},{96,160},{112,17... | collective-permute-start | bytes 294920 | tf_op jit(solution)/shard_map/ppermute | solution.py:317
  77.6 12.2 %collective-permute-start.24 = (f32[192,128]{1,0:T(8,128)S(1)}, f32[192,128]{1,0:T(8,128)S(1)}, u32[]{:S(2)}, u32[]{:S(2)}) collective-permute-start(f32[192,128]{1,0:T(8,128)S(1)} %get-tuple-element.125.rest_7_), channel_id=1, source_target_pairs={{0,192},{16,208},{32,224},{48,240},{64,0},{80,16},{96,32},{112,48}... | collective-permute-start | bytes 294920 | tf_op jit(solution)/shard_map/ppermute | solution.py:317
  80.7 11.0 %collective-permute-start.23 = (f32[192,128]{1,0:T(8,128)S(1)}, f32[192,128]{1,0:T(8,128)S(1)}, u32[]{:S(2)}, u32[]{:S(2)}) collective-permute-start(f32[192,128]{1,0:T(8,128)S(1)} %get-tuple-element.125.rest_7_), channel_id=1, source_target_pairs={{0,32},{16,48},{32,64},{48,80},{64,96},{80,112},{96,128},{112,144}... | collective-permute-start | bytes 294920 | tf_op jit(solution)/shard_map/ppermute | solution.py:317
  93.8 7.9 %collective-permute-start.30 = (f32[248,128]{1,0:T(8,128)S(1)}, f32[248,128]{1,0:T(8,128)S(1)}, u32[]{:S(2)}, u32[]{:S(2)}) collective-permute-start(f32[248,128]{1,0:T(8,128)S(1)} %get-tuple-element.128), channel_id=1, source_target_pairs={{0,16},{16,0},{32,48},{48,32},{64,80},{80,64},{96,112},{112,96},{1... | collective-permute-start | bytes 380936 | tf_op jit(solution)/shard_map/ppermute | solution.py:306
  106.4 9.6 %collective-permute-start.33 = (f32[64,512]{1,0:T(8,128)S(1)}, f32[64,512]{1,0:T(8,128)S(1)}, u32[]{:S(2)}, u32[]{:S(2)}) collective-permute-start(f32[64,512]{1,0:T(8,128)S(1)} %get-tuple-element.146), channel_id=1, source_target_pairs={{0,10},{1,11},{2,8},{3,9},{4,14},{5,15},{6,12},{7,13},{8,2},{9,3},... | collective-permute-start | bytes 393224 | tf_op jit(solution)/shard_map/ppermute | solution.py:340
  108.4 9.4 %collective-permute-start.34 = (f32[64,512]{1,0:T(8,128)S(1)}, f32[64,512]{1,0:T(8,128)S(1)}, u32[]{:S(2)}, u32[]{:S(2)}) collective-permute-start(f32[64,512]{1,0:T(8,128)S(1)} %get-tuple-element.147), channel_id=1, source_target_pairs={{0,6},{1,7},{2,4},{3,5},{4,10},{5,11},{6,8},{7,9},{8,14},{9,15},{1... | collective-permute-start | bytes 393224 | tf_op jit(solution)/shard_map/ppermute | solution.py:340
  110.9 9.1 %collective-permute-start.35 = (f32[64,512]{1,0:T(8,128)S(1)}, f32[64,512]{1,0:T(8,128)S(1)}, u32[]{:S(2)}, u32[]{:S(2)}) collective-permute-start(f32[64,512]{1,0:T(8,128)S(1)} %get-tuple-element.148), channel_id=1, source_target_pairs={{0,14},{1,15},{2,12},{3,13},{4,2},{5,3},{6,0},{7,1},{8,6},{9,7},{1... | collective-permute-start | bytes 393224 | tf_op jit(solution)/shard_map/ppermute | solution.py:340
  113.5 7.4 %collective-permute-start.36 = (f32[64,512]{1,0:T(8,128)S(1)}, f32[64,512]{1,0:T(8,128)S(1)}, u32[]{:S(2)}, u32[]{:S(2)}) collective-permute-start(f32[64,512]{1,0:T(8,128)S(1)} %get-tuple-element.149), channel_id=1, source_target_pairs={{0,8},{1,9},{2,10},{3,11},{4,12},{5,13},{6,14},{7,15},{8,0},{9,1},... | collective-permute-start | bytes 393224 | tf_op jit(solution)/shard_map/ppermute | solution.py:340
  113.5 9.2 %collective-permute-start.37 = (f32[64,512]{1,0:T(8,128)S(1)}, f32[64,512]{1,0:T(8,128)S(1)}, u32[]{:S(2)}, u32[]{:S(2)}) collective-permute-start(f32[64,512]{1,0:T(8,128)S(1)} %get-tuple-element.150), channel_id=1, source_target_pairs={{0,2},{1,3},{2,0},{3,1},{4,6},{5,7},{6,4},{7,5},{8,10},{9,11},{10,... | collective-permute-start | bytes 393224 | tf_op jit(solution)/shard_map/ppermute | solution.py:340
  116.0 7.8 %collective-permute-start.38 = (f32[64,512]{1,0:T(8,128)S(1)}, f32[64,512]{1,0:T(8,128)S(1)}, u32[]{:S(2)}, u32[]{:S(2)}) collective-permute-start(f32[64,512]{1,0:T(8,128)S(1)} %get-tuple-element.151), channel_id=1, source_target_pairs={{0,4},{1,5},{2,6},{3,7},{4,8},{5,9},{6,10},{7,11},{8,12},{9,13},{1... | collective-permute-start | bytes 393224 | tf_op jit(solution)/shard_map/ppermute | solution.py:340
  (25 other events, 199.6 us)

commit v5 on v4

--- a/solution.py
+++ b/solution.py
@@ -166,7 +166,7 @@
 
 
 RIM_ROWS = 248
-SENT = (-1, 1, -2, 2, -3, 3, 4)
+SENT = (4, 3, -3, 2, -2, 1, -1)
 
 
 def face_rows(offsets):
@@ -181,23 +181,35 @@
     return pl.ds(128, 64)
 
 
-def rims_kernel(place, own_table, other_table, *rest):
+def plan_kernel(place, own_table, other_table, plan):
+    core, low_x, depth = place[0], place[1], place[2]
+    for peer in range(4):
+        table = other_table if peer & 1 else own_table
+        slot = core ^ (peer >> 1)
+        for number in range(26):
+            entry = table[slot, number]
+            here = (entry >= 0) & ((entry & 1) == core) & (((entry >> 1) & 1) == low_x)
+            plan[peer, number] = jnp.where(here, (depth - (entry >> 2)) & 7, -1)
+
+
+def make_plan(place, own_table, other_table):
+    return call(plan_kernel, arr((4, 26), jnp.int32))(in_specs=[SMEM, SMEM, SMEM], out_specs=SMEM)(
+        place, own_table, other_table
+    )
+
+
+def rims_kernel(plan, *rest):
     blocks, outs, gathered = rest[:8], rest[8:12], rest[12]
-    core, low_x, depth = place[0], place[1], place[2]
     for number, step in enumerate(SENT + (0,)):
         gathered[step % 8] = blocks[number][...]
     for peer in range(4):
-        table = other_table if peer & 1 else own_table
-        slot = core ^ (peer >> 1)
         out = outs[peer]
         out[240:248, :] = jnp.zeros((8, 128), F32)
 
         def load(offsets):
-            entry = table[slot, DIRECTIONS.index(offsets)]
-            found = jnp.clip(entry, 0, 31)
-            here = (entry >= 0) & ((found & 1) == core) & (((found >> 1) & 1) == low_x)
-            value = gathered[(depth - (found >> 2)) & 7, face_rows(offsets), :]
-            return jnp.where(here, value, 0.0)
+            index = plan[peer, DIRECTIONS.index(offsets)]
+            value = gathered[jnp.maximum(index, 0), face_rows(offsets), :]
+            return jnp.where(index >= 0, value, 0.0)
 
         for offsets, begin, count in rim_list():
             up, down = load(offsets), load(tuple(-step for step in offsets))
@@ -205,14 +217,14 @@
             out[begin : begin + count, :] = jnp.where(lane < 64, up, down)
 
 
-def cut_rims(place, own_table, other_table, blocks):
+def cut_rims(plan, blocks):
     outs = tuple(close((RIM_ROWS, 128)) for _ in range(4))
     return call(rims_kernel, outs, [pltpu.VMEM((8, 192, 128), F32)], touched=1000000)(
-        in_specs=[SMEM, SMEM, SMEM] + [VMEM] * 8, out_specs=tuple([VMEM] * 4)
-    )(place, own_table, other_table, *near(blocks))
-
-
-def fill_rims(rims, padded):
+        in_specs=[SMEM] + [VMEM] * 8, out_specs=tuple([VMEM] * 4)
+    )(plan, *near(blocks))
+
+
+def fill_rims(rims, padded, columns, after):
     def at(x, y):
         return (x * 10 + y) * ROWS
 
@@ -231,7 +243,14 @@
                     elif b:
                         padded[pl.ds(at(1 + n, py) + 8, 8), :] = piece
                     else:
-                        padded[pl.ds(at(1 + n, 1) + row, 8, stride=ROWS), :] = piece
+                        begins = ((1 + n) * 10 + 1) * 8
+                        if c < 0:
+                            where = pl.ds(begins, 8, stride=8)
+                            lane = lax.broadcasted_iota(jnp.int32, (8, 128), 1)
+                            wide = jnp.concatenate([piece, piece], axis=1)
+                            columns[where, :] = jnp.where(lane < 64, wide, columns[where, :])
+                        else:
+                            after[pl.ds(begins + 7, 8, stride=8), :] = piece
             elif count == 1:
                 padded[pl.ds(at(px, py) + row, 1), :] = value
             elif c == 0:
@@ -242,32 +261,51 @@
                 padded[pl.ds(at(1, py) + row, 8, stride=10 * ROWS), :] = value
 
 
-def conv_kernel(place, rows, *rest):
+def lay_out(padded, begin, columns, after, row):
+    before = padded[pl.ds(begin + 7, 8), :]
+    same = padded[pl.ds(begin + 8, 8), :]
+    columns[row : row + 8, :] = jnp.concatenate([before, same], axis=1)
+    after[row : row + 8, :] = padded[pl.ds(begin + 9, 8), :]
+
+
+def center_kernel(rows, center, center_after, padded):
+    center[...] = jnp.zeros(center.shape, F32)
+    center_after[...] = jnp.zeros(center_after.shape, F32)
+    padded[...] = jnp.zeros(padded.shape, F32)
+    for spot in range(64):
+        padded[pl.ds(spot * ROWS + 8, 8), :] = rows[8 * spot : 8 * spot + 8, :]
+    for spot in range(64):
+        lay_out(padded, spot * ROWS, center, center_after, ((1 + spot // 8) * 10 + 1 + spot % 8) * 8)
+
+
+def make_center(rows):
+    return call(center_kernel, (close((800, 128)), close((800, 64))), [pltpu.VMEM((64 * ROWS, 64), F32)])(
+        in_specs=[VMEM], out_specs=(VMEM, VMEM)
+    )(*near([rows]))
+
+
+def conv_kernel(place, center, center_after, *rest):
     pieces = rest[:4]
     stacked = rest[4]
     outs = rest[5:13]
-    rims, padded, columns, total, turned = rest[13:]
+    rims, padded, columns, after, total, turned = rest[13:]
     rims[...] = (pieces[0][...] + pieces[1][...]) + (pieces[2][...] + pieces[3][...])
-    for x in range(8):
-        for y in range(8):
-            padded[pl.ds(((1 + x) * 10 + 1 + y) * ROWS + 8, 8), :] = rows[pl.ds(x * 64 + y * 8, 8), :]
-    fill_rims(rims, padded)
+    columns[...] = center[...]
+    after[...] = center_after[...]
+    fill_rims(rims, padded, columns, after)
     for spot in range(100):
-        before = padded[pl.ds(spot * ROWS + 7, 8), :]
-        same = padded[pl.ds(spot * ROWS + 8, 8), :]
-        after = padded[pl.ds(spot * ROWS + 9, 8), :]
-        columns[spot // 10, spot % 10, :, 0:128] = jnp.concatenate([before, same], axis=1)
-        columns[spot // 10, spot % 10, :, 128:192] = after
-
+        if spot // 10 in (0, 9) or spot % 10 in (0, 9):
+            lay_out(padded, spot * ROWS, columns, after, spot * 8)
     for p in range(3):
         firsts, pairs, tails = [], [], []
         for q in range(3):
-            values = columns[p : p + 8, q : q + 8, :, 0:192].reshape(512, 192)
-            top = values.astype(BF16).astype(F32)
-            low = values - top
-            firsts += [top[:, 0:128], low[:, 0:128], top[:, 0:128]]
-            pairs.append(jnp.concatenate([top[:, 128:192], low[:, 128:192]], axis=1))
-            tails.append(top[:, 128:192])
+            begins = [((p + x) * 10 + q) * 8 for x in range(8)]
+            values = jnp.concatenate([columns[begin : begin + 64, :] for begin in begins], axis=0)
+            ending = jnp.concatenate([after[begin : begin + 64, :] for begin in begins], axis=0)
+            top, last = values.astype(BF16).astype(F32), ending.astype(BF16).astype(F32)
+            firsts += [top, values - top, top]
+            pairs.append(jnp.concatenate([last, ending - last], axis=1))
+            tails.append(last)
         ends = [jnp.concatenate(tails[:2], axis=1), tails[2]]
         left = jnp.concatenate([piece.astype(BF16) for piece in firsts + pairs + ends], axis=1)
         sums = jnp.dot(left, stacked[p], preferred_element_type=F32)
@@ -282,20 +320,21 @@
         outs[step][...] = turned[pl.ds(pl.multiple_of(target * 64, 64), 64), :]
 
 
-def conv(place, rows, rims, stacked):
+def conv(place, center, rims, stacked):
     outs = tuple(close((64, 512)) for _ in range(8))
     scratch = [
         pltpu.VMEM((RIM_ROWS, 128), F32),
         pltpu.VMEM((100 * ROWS, 64), F32),
-        pltpu.VMEM((10, 10, 8, 256), F32),
+        pltpu.VMEM((800, 128), F32),
+        pltpu.VMEM((800, 64), F32),
         pltpu.VMEM((512, 512), F32),
         pltpu.VMEM((512, 512), F32),
     ]
     return call(
         conv_kernel, outs, scratch, flops=2 * 3 * 1024 * 1728 * 256, touched=8000000, room=24
     )(
-        in_specs=[SMEM] + [VMEM] * 6, out_specs=tuple([VMEM] * 8)
-    )(place, *near([rows, *rims, stacked]))
+        in_specs=[SMEM] + [VMEM] * 7, out_specs=tuple([VMEM] * 8)
+    )(place, *near([*center, *rims, stacked]))
 
 
 def to_other_core(value):
@@ -311,19 +350,18 @@
     return lax.ppermute(value, ("leaf", "chan"), pairs)
 
 
-def gather_rims(place, tables, faces, weights=None):
+def gather_rims(plan, faces, ready):
     found = []
     for step in SENT:
         found.append(lax.ppermute(faces, "leaf", [(i, (i + 2 * step) % 16) for i in range(16)]))
-    if weights is not None:
-        found, weights = lax.optimization_barrier((found, weights))
-    own, beside, across, both = cut_rims(place, *tables, found + [faces])
-    return [own, to_other_both(both), to_other_x(beside), to_other_core(across)], weights
-
-
-def conv_beside(place, rows, rims, weights, moved):
+    found, ready, plan = lax.optimization_barrier((found, ready, plan))
+    own, beside, across, both = cut_rims(plan, found + [faces])
+    return [own, to_other_both(both), to_other_x(beside), to_other_core(across)], ready
+
+
+def conv_beside(place, center, rims, weights, moved):
     rims, moved = lax.optimization_barrier((rims, moved))
-    parts = conv(place, rows, rims, weights)
+    parts = conv(place, center, rims, weights)
     return lax.optimization_barrier((parts, [to_other_core(value) for value in moved]))
 
 
@@ -358,16 +396,17 @@
     swapped, tables = lax.optimization_barrier((to_other_core(weight_in), tables))
     weights = split_weights(place, weight_in, swapped)
 
-    rims, weights = gather_rims(place, tables, faces, weights)
-    parts, (swapped, other_bias) = conv_beside(place, rows, rims, weights, [weight_out, bias_in])
+    plan = make_plan(place, *tables)
+    rims, (weights, center) = gather_rims(plan, faces, (weights, make_center(rows)))
+    parts, (swapped, other_bias) = conv_beside(place, center, rims, weights, [weight_out, bias_in])
     weights = split_weights(place, weight_out, swapped)
     parts = add_over_chips(parts)
     rows, faces = call(hidden_kernel, (close((512, 64)), close((192, 128))))(
         in_specs=[SMEM, SMEM] + [VMEM] * 11, out_specs=(VMEM, VMEM)
     )(place, leaf_counts, occupancy, bias_in, other_bias, *near(parts))
 
-    rims, _ = gather_rims(place, tables, faces)
-    parts, (other_bias,) = conv_beside(place, rows, rims, weights, [bias_out])
+    rims, center = gather_rims(plan, faces, make_center(rows))
+    parts, (other_bias,) = conv_beside(place, center, rims, weights, [bias_out])
     parts = add_over_chips(parts)
     keep, give = call(result_kernel, (close((32, 512)), close((32, 512))))(
         in_specs=[SMEM, SMEM] + [VMEM] * 11, out_specs=(VMEM, VMEM)

time: 128 us -> 128 us (level)
  waiting for transfers between devices: 45.1 us -> 41.3 us
  starting transfers between devices: 61.1 us -> 63.6 us
    ppermute x14, waiting for transfers between devices: 15.9 us -> 12.4 us  [gather_rims(): lax.ppermute(faces, 'leaf', [(i, (i + 2 * step) % 16) for i in range(16)])]
    ppermute x14, starting transfers between devices: 27.6 us -> 29.9 us  [gather_rims(): lax.ppermute(faces, 'leaf', [(i, (i + 2 * step) % 16) for i in range(16)])]
    pallas_call x0 -> x3, Pallas kernels: none -> 2.07 us  [the longest x1 1.62 us: make_plan(): call(plan_kernel, arr((4, 26), jnp.int32))]
  transfers between devices with their start and end apart: 41 -> 41, of which waited for: 22 -> 21; matrix products, arithmetic and copies ran while one was open for 0% -> 0% of each run, Pallas kernels for 9% -> 11%
where the time goes in v5:
time: 128 us
  starting transfers between devices  63.6 us (50%)
  waiting for transfers between devices  41.3 us (32%)
  Pallas kernels  18.6 us (15%)
  local copies, waits for them, and re-layouts  3.74 us (3%)
    ppermute x14, starting transfers between devices, gather_rims(): lax.ppermute(faces, 'leaf', [(i, (i + 2 * step) % 16) for i in range(16)])  29.9 us
    ppermute x14, starting transfers between devices, add_over_chips(): lax.ppermute(part, 'chan', [(i, route_target(i, route)) for i in range(16)])  21.9 us
    ppermute x14, waiting for transfers between devices, add_over_chips(): lax.ppermute(part, 'chan', [(i, route_target(i, route)) for i in range(16)])  16 us
    ppermute x14, waiting for transfers between devices, gather_rims(): lax.ppermute(faces, 'leaf', [(i, (i + 2 * step) % 16) for i in range(16)])  12.4 us
    pallas_call x2, Pallas kernels, conv(): call(conv_kernel, outs, scratch, flops=2 * 3 * 1024 * 1728 * 256, touched...  8.14 us
    ppermute x8, starting transfers between devices, to_other_core(): return lax.ppermute(value, 'chan', [(i, i ^ 1) for i in range(16)])  5.97 us
    ppermute x2, waiting for transfers between devices, to_other_both(): return lax.ppermute(value, ('leaf', 'chan'), pairs)  5.77 us
    ppermute x3, waiting for transfers between devices, to_other_x(): return lax.ppermute(value, 'leaf', [(i, i ^ 1) for i in range(16)])  5.35 us
  transfers between devices with their start and end apart: 41, of which 21 were waited for; matrix products, arithmetic and copies ran while one was open for 0% of the time, Pallas kernels for 11%

profile of v5, /device:TPU:1, one launch (start us, length us, event | category | flops | bytes accessed | tf_op | source)
XLA Modules:
  0.0 128.2 jit_solution(11228640894962685425)
XLA Ops:
  0.1 3.3 %collective-permute-start.8 = (f32[27,32,512]{2,1,0:T(8,128)}, f32[27,32,512]{2,1,0:T(8,128)S(1)}, u32[]{:S(2)}, u32[]{:S(2)}) collective-permute-start(f32[27,32,512]{2,1,0:T(8,128)} %own.3), channel_id=1, source_target_pairs={{0,1},{1,0},{2,3},{3,2},{4,5},{5,4},{6,7},{7,6},{8,9},{9,8},{10,11... | collective-permute-start | bytes 5308424 | tf_op jit(solution)/shard_map/ppermute | solution.py:341
  7.9 5.3 %collective-permute-start.1 = (f32[192,128]{1,0:T(8,128)S(1)}, f32[192,128]{1,0:T(8,128)S(1)}, u32[]{:S(2)}, u32[]{:S(2)}) collective-permute-start(f32[192,128]{1,0:T(8,128)S(1)} %get-tuple-element.100.rest_7_), channel_id=1, source_target_pairs={{0,128},{16,144},{32,160},{48,176},{64,192},{80,208},{96,224},{112... | collective-permute-start | bytes 294920 | tf_op jit(solution)/shard_map/ppermute | solution.py:356
  16.0 2.8 %collective-permute-start.3 = (f32[192,128]{1,0:T(8,128)S(1)}, f32[192,128]{1,0:T(8,128)S(1)}, u32[]{:S(2)}, u32[]{:S(2)}) collective-permute-start(f32[192,128]{1,0:T(8,128)S(1)} %get-tuple-element.100.rest_7_), channel_id=1, source_target_pairs={{0,160},{16,176},{32,192},{48,208},{64,224},{80,240},{96,0},{112,1... | collective-permute-start | bytes 294920 | tf_op jit(solution)/shard_map/ppermute | solution.py:356
  20.0 2.4 %collective-permute-start.5 = (f32[192,128]{1,0:T(8,128)S(1)}, f32[192,128]{1,0:T(8,128)S(1)}, u32[]{:S(2)}, u32[]{:S(2)}) collective-permute-start(f32[192,128]{1,0:T(8,128)S(1)} %get-tuple-element.100.rest_7_), channel_id=1, source_target_pairs={{0,192},{16,208},{32,224},{48,240},{64,0},{80,16},{96,32},{112,48}... | collective-permute-start | bytes 294920 | tf_op jit(solution)/shard_map/ppermute | solution.py:356
  22.4 3.1 %collective-permute-done.2.rest_1_ = f32[192,128]{1,0:T(8,128)S(1)} collective-permute-done((f32[192,128]{1,0:T(8,128)S(1)}, f32[192,128]{1,0:T(8,128)S(1)}, u32[]{:S(2)}, u32[]{:S(2)}) %collective-permute-start.2) | collective-permute-done | bytes 98336 | tf_op jit(solution)/shard_map/ppermute | solution.py:356
  25.5 2.7 %collective-permute-start.7 = (f32[192,128]{1,0:T(8,128)S(1)}, f32[192,128]{1,0:T(8,128)S(1)}, u32[]{:S(2)}, u32[]{:S(2)}) collective-permute-start(f32[192,128]{1,0:T(8,128)S(1)} %get-tuple-element.100.rest_7_), channel_id=1, source_target_pairs={{0,224},{16,240},{32,0},{48,16},{64,32},{80,48},{96,64},{112,80},{... | collective-permute-start | bytes 294920 | tf_op jit(solution)/shard_map/ppermute | solution.py:356
  36.9 3.3 %collective-permute-done.10.rest_1_ = f32[248,128]{1,0:T(8,128)S(1)} collective-permute-done((f32[248,128]{1,0:T(8,128)S(1)}, f32[248,128]{1,0:T(8,128)S(1)}, u32[]{:S(2)}, u32[]{:S(2)}) %collective-permute-start.10) | collective-permute-done | bytes 127008 | tf_op jit(solution)/shard_map/ppermute | solution.py:350
  40.3 2.7 %collective-permute-done.11.rest_2_ = f32[248,128]{1,0:T(8,128)S(1)} collective-permute-done((f32[248,128]{1,0:T(8,128)S(1)}, f32[248,128]{1,0:T(8,128)S(1)}, u32[]{:S(2)}, u32[]{:S(2)}) %collective-permute-start.11) | collective-permute-done | bytes 127008 | tf_op jit(solution)/shard_map/ppermute | solution.py:345
  43.8 4.1 %shard_map.88 = (f32[64,512]{1,0:T(8,128)S(1)}, f32[64,512]{1,0:T(8,128)S(1)}, f32[64,512]{1,0:T(8,128)S(1)}, f32[64,512]{1,0:T(8,128)S(1)}, f32[64,512]{1,0:T(8...) custom-call(s32[4]{0:T(128)S(1)} %pad_add_fusion.place, ...), custom_call_target="tpu_custom_call" | custom-call | flops 2717908992 | bytes 8000000 | tf_op jit(solution)/shard_map/pallas_call | solution.py:333
  47.9 5.2 %collective-permute-start.15 = (f32[64,512]{1,0:T(8,128)S(1)}, f32[64,512]{1,0:T(8,128)S(1)}, u32[]{:S(2)}, u32[]{:S(2)}) collective-permute-start(f32[64,512]{1,0:T(8,128)S(1)} %get-tuple-element.139), channel_id=1, source_target_pairs={{0,10},{1,11},{2,8},{3,9},{4,14},{5,15},{6,12},{7,13},{8,2},{9,3},... | collective-permute-start | bytes 393224 | tf_op jit(solution)/shard_map/ppermute | solution.py:378
  53.9 4.3 %collective-permute-start.17 = (f32[64,512]{1,0:T(8,128)S(1)}, f32[64,512]{1,0:T(8,128)S(1)}, u32[]{:S(2)}, u32[]{:S(2)}) collective-permute-start(f32[64,512]{1,0:T(8,128)S(1)} %get-tuple-element.141), channel_id=1, source_target_pairs={{0,14},{1,15},{2,12},{3,13},{4,2},{5,3},{6,0},{7,1},{8,6},{9,7},{1... | collective-permute-start | bytes 393224 | tf_op jit(solution)/shard_map/ppermute | solution.py:378
  59.0 2.2 %collective-permute-done.16.rest_2_ = f32[64,512]{1,0:T(8,128)S(1)} collective-permute-done((f32[64,512]{1,0:T(8,128)S(1)}, f32[64,512]{1,0:T(8,128)S(1)}, u32[]{:S(2)}, u32[]{:S(2)}) %collective-permute-start.16) | collective-permute-done | bytes 131104 | tf_op jit(solution)/shard_map/ppermute | solution.py:378
  65.5 2.8 %collective-permute-done.20.rest_6_ = f32[64,512]{1,0:T(8,128)S(1)} collective-permute-done((f32[64,512]{1,0:T(8,128)S(1)}, f32[64,512]{1,0:T(8,128)S(1)}, u32[]{:S(2)}, u32[]{:S(2)}) %collective-permute-start.20) | collective-permute-done | bytes 131104 | tf_op jit(solution)/shard_map/ppermute | solution.py:378
  69.3 5.4 %collective-permute-start.22 = (f32[192,128]{1,0:T(8,128)S(1)}, f32[192,128]{1,0:T(8,128)S(1)}, u32[]{:S(2)}, u32[]{:S(2)}) collective-permute-start(f32[192,128]{1,0:T(8,128)S(1)} %get-tuple-element.146.rest_7_), channel_id=1, source_target_pairs={{0,128},{16,144},{32,160},{48,176},{64,192},{80,208},{96,224},{112... | collective-permute-start | bytes 294920 | tf_op jit(solution)/shard_map/ppermute | solution.py:356
  74.8 4.5 %collective-permute-start.24 = (f32[192,128]{1,0:T(8,128)S(1)}, f32[192,128]{1,0:T(8,128)S(1)}, u32[]{:S(2)}, u32[]{:S(2)}) collective-permute-start(f32[192,128]{1,0:T(8,128)S(1)} %get-tuple-element.146.rest_7_), channel_id=1, source_target_pairs={{0,160},{16,176},{32,192},{48,208},{64,224},{80,240},{96,0},{112,1... | collective-permute-start | bytes 294920 | tf_op jit(solution)/shard_map/ppermute | solution.py:356
  79.2 3.6 %collective-permute-start.26 = (f32[192,128]{1,0:T(8,128)S(1)}, f32[192,128]{1,0:T(8,128)S(1)}, u32[]{:S(2)}, u32[]{:S(2)}) collective-permute-start(f32[192,128]{1,0:T(8,128)S(1)} %get-tuple-element.146.rest_7_), channel_id=1, source_target_pairs={{0,192},{16,208},{32,224},{48,240},{64,0},{80,16},{96,32},{112,48}... | collective-permute-start | bytes 294920 | tf_op jit(solution)/shard_map/ppermute | solution.py:356
  82.8 2.2 %collective-permute-done.23.rest_1_ = f32[192,128]{1,0:T(8,128)S(1)} collective-permute-done((f32[192,128]{1,0:T(8,128)S(1)}, f32[192,128]{1,0:T(8,128)S(1)}, u32[]{:S(2)}, u32[]{:S(2)}) %collective-permute-start.23) | collective-permute-done | bytes 98336 | tf_op jit(solution)/shard_map/ppermute | solution.py:356
  85.7 4.1 %collective-permute-done.25.rest_3_ = f32[192,128]{1,0:T(8,128)S(1)} collective-permute-done((f32[192,128]{1,0:T(8,128)S(1)}, f32[192,128]{1,0:T(8,128)S(1)}, u32[]{:S(2)}, u32[]{:S(2)}) %collective-permute-start.25) | collective-permute-done | bytes 98336 | tf_op jit(solution)/shard_map/ppermute | solution.py:356
  89.9 2.9 %collective-permute-done.27.rest_5_ = f32[192,128]{1,0:T(8,128)S(1)} collective-permute-done((f32[192,128]{1,0:T(8,128)S(1)}, f32[192,128]{1,0:T(8,128)S(1)}, u32[]{:S(2)}, u32[]{:S(2)}) %collective-permute-start.27) | collective-permute-done | bytes 98336 | tf_op jit(solution)/shard_map/ppermute | solution.py:356
  97.0 2.4 %collective-permute-done.29.rest_1_ = f32[248,128]{1,0:T(8,128)S(1)} collective-permute-done((f32[248,128]{1,0:T(8,128)S(1)}, f32[248,128]{1,0:T(8,128)S(1)}, u32[]{:S(2)}, u32[]{:S(2)}) %collective-permute-start.29) | collective-permute-done | bytes 127008 | tf_op jit(solution)/shard_map/ppermute | solution.py:350
  99.5 2.6 %collective-permute-done.30.rest_2_ = f32[248,128]{1,0:T(8,128)S(1)} collective-permute-done((f32[248,128]{1,0:T(8,128)S(1)}, f32[248,128]{1,0:T(8,128)S(1)}, u32[]{:S(2)}, u32[]{:S(2)}) %collective-permute-start.30) | collective-permute-done | bytes 127008 | tf_op jit(solution)/shard_map/ppermute | solution.py:345
  102.7 4.1 %shard_map.93 = (f32[64,512]{1,0:T(8,128)S(1)}, f32[64,512]{1,0:T(8,128)S(1)}, f32[64,512]{1,0:T(8,128)S(1)}, f32[64,512]{1,0:T(8,128)S(1)}, f32[64,512]{1,0:T(8...) custom-call(s32[4]{0:T(128)S(1)} %pad_add_fusion.place, ...), custom_call_target="tpu_custom_call" | custom-call | flops 2717908992 | bytes 8000000 | tf_op jit(solution)/shard_map/pallas_call | solution.py:333
  111.1 2.9 %collective-permute-start.35 = (f32[64,512]{1,0:T(8,128)S(1)}, f32[64,512]{1,0:T(8,128)S(1)}, u32[]{:S(2)}, u32[]{:S(2)}) collective-permute-start(f32[64,512]{1,0:T(8,128)S(1)} %get-tuple-element.182), channel_id=1, source_target_pairs={{0,14},{1,15},{2,12},{3,13},{4,2},{5,3},{6,0},{7,1},{8,6},{9,7},{1... | collective-permute-start | bytes 393224 | tf_op jit(solution)/shard_map/ppermute | solution.py:378
  114.1 2.4 %collective-permute-start.37 = (f32[64,512]{1,0:T(8,128)S(1)}, f32[64,512]{1,0:T(8,128)S(1)}, u32[]{:S(2)}, u32[]{:S(2)}) collective-permute-start(f32[64,512]{1,0:T(8,128)S(1)} %get-tuple-element.184), channel_id=1, source_target_pairs={{0,2},{1,3},{2,0},{3,1},{4,6},{5,7},{6,4},{7,5},{8,10},{9,11},{10,... | collective-permute-start | bytes 393224 | tf_op jit(solution)/shard_map/ppermute | solution.py:378
  (89 shorter events, 46.1 us)
Async XLA Ops:
  0.1 25.4 %collective-permute-start.8 = (f32[27,32,512]{2,1,0:T(8,128)}, f32[27,32,512]{2,1,0:T(8,128)S(1)}, u32[]{:S(2)}, u32[]{:S(2)}) collective-permute-start(f32[27,32,512]{2,1,0:T(8,128)} %own.3), channel_id=1, source_target_pairs={{0,1},{1,0},{2,3},{3,2},{4,5},{5,4},{6,7},{7,6},{8,9},{9,8},{10,11... | collective-permute-start | bytes 5308424 | tf_op jit(solution)/shard_map/ppermute | solution.py:341
  7.9 12.1 %collective-permute-start.1 = (f32[192,128]{1,0:T(8,128)S(1)}, f32[192,128]{1,0:T(8,128)S(1)}, u32[]{:S(2)}, u32[]{:S(2)}) collective-permute-start(f32[192,128]{1,0:T(8,128)S(1)} %get-tuple-element.100.rest_7_), channel_id=1, source_target_pairs={{0,128},{16,144},{32,160},{48,176},{64,192},{80,208},{96,224},{112... | collective-permute-start | bytes 294920 | tf_op jit(solution)/shard_map/ppermute | solution.py:356
  13.1 12.4 %collective-permute-start.2 = (f32[192,128]{1,0:T(8,128)S(1)}, f32[192,128]{1,0:T(8,128)S(1)}, u32[]{:S(2)}, u32[]{:S(2)}) collective-permute-start(f32[192,128]{1,0:T(8,128)S(1)} %get-tuple-element.100.rest_7_), channel_id=1, source_target_pairs={{0,96},{16,112},{32,128},{48,144},{64,160},{80,176},{96,192},{112,... | collective-permute-start | bytes 294920 | tf_op jit(solution)/shard_map/ppermute | solution.py:356
  16.0 17.3 %collective-permute-start.3 = (f32[192,128]{1,0:T(8,128)S(1)}, f32[192,128]{1,0:T(8,128)S(1)}, u32[]{:S(2)}, u32[]{:S(2)}) collective-permute-start(f32[192,128]{1,0:T(8,128)S(1)} %get-tuple-element.100.rest_7_), channel_id=1, source_target_pairs={{0,160},{16,176},{32,192},{48,208},{64,224},{80,240},{96,0},{112,1... | collective-permute-start | bytes 294920 | tf_op jit(solution)/shard_map/ppermute | solution.py:356
  18.8 14.5 %collective-permute-start.4 = (f32[192,128]{1,0:T(8,128)S(1)}, f32[192,128]{1,0:T(8,128)S(1)}, u32[]{:S(2)}, u32[]{:S(2)}) collective-permute-start(f32[192,128]{1,0:T(8,128)S(1)} %get-tuple-element.100.rest_7_), channel_id=1, source_target_pairs={{0,64},{16,80},{32,96},{48,112},{64,128},{80,144},{96,160},{112,17... | collective-permute-start | bytes 294920 | tf_op jit(solution)/shard_map/ppermute | solution.py:356
  20.0 13.3 %collective-permute-start.5 = (f32[192,128]{1,0:T(8,128)S(1)}, f32[192,128]{1,0:T(8,128)S(1)}, u32[]{:S(2)}, u32[]{:S(2)}) collective-permute-start(f32[192,128]{1,0:T(8,128)S(1)} %get-tuple-element.100.rest_7_), channel_id=1, source_target_pairs={{0,192},{16,208},{32,224},{48,240},{64,0},{80,16},{96,32},{112,48}... | collective-permute-start | bytes 294920 | tf_op jit(solution)/shard_map/ppermute | solution.py:356
  25.5 7.9 %collective-permute-start.6 = (f32[192,128]{1,0:T(8,128)S(1)}, f32[192,128]{1,0:T(8,128)S(1)}, u32[]{:S(2)}, u32[]{:S(2)}) collective-permute-start(f32[192,128]{1,0:T(8,128)S(1)} %get-tuple-element.100.rest_7_), channel_id=1, source_target_pairs={{0,32},{16,48},{32,64},{48,80},{64,96},{80,112},{96,128},{112,144}... | collective-permute-start | bytes 294920 | tf_op jit(solution)/shard_map/ppermute | solution.py:356
  25.5 7.9 %collective-permute-start.7 = (f32[192,128]{1,0:T(8,128)S(1)}, f32[192,128]{1,0:T(8,128)S(1)}, u32[]{:S(2)}, u32[]{:S(2)}) collective-permute-start(f32[192,128]{1,0:T(8,128)S(1)} %get-tuple-element.100.rest_7_), channel_id=1, source_target_pairs={{0,224},{16,240},{32,0},{48,16},{64,32},{80,48},{96,64},{112,80},{... | collective-permute-start | bytes 294920 | tf_op jit(solution)/shard_map/ppermute | solution.py:356
  47.9 11.0 %collective-permute-start.15 = (f32[64,512]{1,0:T(8,128)S(1)}, f32[64,512]{1,0:T(8,128)S(1)}, u32[]{:S(2)}, u32[]{:S(2)}) collective-permute-start(f32[64,512]{1,0:T(8,128)S(1)} %get-tuple-element.139), channel_id=1, source_target_pairs={{0,10},{1,11},{2,8},{3,9},{4,14},{5,15},{6,12},{7,13},{8,2},{9,3},... | collective-permute-start | bytes 393224 | tf_op jit(solution)/shard_map/ppermute | solution.py:378
  53.1 8.2 %collective-permute-start.16 = (f32[64,512]{1,0:T(8,128)S(1)}, f32[64,512]{1,0:T(8,128)S(1)}, u32[]{:S(2)}, u32[]{:S(2)}) collective-permute-start(f32[64,512]{1,0:T(8,128)S(1)} %get-tuple-element.140), channel_id=1, source_target_pairs={{0,6},{1,7},{2,4},{3,5},{4,10},{5,11},{6,8},{7,9},{8,14},{9,15},{1... | collective-permute-start | bytes 393224 | tf_op jit(solution)/shard_map/ppermute | solution.py:378
  53.9 9.0 %collective-permute-start.17 = (f32[64,512]{1,0:T(8,128)S(1)}, f32[64,512]{1,0:T(8,128)S(1)}, u32[]{:S(2)}, u32[]{:S(2)}) collective-permute-start(f32[64,512]{1,0:T(8,128)S(1)} %get-tuple-element.141), channel_id=1, source_target_pairs={{0,14},{1,15},{2,12},{3,13},{4,2},{5,3},{6,0},{7,1},{8,6},{9,7},{1... | collective-permute-start | bytes 393224 | tf_op jit(solution)/shard_map/ppermute | solution.py:378
  58.9 9.4 %collective-permute-start.20 = (f32[64,512]{1,0:T(8,128)S(1)}, f32[64,512]{1,0:T(8,128)S(1)}, u32[]{:S(2)}, u32[]{:S(2)}) collective-permute-start(f32[64,512]{1,0:T(8,128)S(1)} %get-tuple-element.144), channel_id=1, source_target_pairs={{0,4},{1,5},{2,6},{3,7},{4,8},{5,9},{6,10},{7,11},{8,12},{9,13},{1... | collective-permute-start | bytes 393224 | tf_op jit(solution)/shard_map/ppermute | solution.py:378
  69.3 13.5 %collective-permute-start.22 = (f32[192,128]{1,0:T(8,128)S(1)}, f32[192,128]{1,0:T(8,128)S(1)}, u32[]{:S(2)}, u32[]{:S(2)}) collective-permute-start(f32[192,128]{1,0:T(8,128)S(1)} %get-tuple-element.146.rest_7_), channel_id=1, source_target_pairs={{0,128},{16,144},{32,160},{48,176},{64,192},{80,208},{96,224},{112... | collective-permute-start | bytes 294920 | tf_op jit(solution)/shard_map/ppermute | solution.py:356
  74.7 10.3 %collective-permute-start.23 = (f32[192,128]{1,0:T(8,128)S(1)}, f32[192,128]{1,0:T(8,128)S(1)}, u32[]{:S(2)}, u32[]{:S(2)}) collective-permute-start(f32[192,128]{1,0:T(8,128)S(1)} %get-tuple-element.146.rest_7_), channel_id=1, source_target_pairs={{0,96},{16,112},{32,128},{48,144},{64,160},{80,176},{96,192},{112,... | collective-permute-start | bytes 294920 | tf_op jit(solution)/shard_map/ppermute | solution.py:356
  74.8 11.0 %collective-permute-start.24 = (f32[192,128]{1,0:T(8,128)S(1)}, f32[192,128]{1,0:T(8,128)S(1)}, u32[]{:S(2)}, u32[]{:S(2)}) collective-permute-start(f32[192,128]{1,0:T(8,128)S(1)} %get-tuple-element.146.rest_7_), channel_id=1, source_target_pairs={{0,160},{16,176},{32,192},{48,208},{64,224},{80,240},{96,0},{112,1... | collective-permute-start | bytes 294920 | tf_op jit(solution)/shard_map/ppermute | solution.py:356
  79.2 10.6 %collective-permute-start.25 = (f32[192,128]{1,0:T(8,128)S(1)}, f32[192,128]{1,0:T(8,128)S(1)}, u32[]{:S(2)}, u32[]{:S(2)}) collective-permute-start(f32[192,128]{1,0:T(8,128)S(1)} %get-tuple-element.146.rest_7_), channel_id=1, source_target_pairs={{0,64},{16,80},{32,96},{48,112},{64,128},{80,144},{96,160},{112,17... | collective-permute-start | bytes 294920 | tf_op jit(solution)/shard_map/ppermute | solution.py:356
  79.2 10.7 %collective-permute-start.26 = (f32[192,128]{1,0:T(8,128)S(1)}, f32[192,128]{1,0:T(8,128)S(1)}, u32[]{:S(2)}, u32[]{:S(2)}) collective-permute-start(f32[192,128]{1,0:T(8,128)S(1)} %get-tuple-element.146.rest_7_), channel_id=1, source_target_pairs={{0,192},{16,208},{32,224},{48,240},{64,0},{80,16},{96,32},{112,48}... | collective-permute-start | bytes 294920 | tf_op jit(solution)/shard_map/ppermute | solution.py:356
  82.8 10.0 %collective-permute-start.27 = (f32[192,128]{1,0:T(8,128)S(1)}, f32[192,128]{1,0:T(8,128)S(1)}, u32[]{:S(2)}, u32[]{:S(2)}) collective-permute-start(f32[192,128]{1,0:T(8,128)S(1)} %get-tuple-element.146.rest_7_), channel_id=1, source_target_pairs={{0,32},{16,48},{32,64},{48,80},{64,96},{80,112},{96,128},{112,144}... | collective-permute-start | bytes 294920 | tf_op jit(solution)/shard_map/ppermute | solution.py:356
  93.8 8.3 %collective-permute-start.30 = (f32[248,128]{1,0:T(8,128)S(1)}, f32[248,128]{1,0:T(8,128)S(1)}, u32[]{:S(2)}, u32[]{:S(2)}) collective-permute-start(f32[248,128]{1,0:T(8,128)S(1)} %get-tuple-element.162), channel_id=1, source_target_pairs={{0,16},{16,0},{32,48},{48,32},{64,80},{80,64},{96,112},{112,96},{1... | collective-permute-start | bytes 380936 | tf_op jit(solution)/shard_map/ppermute | solution.py:345
  106.8 9.6 %collective-permute-start.33 = (f32[64,512]{1,0:T(8,128)S(1)}, f32[64,512]{1,0:T(8,128)S(1)}, u32[]{:S(2)}, u32[]{:S(2)}) collective-permute-start(f32[64,512]{1,0:T(8,128)S(1)} %get-tuple-element.180), channel_id=1, source_target_pairs={{0,10},{1,11},{2,8},{3,9},{4,14},{5,15},{6,12},{7,13},{8,2},{9,3},... | collective-permute-start | bytes 393224 | tf_op jit(solution)/shard_map/ppermute | solution.py:378
  109.0 9.5 %collective-permute-start.34 = (f32[64,512]{1,0:T(8,128)S(1)}, f32[64,512]{1,0:T(8,128)S(1)}, u32[]{:S(2)}, u32[]{:S(2)}) collective-permute-start(f32[64,512]{1,0:T(8,128)S(1)} %get-tuple-element.181), channel_id=1, source_target_pairs={{0,6},{1,7},{2,4},{3,5},{4,10},{5,11},{6,8},{7,9},{8,14},{9,15},{1... | collective-permute-start | bytes 393224 | tf_op jit(solution)/shard_map/ppermute | solution.py:378
  111.1 9.4 %collective-permute-start.35 = (f32[64,512]{1,0:T(8,128)S(1)}, f32[64,512]{1,0:T(8,128)S(1)}, u32[]{:S(2)}, u32[]{:S(2)}) collective-permute-start(f32[64,512]{1,0:T(8,128)S(1)} %get-tuple-element.182), channel_id=1, source_target_pairs={{0,14},{1,15},{2,12},{3,13},{4,2},{5,3},{6,0},{7,1},{8,6},{9,7},{1... | collective-permute-start | bytes 393224 | tf_op jit(solution)/shard_map/ppermute | solution.py:378
  114.1 8.8 %collective-permute-start.37 = (f32[64,512]{1,0:T(8,128)S(1)}, f32[64,512]{1,0:T(8,128)S(1)}, u32[]{:S(2)}, u32[]{:S(2)}) collective-permute-start(f32[64,512]{1,0:T(8,128)S(1)} %get-tuple-element.184), channel_id=1, source_target_pairs={{0,2},{1,3},{2,0},{3,1},{4,6},{5,7},{6,4},{7,5},{8,10},{9,11},{10,... | collective-permute-start | bytes 393224 | tf_op jit(solution)/shard_map/ppermute | solution.py:378
  116.4 7.9 %collective-permute-start.38 = (f32[64,512]{1,0:T(8,128)S(1)}, f32[64,512]{1,0:T(8,128)S(1)}, u32[]{:S(2)}, u32[]{:S(2)}) collective-permute-start(f32[64,512]{1,0:T(8,128)S(1)} %get-tuple-element.185), channel_id=1, source_target_pairs={{0,4},{1,5},{2,6},{3,7},{4,8},{5,9},{6,10},{7,11},{8,12},{9,13},{1... | collective-permute-start | bytes 393224 | tf_op jit(solution)/shard_map/ppermute | solution.py:378
  (25 other events, 153.4 us)

commit v6 on v5

--- a/solution.py
+++ b/solution.py
@@ -166,7 +166,7 @@
 
 
 RIM_ROWS = 248
-SENT = (4, 3, -3, 2, -2, 1, -1)
+SENT = (-1, 1, -2, 2, -3, 3, 4)
 
 
 def face_rows(offsets):
@@ -360,7 +360,7 @@
 
 
 def conv_beside(place, center, rims, weights, moved):
-    rims, moved = lax.optimization_barrier((rims, moved))
+    rims, moved, weights = lax.optimization_barrier((rims, moved, weights))
     parts = conv(place, center, rims, weights)
     return lax.optimization_barrier((parts, [to_other_core(value) for value in moved]))
 
@@ -397,7 +397,7 @@
     weights = split_weights(place, weight_in, swapped)
 
     plan = make_plan(place, *tables)
-    rims, (weights, center) = gather_rims(plan, faces, (weights, make_center(rows)))
+    rims, center = gather_rims(plan, faces, make_center(rows))
     parts, (swapped, other_bias) = conv_beside(place, center, rims, weights, [weight_out, bias_in])
     weights = split_weights(place, weight_out, swapped)
     parts = add_over_chips(parts)

time: 128 us -> 127 us (level)
  starting transfers between devices: 63.6 us -> 61.1 us
    ppermute x14, waiting for transfers between devices: 12.4 us -> 15.8 us  [gather_rims(): lax.ppermute(faces, 'leaf', [(i, (i + 2 * step) % 16) for i in range(16)])]
    ppermute x14, starting transfers between devices: 29.9 us -> 27.5 us  [gather_rims(): lax.ppermute(faces, 'leaf', [(i, (i + 2 * step) % 16) for i in range(16)])]
    ppermute x2, waiting for transfers between devices: 5.77 us -> 3.61 us  [to_other_both(): return lax.ppermute(value, ('leaf', 'chan'), pairs)]
  transfers between devices with their start and end apart: 41 -> 41, of which waited for: 21 -> 22; matrix products, arithmetic and copies ran while one was open for 0% -> 0% of each run, Pallas kernels for 11% -> 11%
where the time goes in v6:
time: 127 us
  starting transfers between devices  61.1 us (48%)
  waiting for transfers between devices  42.4 us (33%)
  Pallas kernels  18.6 us (15%)
  local copies, waits for them, and re-layouts  3.75 us (3%)
    ppermute x14, starting transfers between devices, gather_rims(): lax.ppermute(faces, 'leaf', [(i, (i + 2 * step) % 16) for i in range(16)])  27.5 us
    ppermute x14, starting transfers between devices, add_over_chips(): lax.ppermute(part, 'chan', [(i, route_target(i, route)) for i in range(16)])  21.9 us
    ppermute x14, waiting for transfers between devices, add_over_chips(): lax.ppermute(part, 'chan', [(i, route_target(i, route)) for i in range(16)])  15.8 us
    ppermute x14, waiting for transfers between devices, gather_rims(): lax.ppermute(faces, 'leaf', [(i, (i + 2 * step) % 16) for i in range(16)])  15.8 us
    pallas_call x2, Pallas kernels, conv(): call(conv_kernel, outs, scratch, flops=2 * 3 * 1024 * 1728 * 256, touched...  8.14 us
    ppermute x8, starting transfers between devices, to_other_core(): return lax.ppermute(value, 'chan', [(i, i ^ 1) for i in range(16)])  5.8 us
    ppermute x3, waiting for transfers between devices, to_other_x(): return lax.ppermute(value, 'leaf', [(i, i ^ 1) for i in range(16)])  5.44 us
    unnamed x16, local copies, waits for them, and re-layouts  3.75 us
  transfers between devices with their start and end apart: 41, of which 22 were waited for; matrix products, arithmetic and copies ran while one was open for 0% of the time, Pallas kernels for 11%

profile of v6, /device:TPU:1, one launch (start us, length us, event | category | flops | bytes accessed | tf_op | source)
XLA Modules:
  0.0 126.8 jit_solution(14298261247044419176)
XLA Ops:
  0.1 3.3 %collective-permute-start.8 = (f32[27,32,512]{2,1,0:T(8,128)}, f32[27,32,512]{2,1,0:T(8,128)S(1)}, u32[]{:S(2)}, u32[]{:S(2)}) collective-permute-start(f32[27,32,512]{2,1,0:T(8,128)} %own.3), channel_id=1, source_target_pairs={{0,1},{1,0},{2,3},{3,2},{4,5},{5,4},{6,7},{7,6},{8,9},{9,8},{10,11... | collective-permute-start | bytes 5308424 | tf_op jit(solution)/shard_map/ppermute | solution.py:341
  7.9 5.3 %collective-permute-start.7 = (f32[192,128]{1,0:T(8,128)S(1)}, f32[192,128]{1,0:T(8,128)S(1)}, u32[]{:S(2)}, u32[]{:S(2)}) collective-permute-start(f32[192,128]{1,0:T(8,128)S(1)} %get-tuple-element.101.rest_7_), channel_id=1, source_target_pairs={{0,128},{16,144},{32,160},{48,176},{64,192},{80,208},{96,224},{112... | collective-permute-start | bytes 294920 | tf_op jit(solution)/shard_map/ppermute | solution.py:356
  16.0 2.8 %collective-permute-start.5 = (f32[192,128]{1,0:T(8,128)S(1)}, f32[192,128]{1,0:T(8,128)S(1)}, u32[]{:S(2)}, u32[]{:S(2)}) collective-permute-start(f32[192,128]{1,0:T(8,128)S(1)} %get-tuple-element.101.rest_7_), channel_id=1, source_target_pairs={{0,160},{16,176},{32,192},{48,208},{64,224},{80,240},{96,0},{112,1... | collective-permute-start | bytes 294920 | tf_op jit(solution)/shard_map/ppermute | solution.py:356
  20.0 2.4 %collective-permute-start.3 = (f32[192,128]{1,0:T(8,128)S(1)}, f32[192,128]{1,0:T(8,128)S(1)}, u32[]{:S(2)}, u32[]{:S(2)}) collective-permute-start(f32[192,128]{1,0:T(8,128)S(1)} %get-tuple-element.101.rest_7_), channel_id=1, source_target_pairs={{0,192},{16,208},{32,224},{48,240},{64,0},{80,16},{96,32},{112,48}... | collective-permute-start | bytes 294920 | tf_op jit(solution)/shard_map/ppermute | solution.py:356
  22.4 3.1 %collective-permute-done.6.rest_5_ = f32[192,128]{1,0:T(8,128)S(1)} collective-permute-done((f32[192,128]{1,0:T(8,128)S(1)}, f32[192,128]{1,0:T(8,128)S(1)}, u32[]{:S(2)}, u32[]{:S(2)}) %collective-permute-start.6) | collective-permute-done | bytes 98336 | tf_op jit(solution)/shard_map/ppermute | solution.py:356
  25.5 2.7 %collective-permute-start.1 = (f32[192,128]{1,0:T(8,128)S(1)}, f32[192,128]{1,0:T(8,128)S(1)}, u32[]{:S(2)}, u32[]{:S(2)}) collective-permute-start(f32[192,128]{1,0:T(8,128)S(1)} %get-tuple-element.101.rest_7_), channel_id=1, source_target_pairs={{0,224},{16,240},{32,0},{48,16},{64,32},{80,48},{96,64},{112,80},{... | collective-permute-start | bytes 294920 | tf_op jit(solution)/shard_map/ppermute | solution.py:356
  33.4 2.2 %collective-permute-start.10 = (f32[248,128]{1,0:T(8,128)S(1)}, f32[248,128]{1,0:T(8,128)S(1)}, u32[]{:S(2)}, u32[]{:S(2)}) collective-permute-start(f32[248,128]{1,0:T(8,128)S(1)} %get-tuple-element.119), channel_id=1, source_target_pairs={{0,17},{1,16},{2,19},{3,18},{4,21},{5,20},{6,23},{7,22},{8,25},{9,... | collective-permute-start | bytes 380936 | tf_op jit(solution)/shard_map/ppermute | solution.py:350
  39.7 2.7 %collective-permute-done.11.rest_2_ = f32[248,128]{1,0:T(8,128)S(1)} collective-permute-done((f32[248,128]{1,0:T(8,128)S(1)}, f32[248,128]{1,0:T(8,128)S(1)}, u32[]{:S(2)}, u32[]{:S(2)}) %collective-permute-start.11) | collective-permute-done | bytes 127008 | tf_op jit(solution)/shard_map/ppermute | solution.py:345
  43.2 4.1 %shard_map.88 = (f32[64,512]{1,0:T(8,128)S(1)}, f32[64,512]{1,0:T(8,128)S(1)}, f32[64,512]{1,0:T(8,128)S(1)}, f32[64,512]{1,0:T(8,128)S(1)}, f32[64,512]{1,0:T(8...) custom-call(s32[4]{0:T(128)S(1)} %pad_add_fusion.place, ...), custom_call_target="tpu_custom_call" | custom-call | flops 2717908992 | bytes 8000000 | tf_op jit(solution)/shard_map/pallas_call | solution.py:333
  47.3 5.1 %collective-permute-start.15 = (f32[64,512]{1,0:T(8,128)S(1)}, f32[64,512]{1,0:T(8,128)S(1)}, u32[]{:S(2)}, u32[]{:S(2)}) collective-permute-start(f32[64,512]{1,0:T(8,128)S(1)} %get-tuple-element.140), channel_id=1, source_target_pairs={{0,10},{1,11},{2,8},{3,9},{4,14},{5,15},{6,12},{7,13},{8,2},{9,3},... | collective-permute-start | bytes 393224 | tf_op jit(solution)/shard_map/ppermute | solution.py:378
  53.1 4.4 %collective-permute-start.17 = (f32[64,512]{1,0:T(8,128)S(1)}, f32[64,512]{1,0:T(8,128)S(1)}, u32[]{:S(2)}, u32[]{:S(2)}) collective-permute-start(f32[64,512]{1,0:T(8,128)S(1)} %get-tuple-element.142), channel_id=1, source_target_pairs={{0,14},{1,15},{2,12},{3,13},{4,2},{5,3},{6,0},{7,1},{8,6},{9,7},{1... | collective-permute-start | bytes 393224 | tf_op jit(solution)/shard_map/ppermute | solution.py:378
  58.3 2.2 %collective-permute-done.16.rest_2_ = f32[64,512]{1,0:T(8,128)S(1)} collective-permute-done((f32[64,512]{1,0:T(8,128)S(1)}, f32[64,512]{1,0:T(8,128)S(1)}, u32[]{:S(2)}, u32[]{:S(2)}) %collective-permute-start.16) | collective-permute-done | bytes 131104 | tf_op jit(solution)/shard_map/ppermute | solution.py:378
  64.7 2.9 %collective-permute-done.20.rest_6_ = f32[64,512]{1,0:T(8,128)S(1)} collective-permute-done((f32[64,512]{1,0:T(8,128)S(1)}, f32[64,512]{1,0:T(8,128)S(1)}, u32[]{:S(2)}, u32[]{:S(2)}) %collective-permute-start.20) | collective-permute-done | bytes 131104 | tf_op jit(solution)/shard_map/ppermute | solution.py:378
  68.7 3.5 %collective-permute-start.28 = (f32[192,128]{1,0:T(8,128)S(1)}, f32[192,128]{1,0:T(8,128)S(1)}, u32[]{:S(2)}, u32[]{:S(2)}) collective-permute-start(f32[192,128]{1,0:T(8,128)S(1)} %get-tuple-element.147.rest_7_), channel_id=1, source_target_pairs={{0,128},{16,144},{32,160},{48,176},{64,192},{80,208},{96,224},{112... | collective-permute-start | bytes 294920 | tf_op jit(solution)/shard_map/ppermute | solution.py:356
  73.2 3.4 %collective-permute-start.26 = (f32[192,128]{1,0:T(8,128)S(1)}, f32[192,128]{1,0:T(8,128)S(1)}, u32[]{:S(2)}, u32[]{:S(2)}) collective-permute-start(f32[192,128]{1,0:T(8,128)S(1)} %get-tuple-element.147.rest_7_), channel_id=1, source_target_pairs={{0,160},{16,176},{32,192},{48,208},{64,224},{80,240},{96,0},{112,1... | collective-permute-start | bytes 294920 | tf_op jit(solution)/shard_map/ppermute | solution.py:356
  77.2 3.0 %collective-permute-start.24 = (f32[192,128]{1,0:T(8,128)S(1)}, f32[192,128]{1,0:T(8,128)S(1)}, u32[]{:S(2)}, u32[]{:S(2)}) collective-permute-start(f32[192,128]{1,0:T(8,128)S(1)} %get-tuple-element.147.rest_7_), channel_id=1, source_target_pairs={{0,192},{16,208},{32,224},{48,240},{64,0},{80,16},{96,32},{112,48}... | collective-permute-start | bytes 294920 | tf_op jit(solution)/shard_map/ppermute | solution.py:356
  80.2 6.0 %collective-permute-done.27.rest_5_ = f32[192,128]{1,0:T(8,128)S(1)} collective-permute-done((f32[192,128]{1,0:T(8,128)S(1)}, f32[192,128]{1,0:T(8,128)S(1)}, u32[]{:S(2)}, u32[]{:S(2)}) %collective-permute-start.27) | collective-permute-done | bytes 98336 | tf_op jit(solution)/shard_map/ppermute | solution.py:356
  87.2 2.1 %collective-permute-done.24.rest_2_ = f32[192,128]{1,0:T(8,128)S(1)} collective-permute-done((f32[192,128]{1,0:T(8,128)S(1)}, f32[192,128]{1,0:T(8,128)S(1)}, u32[]{:S(2)}, u32[]{:S(2)}) %collective-permute-start.24) | collective-permute-done | bytes 98336 | tf_op jit(solution)/shard_map/ppermute | solution.py:356
  95.5 2.6 %collective-permute-done.29.rest_1_ = f32[248,128]{1,0:T(8,128)S(1)} collective-permute-done((f32[248,128]{1,0:T(8,128)S(1)}, f32[248,128]{1,0:T(8,128)S(1)}, u32[]{:S(2)}, u32[]{:S(2)}) %collective-permute-start.29) | collective-permute-done | bytes 127008 | tf_op jit(solution)/shard_map/ppermute | solution.py:350
  98.1 2.7 %collective-permute-done.30.rest_2_ = f32[248,128]{1,0:T(8,128)S(1)} collective-permute-done((f32[248,128]{1,0:T(8,128)S(1)}, f32[248,128]{1,0:T(8,128)S(1)}, u32[]{:S(2)}, u32[]{:S(2)}) %collective-permute-start.30) | collective-permute-done | bytes 127008 | tf_op jit(solution)/shard_map/ppermute | solution.py:345
  101.3 4.1 %shard_map.93 = (f32[64,512]{1,0:T(8,128)S(1)}, f32[64,512]{1,0:T(8,128)S(1)}, f32[64,512]{1,0:T(8,128)S(1)}, f32[64,512]{1,0:T(8,128)S(1)}, f32[64,512]{1,0:T(8...) custom-call(s32[4]{0:T(128)S(1)} %pad_add_fusion.place, ...), custom_call_target="tpu_custom_call" | custom-call | flops 2717908992 | bytes 8000000 | tf_op jit(solution)/shard_map/pallas_call | solution.py:333
  107.5 2.5 %collective-permute-start.34 = (f32[64,512]{1,0:T(8,128)S(1)}, f32[64,512]{1,0:T(8,128)S(1)}, u32[]{:S(2)}, u32[]{:S(2)}) collective-permute-start(f32[64,512]{1,0:T(8,128)S(1)} %get-tuple-element.183), channel_id=1, source_target_pairs={{0,6},{1,7},{2,4},{3,5},{4,10},{5,11},{6,8},{7,9},{8,14},{9,15},{1... | collective-permute-start | bytes 393224 | tf_op jit(solution)/shard_map/ppermute | solution.py:378
  110.0 2.6 %collective-permute-start.35 = (f32[64,512]{1,0:T(8,128)S(1)}, f32[64,512]{1,0:T(8,128)S(1)}, u32[]{:S(2)}, u32[]{:S(2)}) collective-permute-start(f32[64,512]{1,0:T(8,128)S(1)} %get-tuple-element.184), channel_id=1, source_target_pairs={{0,14},{1,15},{2,12},{3,13},{4,2},{5,3},{6,0},{7,1},{8,6},{9,7},{1... | collective-permute-start | bytes 393224 | tf_op jit(solution)/shard_map/ppermute | solution.py:378
  112.6 2.4 %collective-permute-start.37 = (f32[64,512]{1,0:T(8,128)S(1)}, f32[64,512]{1,0:T(8,128)S(1)}, u32[]{:S(2)}, u32[]{:S(2)}) collective-permute-start(f32[64,512]{1,0:T(8,128)S(1)} %get-tuple-element.186), channel_id=1, source_target_pairs={{0,2},{1,3},{2,0},{3,1},{4,6},{5,7},{6,4},{7,5},{8,10},{9,11},{10,... | collective-permute-start | bytes 393224 | tf_op jit(solution)/shard_map/ppermute | solution.py:378
  (89 shorter events, 48.0 us)
Async XLA Ops:
  0.1 25.4 %collective-permute-start.8 = (f32[27,32,512]{2,1,0:T(8,128)}, f32[27,32,512]{2,1,0:T(8,128)S(1)}, u32[]{:S(2)}, u32[]{:S(2)}) collective-permute-start(f32[27,32,512]{2,1,0:T(8,128)} %own.3), channel_id=1, source_target_pairs={{0,1},{1,0},{2,3},{3,2},{4,5},{5,4},{6,7},{7,6},{8,9},{9,8},{10,11... | collective-permute-start | bytes 5308424 | tf_op jit(solution)/shard_map/ppermute | solution.py:341
  7.9 12.1 %collective-permute-start.7 = (f32[192,128]{1,0:T(8,128)S(1)}, f32[192,128]{1,0:T(8,128)S(1)}, u32[]{:S(2)}, u32[]{:S(2)}) collective-permute-start(f32[192,128]{1,0:T(8,128)S(1)} %get-tuple-element.101.rest_7_), channel_id=1, source_target_pairs={{0,128},{16,144},{32,160},{48,176},{64,192},{80,208},{96,224},{112... | collective-permute-start | bytes 294920 | tf_op jit(solution)/shard_map/ppermute | solution.py:356
  13.1 12.4 %collective-permute-start.6 = (f32[192,128]{1,0:T(8,128)S(1)}, f32[192,128]{1,0:T(8,128)S(1)}, u32[]{:S(2)}, u32[]{:S(2)}) collective-permute-start(f32[192,128]{1,0:T(8,128)S(1)} %get-tuple-element.101.rest_7_), channel_id=1, source_target_pairs={{0,96},{16,112},{32,128},{48,144},{64,160},{80,176},{96,192},{112,... | collective-permute-start | bytes 294920 | tf_op jit(solution)/shard_map/ppermute | solution.py:356
  16.0 14.7 %collective-permute-start.5 = (f32[192,128]{1,0:T(8,128)S(1)}, f32[192,128]{1,0:T(8,128)S(1)}, u32[]{:S(2)}, u32[]{:S(2)}) collective-permute-start(f32[192,128]{1,0:T(8,128)S(1)} %get-tuple-element.101.rest_7_), channel_id=1, source_target_pairs={{0,160},{16,176},{32,192},{48,208},{64,224},{80,240},{96,0},{112,1... | collective-permute-start | bytes 294920 | tf_op jit(solution)/shard_map/ppermute | solution.py:356
  18.8 11.9 %collective-permute-start.4 = (f32[192,128]{1,0:T(8,128)S(1)}, f32[192,128]{1,0:T(8,128)S(1)}, u32[]{:S(2)}, u32[]{:S(2)}) collective-permute-start(f32[192,128]{1,0:T(8,128)S(1)} %get-tuple-element.101.rest_7_), channel_id=1, source_target_pairs={{0,64},{16,80},{32,96},{48,112},{64,128},{80,144},{96,160},{112,17... | collective-permute-start | bytes 294920 | tf_op jit(solution)/shard_map/ppermute | solution.py:356
  20.0 10.7 %collective-permute-start.3 = (f32[192,128]{1,0:T(8,128)S(1)}, f32[192,128]{1,0:T(8,128)S(1)}, u32[]{:S(2)}, u32[]{:S(2)}) collective-permute-start(f32[192,128]{1,0:T(8,128)S(1)} %get-tuple-element.101.rest_7_), channel_id=1, source_target_pairs={{0,192},{16,208},{32,224},{48,240},{64,0},{80,16},{96,32},{112,48}... | collective-permute-start | bytes 294920 | tf_op jit(solution)/shard_map/ppermute | solution.py:356
  47.3 10.8 %collective-permute-start.15 = (f32[64,512]{1,0:T(8,128)S(1)}, f32[64,512]{1,0:T(8,128)S(1)}, u32[]{:S(2)}, u32[]{:S(2)}) collective-permute-start(f32[64,512]{1,0:T(8,128)S(1)} %get-tuple-element.140), channel_id=1, source_target_pairs={{0,10},{1,11},{2,8},{3,9},{4,14},{5,15},{6,12},{7,13},{8,2},{9,3},... | collective-permute-start | bytes 393224 | tf_op jit(solution)/shard_map/ppermute | solution.py:378
  52.4 8.2 %collective-permute-start.16 = (f32[64,512]{1,0:T(8,128)S(1)}, f32[64,512]{1,0:T(8,128)S(1)}, u32[]{:S(2)}, u32[]{:S(2)}) collective-permute-start(f32[64,512]{1,0:T(8,128)S(1)} %get-tuple-element.141), channel_id=1, source_target_pairs={{0,6},{1,7},{2,4},{3,5},{4,10},{5,11},{6,8},{7,9},{8,14},{9,15},{1... | collective-permute-start | bytes 393224 | tf_op jit(solution)/shard_map/ppermute | solution.py:378
  53.1 9.0 %collective-permute-start.17 = (f32[64,512]{1,0:T(8,128)S(1)}, f32[64,512]{1,0:T(8,128)S(1)}, u32[]{:S(2)}, u32[]{:S(2)}) collective-permute-start(f32[64,512]{1,0:T(8,128)S(1)} %get-tuple-element.142), channel_id=1, source_target_pairs={{0,14},{1,15},{2,12},{3,13},{4,2},{5,3},{6,0},{7,1},{8,6},{9,7},{1... | collective-permute-start | bytes 393224 | tf_op jit(solution)/shard_map/ppermute | solution.py:378
  57.5 7.3 %collective-permute-start.19 = (f32[64,512]{1,0:T(8,128)S(1)}, f32[64,512]{1,0:T(8,128)S(1)}, u32[]{:S(2)}, u32[]{:S(2)}) collective-permute-start(f32[64,512]{1,0:T(8,128)S(1)} %get-tuple-element.144), channel_id=1, source_target_pairs={{0,2},{1,3},{2,0},{3,1},{4,6},{5,7},{6,4},{7,5},{8,10},{9,11},{10,... | collective-permute-start | bytes 393224 | tf_op jit(solution)/shard_map/ppermute | solution.py:378
  58.1 9.5 %collective-permute-start.20 = (f32[64,512]{1,0:T(8,128)S(1)}, f32[64,512]{1,0:T(8,128)S(1)}, u32[]{:S(2)}, u32[]{:S(2)}) collective-permute-start(f32[64,512]{1,0:T(8,128)S(1)} %get-tuple-element.145), channel_id=1, source_target_pairs={{0,4},{1,5},{2,6},{3,7},{4,8},{5,9},{6,10},{7,11},{8,12},{9,13},{1... | collective-permute-start | bytes 393224 | tf_op jit(solution)/shard_map/ppermute | solution.py:378
  68.7 11.5 %collective-permute-start.28 = (f32[192,128]{1,0:T(8,128)S(1)}, f32[192,128]{1,0:T(8,128)S(1)}, u32[]{:S(2)}, u32[]{:S(2)}) collective-permute-start(f32[192,128]{1,0:T(8,128)S(1)} %get-tuple-element.147.rest_7_), channel_id=1, source_target_pairs={{0,128},{16,144},{32,160},{48,176},{64,192},{80,208},{96,224},{112... | collective-permute-start | bytes 294920 | tf_op jit(solution)/shard_map/ppermute | solution.py:356
  72.1 14.1 %collective-permute-start.27 = (f32[192,128]{1,0:T(8,128)S(1)}, f32[192,128]{1,0:T(8,128)S(1)}, u32[]{:S(2)}, u32[]{:S(2)}) collective-permute-start(f32[192,128]{1,0:T(8,128)S(1)} %get-tuple-element.147.rest_7_), channel_id=1, source_target_pairs={{0,96},{16,112},{32,128},{48,144},{64,160},{80,176},{96,192},{112,... | collective-permute-start | bytes 294920 | tf_op jit(solution)/shard_map/ppermute | solution.py:356
  73.2 13.3 %collective-permute-start.26 = (f32[192,128]{1,0:T(8,128)S(1)}, f32[192,128]{1,0:T(8,128)S(1)}, u32[]{:S(2)}, u32[]{:S(2)}) collective-permute-start(f32[192,128]{1,0:T(8,128)S(1)} %get-tuple-element.147.rest_7_), channel_id=1, source_target_pairs={{0,160},{16,176},{32,192},{48,208},{64,224},{80,240},{96,0},{112,1... | collective-permute-start | bytes 294920 | tf_op jit(solution)/shard_map/ppermute | solution.py:356
  76.6 10.6 %collective-permute-start.25 = (f32[192,128]{1,0:T(8,128)S(1)}, f32[192,128]{1,0:T(8,128)S(1)}, u32[]{:S(2)}, u32[]{:S(2)}) collective-permute-start(f32[192,128]{1,0:T(8,128)S(1)} %get-tuple-element.147.rest_7_), channel_id=1, source_target_pairs={{0,64},{16,80},{32,96},{48,112},{64,128},{80,144},{96,160},{112,17... | collective-permute-start | bytes 294920 | tf_op jit(solution)/shard_map/ppermute | solution.py:356
  77.2 12.2 %collective-permute-start.24 = (f32[192,128]{1,0:T(8,128)S(1)}, f32[192,128]{1,0:T(8,128)S(1)}, u32[]{:S(2)}, u32[]{:S(2)}) collective-permute-start(f32[192,128]{1,0:T(8,128)S(1)} %get-tuple-element.147.rest_7_), channel_id=1, source_target_pairs={{0,192},{16,208},{32,224},{48,240},{64,0},{80,16},{96,32},{112,48}... | collective-permute-start | bytes 294920 | tf_op jit(solution)/shard_map/ppermute | solution.py:356
  80.2 11.1 %collective-permute-start.23 = (f32[192,128]{1,0:T(8,128)S(1)}, f32[192,128]{1,0:T(8,128)S(1)}, u32[]{:S(2)}, u32[]{:S(2)}) collective-permute-start(f32[192,128]{1,0:T(8,128)S(1)} %get-tuple-element.147.rest_7_), channel_id=1, source_target_pairs={{0,32},{16,48},{32,64},{48,80},{64,96},{80,112},{96,128},{112,144}... | collective-permute-start | bytes 294920 | tf_op jit(solution)/shard_map/ppermute | solution.py:356
  92.9 7.9 %collective-permute-start.30 = (f32[248,128]{1,0:T(8,128)S(1)}, f32[248,128]{1,0:T(8,128)S(1)}, u32[]{:S(2)}, u32[]{:S(2)}) collective-permute-start(f32[248,128]{1,0:T(8,128)S(1)} %get-tuple-element.163), channel_id=1, source_target_pairs={{0,16},{16,0},{32,48},{48,32},{64,80},{80,64},{96,112},{112,96},{1... | collective-permute-start | bytes 380936 | tf_op jit(solution)/shard_map/ppermute | solution.py:345
  105.4 9.6 %collective-permute-start.33 = (f32[64,512]{1,0:T(8,128)S(1)}, f32[64,512]{1,0:T(8,128)S(1)}, u32[]{:S(2)}, u32[]{:S(2)}) collective-permute-start(f32[64,512]{1,0:T(8,128)S(1)} %get-tuple-element.182), channel_id=1, source_target_pairs={{0,10},{1,11},{2,8},{3,9},{4,14},{5,15},{6,12},{7,13},{8,2},{9,3},... | collective-permute-start | bytes 393224 | tf_op jit(solution)/shard_map/ppermute | solution.py:378
  107.5 9.4 %collective-permute-start.34 = (f32[64,512]{1,0:T(8,128)S(1)}, f32[64,512]{1,0:T(8,128)S(1)}, u32[]{:S(2)}, u32[]{:S(2)}) collective-permute-start(f32[64,512]{1,0:T(8,128)S(1)} %get-tuple-element.183), channel_id=1, source_target_pairs={{0,6},{1,7},{2,4},{3,5},{4,10},{5,11},{6,8},{7,9},{8,14},{9,15},{1... | collective-permute-start | bytes 393224 | tf_op jit(solution)/shard_map/ppermute | solution.py:378
  110.0 9.2 %collective-permute-start.35 = (f32[64,512]{1,0:T(8,128)S(1)}, f32[64,512]{1,0:T(8,128)S(1)}, u32[]{:S(2)}, u32[]{:S(2)}) collective-permute-start(f32[64,512]{1,0:T(8,128)S(1)} %get-tuple-element.184), channel_id=1, source_target_pairs={{0,14},{1,15},{2,12},{3,13},{4,2},{5,3},{6,0},{7,1},{8,6},{9,7},{1... | collective-permute-start | bytes 393224 | tf_op jit(solution)/shard_map/ppermute | solution.py:378
  112.6 7.4 %collective-permute-start.36 = (f32[64,512]{1,0:T(8,128)S(1)}, f32[64,512]{1,0:T(8,128)S(1)}, u32[]{:S(2)}, u32[]{:S(2)}) collective-permute-start(f32[64,512]{1,0:T(8,128)S(1)} %get-tuple-element.185), channel_id=1, source_target_pairs={{0,8},{1,9},{2,10},{3,11},{4,12},{5,13},{6,14},{7,15},{8,0},{9,1},... | collective-permute-start | bytes 393224 | tf_op jit(solution)/shard_map/ppermute | solution.py:378
  112.6 8.7 %collective-permute-start.37 = (f32[64,512]{1,0:T(8,128)S(1)}, f32[64,512]{1,0:T(8,128)S(1)}, u32[]{:S(2)}, u32[]{:S(2)}) collective-permute-start(f32[64,512]{1,0:T(8,128)S(1)} %get-tuple-element.186), channel_id=1, source_target_pairs={{0,2},{1,3},{2,0},{3,1},{4,6},{5,7},{6,4},{7,5},{8,10},{9,11},{10,... | collective-permute-start | bytes 393224 | tf_op jit(solution)/shard_map/ppermute | solution.py:378
  115.0 7.8 %collective-permute-start.38 = (f32[64,512]{1,0:T(8,128)S(1)}, f32[64,512]{1,0:T(8,128)S(1)}, u32[]{:S(2)}, u32[]{:S(2)}) collective-permute-start(f32[64,512]{1,0:T(8,128)S(1)} %get-tuple-element.187), channel_id=1, source_target_pairs={{0,4},{1,5},{2,6},{3,7},{4,8},{5,9},{6,10},{7,11},{8,12},{9,13},{1... | collective-permute-start | bytes 393224 | tf_op jit(solution)/shard_map/ppermute | solution.py:378
  (25 other events, 137.5 us)
